TPU v7x, 256 devices: a whole 4x4x8 slice. The times are simulated.
256 devices in a mesh: row: 8 (over y, x_hi), res: 32 (over x_lo, z, core).
Axes of the slice: x: 4 (x_hi: 2, x_lo: 2; x = x_hi * 2 + x_lo), y: 4, z: 8, core: 2. Of those that a mesh axis runs over, the one named last changes fastest.
Arguments:
- sequence_stack: bfloat16 [256, 2048, 64], P('row', 'res'), may hold values from -40 to 40
- twofold_features: bfloat16 [2048, 2048, 128], P('row', 'res'), may hold values from -40 to 40
- incoming_adjoint: bfloat16 [256, 2048, 64], P('row', 'res'), may hold values from -6 to 6
- sequence_present_flags: int32 [256], P('row'), may hold values 0 or 1
- polymer_identifiers: int32 [2048], replicated, may hold values from 0 to 3, as said below
- sequence_position_ids: int32 [2048], replicated, may hold values from 1 to 41159, as said below
- sequence_stack_multiplier: float32 [64], replicated, may hold values from 0.25 to 1.75
- twofold_stack_multiplier: float32 [128], replicated, may hold values from 0.25 to 1.75
- content_projection: bfloat16 [64, 64], replicated, may hold values from -0.75 to 0.75
- sigmoid_projection: bfloat16 [64, 64], replicated, may hold values from -0.75 to 0.75
- final_projection: bfloat16 [64, 64], replicated, may hold values from -0.75 to 0.75
- twofold_head_projection: float32 [128, 8], replicated, may hold values from -0.5 to 0.5
- separation_bucket_shift: float32 [66, 8], replicated, may hold values from -4 to 450
Outputs:
- alignment_gradient: bfloat16 [256, 2048, 64], P('row', 'res')
- pair_gradient: bfloat16 [2048, 2048, 128], P('row', 'res')
Inputs may be any that keep to these rules, and one draw needn't show every extreme that they name: `polymer_identifiers`: non-decreasing along the residues. `sequence_position_ids`: strictly increasing within a chain.
All inputs are finite; a program needn't handle non-finite values. No bound on the sum of `sequence_present_flags` on one device may be relied on, other than what follows from the above.
Results may differ from a plain program's by a relative error of at most 0.025.
Values may be sent and summed in bfloat16 or wider, within the bound.
No kernel may reach another device: no remote copies, remote signals or barrier semaphores. Data moves between devices by JAX's collectives and lax.ppermute only.
A program may use at most 192 MiB of HBM per device.

v0:
```python
import jax
import jax.numpy as jnp
from jax import lax
from jax.sharding import PartitionSpec as P

RMAX = 32


eps = 1e-05
exact = lax.Precision.HIGHEST


def merged(value, axis, join):
    pieces = jax.tree.map(lambda part: lax.all_gather(part, axis), value)
    head = jax.tree.map(lambda part: part[0], pieces)
    tail = jax.tree.map(lambda part: part[1:], pieces)
    so_far, _ = lax.scan(lambda so_far, slab: (join(so_far, slab), None), head, tail)
    return so_far


def standardize_features(field, gain):
    center = field - jnp.mean(field, -1, keepdims=True)
    scale = lax.rsqrt(jnp.mean(center * center, -1, keepdims=True) + eps)
    normed = center * scale
    return (normed * gain, normed, scale)


def layer_norm_backward(grad, normed, scale, gain):
    scaled = grad * gain
    return scale * (
        scaled
        - jnp.mean(scaled, -1, keepdims=True)
        - normed * jnp.mean(scaled * normed, -1, keepdims=True)
    )


def softmax_combine(first, second):
    peak = jnp.maximum(first[0], second[0])
    return (peak, first[1] * jnp.exp(first[0] - peak) + second[1] * jnp.exp(second[0] - peak))


def shards(
    sequence_stack,
    twofold_features,
    incoming_adjoint,
    sequence_present_flags,
    polymer_identifiers,
    sequence_position_ids,
    sequence_stack_multiplier,
    twofold_stack_multiplier,
    content_projection,
    sigmoid_projection,
    final_projection,
    twofold_head_projection,
    separation_bucket_shift,
):
    thirtytwo_bit_type = jnp.float32
    sequence_positions, separation_bucket_list, feature_extent = sequence_stack.shape
    heads = twofold_head_projection.shape[1]
    inner = content_projection.shape[1]
    depth = inner // heads
    block = twofold_features.shape[0]
    total = polymer_identifiers.shape[0]
    classes = separation_bucket_shift.shape[0]
    sequence_minus_mean, standardized_sequences, sequence_stack_factor = standardize_features(
        sequence_stack.astype(thirtytwo_bit_type), sequence_stack_multiplier
    )
    alignment_normalized = sequence_minus_mean.astype(jnp.bfloat16)
    content_every_sequence = jnp.einsum(
        "umv,vw->umw",
        alignment_normalized,
        content_projection,
        preferred_element_type=thirtytwo_bit_type,
    ).astype(jnp.bfloat16)
    gate_activation = jax.nn.sigmoid(
        jnp.einsum(
            "umv,vw->umw",
            alignment_normalized,
            sigmoid_projection,
            preferred_element_type=thirtytwo_bit_type,
        )
    )
    masked_logits = incoming_adjoint * sequence_present_flags.astype(jnp.bfloat16)[:, None, None]
    upstream = jnp.einsum(
        "snc,dc->snd", masked_logits, final_projection, preferred_element_type=thirtytwo_bit_type
    )
    increment_tensor = (gate_activation * upstream).astype(jnp.bfloat16)
    row_start = lax.axis_index("row") * block
    col_start = lax.axis_index("res") * separation_bucket_list
    chain_rows = lax.dynamic_slice_in_dim(polymer_identifiers, row_start, block)
    chain_cols = lax.dynamic_slice_in_dim(polymer_identifiers, col_start, separation_bucket_list)
    index_rows = lax.dynamic_slice_in_dim(sequence_position_ids, row_start, block)
    index_cols = lax.dynamic_slice_in_dim(sequence_position_ids, col_start, separation_bucket_list)
    offset = jnp.clip(index_rows[:, None] - index_cols[None, :] + RMAX, 0, 2 * RMAX)
    bins = jnp.where(chain_rows[:, None] == chain_cols[None, :], offset, 2 * RMAX + 1)
    onehot = (bins[:, :, None] == jnp.arange(classes, dtype=jnp.int32)[None, None, :]).astype(
        thirtytwo_bit_type
    )
    shifted_pair, normed_pair, scale_pair = standardize_features(
        twofold_features.astype(thirtytwo_bit_type), twofold_stack_multiplier
    )
    logits = jnp.einsum("ijc,ch->hij", shifted_pair, twofold_head_projection, precision=exact)
    logits = logits + jnp.einsum("ijk,kh->hij", onehot, separation_bucket_shift, precision=exact)
    top_local = jnp.max(logits, -1)
    sum_local = jnp.sum(jnp.exp(logits - top_local[..., None]), -1)
    peak, summed = merged((top_local, sum_local), "res", softmax_combine)
    weights = (jnp.exp(logits - peak[..., None]) / summed[..., None]).astype(jnp.bfloat16)
    wide = lax.all_gather(weights, "row", axis=1, tiled=True)
    gathered = lax.all_gather(increment_tensor, "res", axis=1, tiled=True)
    gathered_heads = gathered.reshape(sequence_positions, total, heads, depth)
    content_per_head = content_every_sequence.reshape(
        sequence_positions, separation_bucket_list, heads, depth
    )
    content_adjoint = jnp.einsum(
        "ozk,azof->akof", wide, gathered_heads, preferred_element_type=thirtytwo_bit_type
    )
    content_adjoint = content_adjoint.reshape(
        sequence_positions, separation_bucket_list, inner
    ).astype(jnp.bfloat16)
    piece = wide
    term = jnp.einsum(
        "hij,sjhc->ishc", piece, content_per_head, preferred_element_type=thirtytwo_bit_type
    )
    context_local = lax.psum_scatter(
        term.reshape(
            lax.axis_size("res") * separation_bucket_list, sequence_positions * inner
        ).astype(jnp.bfloat16),
        "res",
        scatter_dimension=0,
        tiled=True,
    ).astype(jnp.float32)
    attended_result = context_local.reshape(
        separation_bucket_list, sequence_positions, inner
    ).transpose(1, 0, 2)
    gate_grad = (upstream * attended_result * gate_activation * (1.0 - gate_activation)).astype(
        jnp.bfloat16
    )
    normalized_gradient = jnp.einsum(
        "snd,cd->snc",
        content_adjoint,
        content_projection,
        preferred_element_type=thirtytwo_bit_type,
    )
    normalized_gradient = normalized_gradient + jnp.einsum(
        "snd,cd->snc", gate_grad, sigmoid_projection, preferred_element_type=thirtytwo_bit_type
    )
    alignment_gradient = layer_norm_backward(
        normalized_gradient,
        standardized_sequences,
        sequence_stack_factor,
        sequence_stack_multiplier,
    ).astype(jnp.bfloat16)
    piece = gathered_heads
    term = jnp.einsum(
        "sihc,sjhc->ihj", piece, content_per_head, preferred_element_type=thirtytwo_bit_type
    )
    score_local = lax.psum_scatter(
        term.reshape(lax.axis_size("row") * block, heads * separation_bucket_list).astype(
            jnp.bfloat16
        ),
        "row",
        scatter_dimension=0,
        tiled=True,
    ).astype(jnp.float32)
    scores = score_local.reshape(block, heads, separation_bucket_list).transpose(1, 0, 2)
    chosen = weights.astype(thirtytwo_bit_type)
    row_total = lax.psum(jnp.sum(chosen * scores, -1), "res")
    logit_grad = chosen * (scores - row_total[..., None])
    shifted_grad = jnp.einsum("hij,ch->ijc", logit_grad, twofold_head_projection, precision=exact)
    pair_gradient = layer_norm_backward(
        shifted_grad, normed_pair, scale_pair, twofold_stack_multiplier
    ).astype(jnp.bfloat16)
    return (alignment_gradient, pair_gradient)


def solution(mesh):
    return jax.shard_map(
        shards,
        mesh=mesh,
        in_specs=(
            P("row", "res", None),
            P("row", "res", None),
            P("row", "res", None),
            P("row"),
            P(),
            P(),
            P(),
            P(),
            P(),
            P(),
            P(),
            P(),
            P(),
        ),
        out_specs=(P("row", "res", None), P("row", "res", None)),
        check_vma=False,
    )
```

profile of v0, /device:TPU:32, one launch (start us, length us, event | category | flops | bytes accessed | tf_op | source)
XLA Modules:
  0.0 447.9 jit_solution(12249219047038076403)
XLA Ops:
  7.2 0.0 all-gather.5.cloned.1.call-start
  7.2 0.7 convert_element_type.65
  7.9 1.3 copy.70
  9.2 0.1 convert_reduce_fusion.1
  9.4 0.2 fusion.53
  9.6 1.4 fusion.63
  11.0 1.0 copy-done.4
  12.0 2.4 multiply_convert_fusion
  14.4 0.0 reduce-scatter.5.cloned.1.call-start
  14.4 0.8 dynamic_slice.20
  15.2 0.8 dynamic_slice.22
  15.9 0.8 dynamic_slice.19
  16.7 0.8 dynamic_slice.21
  17.5 0.4 convolution_convert_fusion
  17.9 0.3 copy.80
  18.2 6.8 %copy.73 = bf16[256,64,128]{0,2,1:T(8,128)(2,1)} copy(bf16[256,64,128]{2,1,0:T(8,128)(2,1)} %param.16) | data formatting | bytes 8388608 | tf_op args[1]
  25.0 0.1 clamp_select_fusion
  25.1 3.4 convert_reduce_fusion
  28.5 3.9 fusion.13
  32.4 5.5 %fusion.7 = f32[256,64,8]{0,2,1:T(8,128)S(1)} fusion(bf16[256,64,128]{0,2,1:T(8,128)(2,1)S(1)} %copy-done.1, f32[128]{0:T(128)S(1)} %copy-done.7, f32[256,64]{0,1:T(8,128)S(1)} %add_rsqrt_fusion, f32[256,64]{0,1:T(8,128)S(1)} %broadcast_multiply_fusion.2, f32[128,8]{0,1:T(8,128)S(1)} %copy-done.10), kind=kOutput, calls=%fused_computation.12 | convolution fusion | flops 209715200 | bytes 4854272 | tf_op jit(solution)/shard_map/ijc,ch->hij/dot_general | solution.py:102
  37.9 1.7 fusion.83
  39.5 35.7 %all-gather = f32[256,256]{1,0:T(8,128)S(1)} all-gather(f32[8,256]{1,0:T(8,128)S(1)} %get-tuple-element.60), channel_id=2, replica_groups=mesh['row'=8,'res'=32] {'res'}, dimensions={0}, use_global_device_ids=true | all-gather | bytes 270336 | tf_op jit(solution)/shard_map/all_gather | solution.py:14
  75.3 0.1 exponential_reduce_fusion
  75.4 35.3 %all-gather.1 = f32[256,256]{1,0:T(8,128)S(1)} all-gather(f32[8,256]{1,0:T(8,128)S(1)} %exponential_reduce_fusion), channel_id=3, replica_groups=mesh['row'=8,'res'=32] {'res'}, dimensions={0}, use_global_device_ids=true | all-gather | bytes 270336 | tf_op jit(solution)/shard_map/all_gather | solution.py:14
  110.8 8.6 %all-gather.5.cloned.1.call-done = bf16[32,2048,64]{2,1,0:T(8,128)(2,1)} async-done(((bf16[32,64,64]{2,1,0:T(8,128)(2,1)}), bf16[32,2048,64]{2,1,0:T(8,128)(2,1)}) %all-gather.5.cloned.1.call-update) | async-done | bytes 8388624 | tf_op jit(solution)/shard_map/all_gather | solution.py:109
  119.3 15.9 %copy.72 = bf16[32,2048,64]{1,2,0:T(8,128)(2,1)} copy(bf16[32,2048,64]{2,1,0:T(8,128)(2,1)} %all-gather.5.cloned.1.call-done) | data formatting | bytes 16777216 | tf_op jit(solution)/shard_map/all_gather | solution.py:109
  135.2 6.4 %bitcast_convert_fusion = bf16[8,64,2048]{2,1,0:T(8,128)(2,1)} fusion(bf16[32,2048,64]{1,2,0:T(8,128)(2,1)} %copy.72, bf16[32,64,64]{1,2,0:T(8,128)(2,1)S(1)} %copy.80), kind=kOutput, calls=%fused_computation.26 | convolution fusion | flops 537919488 | bytes 10747904 | tf_op jit(solution)/shard_map/sihc,sjhc->ihj/dot_general | solution.py:154
  141.6 0.0 all-gather.7.cloned.1.call-start
  141.6 1.2 while.12
  142.8 79.5 %reduce-scatter.5.cloned.1.call-done = bf16[256,512]{0,1:T(8,128)(2,1)} async-done(((bf16[2048,512]{0,1:T(8,128)(2,1)}), bf16[256,512]{0,1:T(8,128)(2,1)}) %reduce-scatter.5.cloned.1.call-update) | async-done | bytes 262160 | tf_op jit(solution)/shard_map/reduce_scatter | solution.py:157
  222.3 1.0 bitcast_convert_fusion.1
  223.3 1.0 fusion.57
  224.3 0.0 reduce-scatter.7.cloned.1.call-start
  224.4 59.3 %all-gather.7.cloned.1.call-done = bf16[8,2048,64]{1,0,2:T(8,128)(2,1)} async-done(((bf16[8,256,64]{1,0,2:T(8,128)(2,1)}), bf16[8,2048,64]{1,0,2:T(8,128)(2,1)}) %all-gather.7.cloned.1.call-update) | async-done | bytes 2097168 | tf_op jit(solution)/shard_map/all_gather | solution.py:108
  283.7 8.3 %convert_bitcast_fusion = bf16[2048,32,8,8]{0,3,1,2:T(8,128)(2,1)} fusion(bf16[8,2048,64,1]{1,0,2,3:T(8,128)(2,1)} %bitcast.104, bf16[32,64,64]{1,2,0:T(8,128)(2,1)S(1)} %copy.80), kind=kOutput, calls=%fused_computation.18 | convolution fusion | flops 541065216 | bytes 10747904 | tf_op jit(solution)/shard_map/hij,sjhc->ishc/dot_general | solution.py:121
  292.0 8.3 %copy.83 = bf16[2048,32,8,8]{0,3,2,1:T(8,128)(2,1)} copy(bf16[2048,32,8,8]{0,3,1,2:T(8,128)(2,1)} %convert_bitcast_fusion) | data formatting | bytes 16777216 | tf_op jit(solution)/shard_map/convert_element_type | solution.py:127
  300.3 12.3 %copy.102 = bf16[2048,2048]{1,0:T(8,128)(2,1)} copy(bf16[2048,2048]{0,1:T(8,128)(2,1)} %bitcast.102) | data formatting | bytes 16777216
  312.6 52.7 %psum.7 = f32[8,256]{1,0:T(8,128)S(1)} all-reduce(f32[8,256]{1,0:T(8,128)S(1)} %get-tuple-element.56), channel_id=1, replica_groups=mesh['row'=8,'res'=32] {'res'}, use_global_device_ids=true, to_apply=%region_13.14 | all-reduce | flops 2048 | bytes 16384 | tf_op jit(solution)/shard_map/psum | solution.py:167
  365.3 10.7 %multiply_reduce_fusion = (f32[256,64]{0,1:T(8,128)S(1)}, f32[256,64]{0,1:T(8,128)S(1)}, f32[256,64,128]{0,2,1:T(8,128)S(1)}) fusion(f32[128]{0:T(128)S(1)} %copy-done.7, f32[256,64]{0,1:T(8,128)S(1)} %add_rsqrt_fusion, f32[256,64]{0,1:T(8,128)S(1)} %broadcast_multiply_fusion.2, bf16[256,64,128]{0,2,1:T(8,128)(2,1)} %copy.73, f32[128,8]{0,1:T(8,128)S(1)} %copy-done.10, ...), kind=kOutput, calls=%fused_computation.23 | convolution fusion | flops 216367104 | bytes 13644288 | tf_op jit(solution)/shard_map/hij,ch->ijc/dot_general | solution.py:169
  376.0 5.0 %fusion.12 = bf16[256,64,128]{0,2,1:T(8,128)(2,1)} fusion(bf16[256,64,128]{0,2,1:T(8,128)(2,1)S(1)} %copy-done.2, f32[256,64,128]{0,2,1:T(8,128)S(1)} %get-tuple-element.63, f32[256,64]{0,1:T(8,128)S(1)} %get-tuple-element.66, f32[256,64]{0,1:T(8,128)S(1)} %get-tuple-element.67, f32[128]{0:T(128)S(1)} %copy-done.7, f32[256,64]{0,1:T(8,128)S(1)} %add_rsqrt_fusion, ...), kind=kLoop, calls=%fused_computation.16 | loop fusion | flops 18874368 | bytes 17039872 | tf_op jit(solution)/shard_map/convert_element_type | solution.py:172
  381.0 6.6 %copy.90 = bf16[256,64,128]{2,1,0:T(8,128)(2,1)} copy(bf16[256,64,128]{0,2,1:T(8,128)(2,1)} %fusion.12) | data formatting | bytes 8388608
  387.6 5.8 %fusion.41 = bf16[32,64,8,8]{1,3,0,2:T(8,128)(2,1)S(1)} fusion(bf16[8,2048,64,1]{1,0,2,3:T(8,128)(2,1)S(1)} %bitcast.105, bf16[32,2048,64]{1,2,0:T(8,128)(2,1)} %copy.72), kind=kOutput, calls=%fused_computation.48 | convolution fusion | flops 537001984 | bytes 10747904 | tf_op jit(solution)/shard_map/ozk,azof->akof/dot_general | solution.py:114
  393.4 42.3 %reduce-scatter.7.cloned.1.call-done = bf16[64,2048]{1,0:T(8,128)(2,1)} async-done(((bf16[2048,2048]{1,0:T(8,128)(2,1)}), bf16[64,2048]{1,0:T(8,128)(2,1)}) %reduce-scatter.7.cloned.1.call-update) | async-done | bytes 262160 | tf_op jit(solution)/shard_map/reduce_scatter | solution.py:124
  435.7 1.4 reshape.132
  437.0 2.4 fusion.59
  439.4 0.5 fusion.82
  440.0 0.3 fusion.52
  440.3 1.0 copy.89
  (66 shorter events, 0.8 us)
Async XLA Ops:
  7.2 4.8 %copy-start = (bf16[64,64]{1,0:T(8,128)(2,1)S(1)}, bf16[64,64]{1,0:T(8,128)(2,1)}, u32[]{:S(2)}) copy-start(bf16[64,64]{1,0:T(8,128)(2,1)} %param.24) | copy-start | bytes 24580
  7.2 10.3 %copy-start.8 = (f32[64]{0:T(128)S(1)}, f32[64]{0:T(128)}, u32[]{:S(2)}) copy-start(f32[64]{0:T(128)} %param.21) | copy-start | bytes 772
  7.2 10.3 %copy-start.6 = (bf16[64,64]{1,0:T(8,128)(2,1)S(1)}, bf16[64,64]{1,0:T(8,128)(2,1)}, u32[]{:S(2)}) copy-start(bf16[64,64]{1,0:T(8,128)(2,1)} %param.23) | copy-start | bytes 24580
  7.2 112.1 %all-gather.5.cloned.1.call-start = ((), (), s32[]{:S(2)}) async-start(), calls=%async_computation.2 | async-start | bytes 17301504 | tf_op jit(solution)/shard_map/all_gather | solution.py:109
  11.0 1.0 copy-start.4
  14.4 207.9 %reduce-scatter.5.cloned.1.call-start = ((), (), s32[]{:S(2)}) async-start(), calls=%async_computation.4 | async-start | bytes 2359296 | tf_op jit(solution)/shard_map/reduce_scatter | solution.py:157
  18.1 14.3 %copy-start.7 = (f32[128]{0:T(128)S(1)}, f32[128]{0:T(128)}, u32[]{:S(2)}) copy-start(f32[128]{0:T(128)} %param.22) | copy-start | bytes 1540
  18.2 14.3 %copy-start.10 = (f32[128,8]{0,1:T(8,128)S(1)}, f32[128,8]{0,1:T(8,128)}, u32[]{:S(2)}) copy-start(f32[128,8]{0,1:T(8,128)} %param.26) | copy-start | bytes 12292
  25.0 7.4 %copy-start.1 = (bf16[256,64,128]{0,2,1:T(8,128)(2,1)S(1)}, bf16[256,64,128]{0,2,1:T(8,128)(2,1)}, u32[]{:S(2)}) copy-start(bf16[256,64,128]{0,2,1:T(8,128)(2,1)} %copy.73) | copy-start | bytes 12582916
  25.1 12.8 %copy-start.9 = (f32[66,8]{0,1:T(8,128)S(1)}, f32[66,8]{0,1:T(8,128)}, u32[]{:S(2)}) copy-start(f32[66,8]{0,1:T(8,128)} %param.27) | copy-start | bytes 6340
  141.6 142.2 %all-gather.7.cloned.1.call-start = ((), (), s32[]{:S(2)}) async-start(), calls=%async_computation.3 | async-start | bytes 2359296 | tf_op jit(solution)/shard_map/all_gather | solution.py:108
  224.3 211.3 %reduce-scatter.7.cloned.1.call-start = ((), (), s32[]{:S(2)}) async-start(), calls=%async_computation.5 | async-start | bytes 8650752 | tf_op jit(solution)/shard_map/reduce_scatter | solution.py:124
  312.6 52.7 %copy-start.5 = (bf16[8,256,64]{1,0,2:T(8,128)(2,1)S(1)}, bf16[8,256,64]{1,0,2:T(8,128)(2,1)}, u32[]{:S(2)}) copy-start(bf16[8,256,64]{1,0,2:T(8,128)(2,1)} %get-tuple-element.57) | copy-start | bytes 786436
  365.3 10.7 %copy-start.2 = (bf16[256,64,128]{0,2,1:T(8,128)(2,1)S(1)}, bf16[256,64,128]{0,2,1:T(8,128)(2,1)}, u32[]{:S(2)}) copy-start(bf16[256,64,128]{0,2,1:T(8,128)(2,1)} %copy.73) | copy-start | bytes 12582916
  381.0 6.6 %copy-start.3 = (bf16[8,2048,64]{1,0,2:T(8,128)(2,1)S(1)}, bf16[8,2048,64]{1,0,2:T(8,128)(2,1)}, u32[]{:S(2)}) copy-start(bf16[8,2048,64]{1,0,2:T(8,128)(2,1)} %all-gather.7.cloned.1.call-done) | copy-start | bytes 6291460
Sparse Core Ops, SparseCore 0:
  14.5 104.8 all-gather.4
  141.7 80.5 reduce-scatter.4
  225.3 58.3 all-gather.6
  312.7 122.8 reduce-scatter.6
where the time goes:
time: 454 us; the launch traced here: 448 us
  waiting for transfers between devices  190 us (42%)
  blocking collectives  124 us (27%)
  local copies, waits for them, and re-layouts  57.9 us (13%)
  matrix products  45.3 us (10%)
  other arithmetic  16.4 us (4%)
  between operations  14.1 us (3%)
    reduce_scatter x1, waiting for transfers between devices, shards(): lax.psum_scatter(term.reshape(lax.axis_size('row') * block, heads * separ...  79.5 us
    all_gather x2, blocking collectives, merged(): pieces = jax.tree.map(lambda part: lax.all_gather(part, axis), value)  71 us
    all_gather x1, waiting for transfers between devices, shards(): wide = lax.all_gather(weights, 'row', axis=1, tiled=True)  59.3 us
    psum x1, blocking collectives, shards(): row_total = lax.psum(jnp.sum(chosen * scores, -1), 'res')  52.7 us
    reduce_scatter x1, waiting for transfers between devices, shards(): lax.psum_scatter(term.reshape(lax.axis_size('res') * separation_bucket_li...  42.3 us
    unnamed x27, local copies, waits for them, and re-layouts  29.1 us
    all_gather x1, local copies, waits for them, and re-layouts, shards(): gathered = lax.all_gather(increment_tensor, 'res', axis=1, tiled=True)  15.9 us
    dot_general x1, matrix products, shards(): jnp.einsum('hij,ch->ijc', logit_grad, twofold_head_projection, precision=...  10.7 us
  transfers between devices with their start and end apart: 4, of which 4 were waited for; matrix products, arithmetic and copies ran while one was open for 12% of the time, Pallas kernels for 0%

commit v1 on v0

v1 whole, which is shorter than its diff:
```python
import functools

import jax
import jax.numpy as jnp
from jax import lax
from jax.experimental import pallas as pl
from jax.experimental.pallas import tpu as pltpu
from jax.sharding import Mesh
from jax.sharding import PartitionSpec as P

RMAX = 32
EPS = 1e-05
BF = jnp.bfloat16
F32 = jnp.float32
VMEM = pltpu.CompilerParams(vmem_limit_bytes=48 * 1024 * 1024)
HALF = 64


def mm(a, b):
    return lax.dot_general(a, b, (((1,), (0,)), ((), ())), preferred_element_type=F32)


def mm_nt(a, b):
    return lax.dot_general(a, b, (((1,), (1,)), ((), ())), preferred_element_type=F32)


def mm_tn(a, b):
    return lax.dot_general(a, b, (((0,), (0,)), ((), ())), preferred_element_type=F32)


def iota(shape, dim):
    return lax.broadcasted_iota(jnp.int32, shape, dim)


def split3(x):
    hi = x.astype(BF).astype(F32)
    mid = (x - hi).astype(BF).astype(F32)
    return hi, mid, x - hi - mid


def spread(weight, transposed, out_ref):
    k, l = iota((64, 1024), 0), iota((64, 1024), 1)
    pick = jnp.where((k // 8 == l // 128) & (k % 8 == l % 8), 1.0, 0.0).astype(BF)
    wide = mm_tn(weight, pick) if transposed else mm(weight, pick)
    owner = (l % 128) // 8
    for s in range(16):
        out_ref[s * 64 : (s + 1) * 64, :] = jnp.where(owner == s, wide, 0.0).astype(BF)


def standardize(x):
    center = x - jnp.mean(x, -1, keepdims=True)
    scale = lax.rsqrt(jnp.mean(center * center, -1, keepdims=True) + EPS)
    return center * scale, scale


def msa_forward(flags, msa, adj, gain, wc, ws, wf, u_out, v_out, t_out, bdc, bds, bdf):
    spread(wc[...], False, bdc)
    spread(ws[...], False, bds)
    spread(wf[...], True, bdf)
    g = gain[...]
    for d in range(2):
        normed, masked = [], []
        for s in range(16):
            row = d * 16 + s
            normed.append((standardize(msa[row].astype(F32))[0] * g).astype(BF))
            masked.append((adj[row].astype(F32) * flags[row].astype(F32)).astype(BF))
        x = jnp.concatenate(normed, axis=1)
        y = jnp.concatenate(masked, axis=1)
        values = mm(x, bdc[...]).astype(BF)
        gate = jax.nn.sigmoid(mm(x, bds[...]))
        upstream = mm(y, bdf[...])
        moved = gate * upstream
        update = moved.astype(BF)
        tail = moved * (1.0 - gate)
        for h in range(8):
            cols = slice(h * 128, (h + 1) * 128)
            v_out[h, d] = values[:, cols]
            t_out[h, d] = tail[:, cols]
            for b in range(4):
                u_out[h, d, b] = update[:, cols]


def partner(x, k, lane):
    return jnp.where(lane & k == 0, pltpu.roll(x, 128 - k, 1), pltpu.roll(x, k, 1))


def pair_forward(pair, bins, proj, table, v_in, out, saved, p_s, m_s):
    w_hi, w_mid, w_lo = split3(proj[...])
    ones8 = jnp.full((8, 128), 1.0 / 128, F32)
    lhs = jnp.concatenate([w_hi, w_mid, w_lo, ones8], axis=0).astype(BF)
    ones8 = ones8.astype(BF)
    averager = jnp.full((128, 128), 1.0 / 128, F32).astype(BF)
    b_lhs = jnp.concatenate(list(split3(table[...])) + [jnp.zeros((8, 128), F32)], axis=0).astype(BF)
    lane = iota((8, 128), 1)
    klass = iota((128, 1024), 0)
    for g in range(4):
        x = jnp.concatenate(
            [pair[e * 32 + g * 8 + rho] for rho in range(8) for e in range(2)], axis=0
        )
        center = x.astype(F32) - mm(x, averager)
        square = center * center
        s_hi = square.astype(BF)
        s_lo = (square - s_hi.astype(F32)).astype(BF)
        var = mm_nt(ones8, s_hi) + mm_nt(ones8, s_lo)
        z = mm_nt(lhs, x)
        scale = lax.rsqrt(var + EPS)
        t = (z[0:8] + z[8:16] + z[16:24]) * scale
        saved[g, 0:8, :] = t
        saved[g, 8:16, :] = scale
        saved[g, 16:24, :] = z[24:32]
        onehot = jnp.where(klass == bins[g], 1.0, 0.0).astype(BF)
        zb = mm(b_lhs, onehot)
        logits = t + (zb[0:8] + zb[8:16] + zb[16:24])
        for rho in range(8):
            part = logits[:, rho * 128 : (rho + 1) * 128]
            top = part
            for k in (1, 2, 4, 8, 16, 32):
                top = jnp.maximum(top, partner(top, k, lane))
            top = top.astype(BF).astype(F32)
            p_s[:, g * 8 + rho, :] = jnp.exp(part - top)
            m_s[:, g * 8 + rho, :] = top
    quarter = iota((16, 128), 1) // 32
    for h in range(8):
        weights = p_s[h].astype(BF)
        low, high = m_s[h, 0:16, :], m_s[h, 16:32, :]
        packed = jnp.where(
            quarter == 0,
            low,
            jnp.where(
                quarter == 1, pltpu.roll(low, 64, 1), jnp.where(quarter == 2, pltpu.roll(high, 64, 1), high)
            ),
        ).astype(BF)
        for d in range(2):
            out[h, d, 0, 0:64, :] = v_in[h, d]
            out[h, d, 0, 64:96, :] = weights
            out[h, d, 0, 96:112, :] = packed


def merge_products(ub, vw, p_out, stats, m_s):
    lane = iota((128, 128), 1)
    quarter = lane // 32
    left = lane < HALF
    for half in range(2):
        tops = []
        for c in range(8):
            q = vw[:, c, 96:112, :].astype(F32).reshape(128, 128)
            q64 = pltpu.roll(q, 64, 1)
            if half == 0:
                tops.append(jnp.where(quarter == 0, q, jnp.where(quarter == 3, q64, pltpu.roll(q, 32, 1))))
            else:
                tops.append(jnp.where(quarter == 0, q64, jnp.where(quarter == 3, q, pltpu.roll(q, 96, 1))))
        peak = functools.reduce(jnp.maximum, tops)
        crossed = pltpu.roll(peak, 64, 1)
        m_s[:, 0, half] = jnp.where(left, peak, crossed).reshape(8, 16, 128)
        m_s[:, 1, half] = jnp.where(left, crossed, peak).reshape(8, 16, 128)
        rows = slice(64 + half * 16, 80 + half * 16)
        for cp in range(4):
            one, two = [
                vw[:, c, rows, :].astype(F32).reshape(128, 128) * jnp.exp(tops[c] - peak)
                for c in (2 * cp, 2 * cp + 1)
            ]
            cols = slice(cp * 128, (cp + 1) * 128)
            even = jnp.where(left, one, pltpu.roll(two, 64, 1)).astype(BF)
            odd = jnp.where(left, pltpu.roll(one, 64, 1), two).astype(BF)
            p_out[:, 0, half, :, cols] = even.reshape(8, 16, 128)
            p_out[:, 1, half, :, cols] = odd.reshape(8, 16, 128)
    p = p_out[...].reshape(512, 512)
    total = mm(p, jnp.full((512, 128), 1.0, F32).astype(BF))
    acc = jnp.zeros((512, 128), F32)
    for r in range(0, 8, 2):
        v = jnp.concatenate([vw[r + k, :, 0:64, :].reshape(512, 128) for k in range(2)], axis=1)
        c = mm(p, v)
        for k in range(2):
            acc += ub[r + k].reshape(512, 128).astype(F32) * c[:, k * 128 : (k + 1) * 128]
    score = jnp.sum(acc, axis=1, keepdims=True)
    column = iota((512, 128), 1)
    mixed = jnp.where(
        column == 0,
        m_s[...].reshape(512, 128),
        jnp.where(column == 1, total, jnp.where(column == 2, score, 0.0)),
    )
    rows = jnp.transpose(mixed)[0:8]
    for k in range(8):
        stats[k] = rows


def score_products(ub, vw, out):
    acc = jnp.zeros((512, 512), F32)
    for r in range(0, 8, 2):
        u = jnp.concatenate([ub[r + k].reshape(512, 128) for k in range(2)], axis=1)
        v = jnp.concatenate([vw[r + k, :, 0:64, :].reshape(512, 128) for k in range(2)], axis=1)
        acc += mm_nt(u, v)
    out[...] = acc


def gradients(stats, own, p_in, ub, scores, p_out, out):
    tops, totals, sums = stats[:, 0, :], stats[:, 1, :], stats[:, 2, :]
    peak = jnp.max(tops, axis=0, keepdims=True)
    factor = jnp.exp(tops - peak)
    total = 0.5 * jnp.sum(factor * totals, axis=0, keepdims=True)
    row_total = jnp.sum(factor * sums, axis=0, keepdims=True) / total
    mine = jnp.exp(own[0:1, :] - peak) / total
    which = iota((8, 512), 0)
    columns = jnp.transpose(jnp.where(which == 0, mine, jnp.where(which == 1, 0.5 * row_total, 0.0)))
    p = (p_in[...].reshape(512, 512).astype(F32) * columns[:, 0:1]).astype(BF)
    p_out[...] = p
    grad = (p.astype(F32) * (scores[...] - columns[:, 1:2])).reshape(8, 2, 32, 512)
    left = iota((256, 128), 1) < HALF
    for cp in range(4):
        cols = slice(cp * 128, (cp + 1) * 128)
        even, odd = [grad[:, e, :, cols].reshape(256, 128) for e in range(2)]
        one = jnp.where(left, even, pltpu.roll(odd, 64, 1)).astype(BF)
        two = jnp.where(left, pltpu.roll(even, 64, 1), odd).astype(BF)
        out[:, 2 * cp, 64:96, :] = one.reshape(8, 32, 128)
        out[:, 2 * cp + 1, 64:96, :] = two.reshape(8, 32, 128)
    pt = jnp.transpose(p)
    for r in range(0, 8, 2):
        u = jnp.concatenate([ub[r + k].reshape(512, 128) for k in range(2)], axis=1)
        grad_v = mm(pt, u).astype(BF)
        for k in range(2):
            out[r + k, :, 0:64, :] = grad_v[:, k * 128 : (k + 1) * 128].reshape(8, 64, 128)


def context_products(p, vw, out):
    for r in range(0, 8, 2):
        v = jnp.concatenate([vw[r + k, :, 0:64, :].reshape(512, 128) for k in range(2)], axis=1)
        c = mm(p[...], v).astype(BF)
        for k in range(2):
            out[r + k] = c[:, k * 128 : (k + 1) * 128].reshape(8, 64, 128)


def pair_backward(pair, grads, saved, proj, out, g_s):
    w_hi, w_mid, _ = split3(proj[...])
    row = iota((8, 128), 0)
    flag = jnp.where(row < 3, 1.0, 0.0)
    rhs = jnp.concatenate([w_hi, w_hi, w_mid, flag], axis=0).astype(BF)
    rhs_a = jnp.concatenate([flag, jnp.zeros((8, 128), F32)], axis=0).astype(BF)
    g_s[...] = grads[:, 0, 0].astype(F32) + grads[:, 1, 0].astype(F32)
    which = iota((8, 1024), 0)

    def stacked(x):
        hi, mid, low = split3(x)
        return jnp.where(which == 0, hi, jnp.where(which == 1, mid, jnp.where(which == 2, low, 0.0)))

    for g in range(4):
        grad = jnp.concatenate([g_s[:, g * 8 + rho, :] for rho in range(8)], axis=1)
        t, scale, mean = saved[g, 0:8, :], saved[g, 8:16, :], saved[g, 16:24, :]
        slope = jnp.sum(grad * t, axis=0, keepdims=True) * (1.0 / 128)
        alpha = scale * scale * slope
        scaled = grad * scale
        hi = scaled.astype(BF).astype(F32)
        lhs = jnp.concatenate([hi, scaled - hi, hi, stacked(alpha * mean)], axis=0).astype(BF)
        lhs_a = jnp.concatenate([stacked(alpha), jnp.zeros((8, 1024), F32)], axis=0).astype(BF)
        base = mm_tn(lhs, rhs)
        steep = mm_tn(lhs_a, rhs_a)
        for rho in range(8):
            for e in range(2):
                i = e * 32 + g * 8 + rho
                rows = slice((rho * 2 + e) * 64, (rho * 2 + e + 1) * 64)
                out[i] = (base[rows] - steep[rows] * pair[i].astype(F32)).astype(BF)


def msa_backward(msa, gain, wc, ws, gb, cb, tail, out, bdc, bds):
    spread(wc[...], False, bdc)
    spread(ws[...], False, bds)
    g = gain[...]
    for d in range(2):
        value_grad, gate_grad = [], []
        for h in range(8):
            total = gb[h, d, 0, 0:64, :].astype(F32)
            context = cb[h, d, 0].astype(F32)
            for k in range(1, 4):
                total += gb[h, d, k, 0:64, :].astype(F32)
                context += cb[h, d, k].astype(F32)
            value_grad.append(total.astype(BF))
            gate_grad.append((tail[h, d] * context).astype(BF))
        grad = mm_nt(jnp.concatenate(value_grad, axis=1), bdc[...])
        grad += mm_nt(jnp.concatenate(gate_grad, axis=1), bds[...])
        for s in range(16):
            row = d * 16 + s
            normed, scale = standardize(msa[row].astype(F32))
            scaled = grad[:, s * 64 : (s + 1) * 64] * g
            out[row] = (
                scale
                * (
                    scaled
                    - jnp.mean(scaled, -1, keepdims=True)
                    - normed * jnp.mean(scaled * normed, -1, keepdims=True)
                )
            ).astype(BF)


def exchange(x, axes):
    return lax.all_to_all(x, axes, 0, 0, tiled=True)


def shape(dims, dtype):
    return jax.ShapeDtypeStruct(dims, dtype)


def shards(msa, pair, adj, flags, chains, positions, msa_gain, pair_gain, wc, ws, wf, wp, table):
    vm = pl.BlockSpec(memory_space=pltpu.VMEM)
    sm = pl.BlockSpec(memory_space=pltpu.SMEM)
    gp, gq = ("row", "d", "a"), ("row", "d", "b")
    gain = msa_gain.reshape(1, 64)

    u_send, values, tail = pl.pallas_call(
        msa_forward,
        out_shape=(shape((8, 2, 4, 64, 128), BF), shape((8, 2, 64, 128), BF), shape((8, 2, 64, 128), F32)),
        in_specs=[sm] + [vm] * 6,
        out_specs=(vm, vm, vm),
        scratch_shapes=[pltpu.VMEM((1024, 1024), BF)] * 3,
        compiler_params=VMEM,
        name="msa_forward",
    )(flags, msa, adj, gain, wc, ws, wf)
    ub = exchange(u_send.reshape(64, 64, 128), gq).reshape(8, 8, 64, 128)

    row = lax.axis_index("row")
    col = lax.axis_index("d") * 16 + lax.axis_index("b") * 4 + lax.axis_index("a")

    def rows_of(x):
        return lax.dynamic_slice_in_dim(x, row * 256, 256).reshape(4, 2, 4, 8).transpose(0, 2, 3, 1)

    def cols_of(x):
        return lax.dynamic_slice_in_dim(x, col * 64, 64)

    offset = jnp.clip(rows_of(positions)[..., None] - cols_of(positions) + RMAX, 0, 2 * RMAX)
    bins = jnp.where(rows_of(chains)[..., None] == cols_of(chains), offset, 2 * RMAX + 1)
    bins = bins.reshape(16, 1, 1024)
    scaled = (wp * pair_gain[:, None]).T
    proj = scaled - jnp.mean(scaled, -1, keepdims=True)
    table_t = jnp.pad(table.T, ((0, 0), (0, 128 - table.shape[0])))

    def const(*dims):
        return pl.BlockSpec(dims, lambda k: (0,) * len(dims))

    vw_send, saved = pl.pallas_call(
        pair_forward,
        grid=(4,),
        out_shape=(shape((8, 2, 4, 112, 128), BF), shape((16, 24, 1024), F32)),
        in_specs=[
            pl.BlockSpec((64, 64, 128), lambda k: (k, 0, 0)),
            pl.BlockSpec((4, 1, 1024), lambda k: (k, 0, 0)),
            const(8, 128),
            const(8, 128),
            const(8, 2, 64, 128),
        ],
        out_specs=(
            pl.BlockSpec((8, 2, 1, 112, 128), lambda k: (0, 0, k, 0, 0)),
            pl.BlockSpec((4, 24, 1024), lambda k: (k, 0, 0)),
        ),
        scratch_shapes=[pltpu.VMEM((8, 32, 128), F32)] * 2,
        compiler_params=VMEM,
        name="pair_forward",
    )(pair, bins, proj, table_t, values)
    vw = exchange(vw_send.reshape(64, 112, 128), gp).reshape(8, 8, 112, 128)

    p_raw, stats = pl.pallas_call(
        merge_products,
        out_shape=(shape((8, 2, 2, 16, 512), BF), shape((8, 8, 512), F32)),
        in_specs=[vm, vm],
        out_specs=(vm, vm),
        scratch_shapes=[pltpu.VMEM((8, 2, 2, 16, 128), F32)],
        compiler_params=VMEM,
        name="merge_products",
    )(ub, vw)
    all_stats = exchange(stats, ("d", "b"))
    scores = pl.pallas_call(
        score_products,
        out_shape=shape((512, 512), F32),
        in_specs=[vm, vm],
        out_specs=vm,
        compiler_params=VMEM,
        name="score_products",
    )(ub, vw)
    p, gd_send = pl.pallas_call(
        gradients,
        out_shape=(shape((512, 512), BF), shape((8, 8, 96, 128), BF)),
        in_specs=[vm] * 5,
        out_specs=(vm, vm),
        compiler_params=VMEM,
        name="gradients",
    )(all_stats, stats[0], p_raw, ub, scores)
    gd = exchange(gd_send.reshape(64, 96, 128), gp).reshape(8, 2, 4, 96, 128)
    c_send = pl.pallas_call(
        context_products,
        out_shape=shape((8, 8, 64, 128), BF),
        in_specs=[vm, vm],
        out_specs=vm,
        compiler_params=VMEM,
        name="context_products",
    )(p, vw)
    cb = exchange(c_send.reshape(64, 64, 128), gq).reshape(8, 2, 4, 64, 128)
    pair_gradient = pl.pallas_call(
        pair_backward,
        grid=(4,),
        out_shape=shape((256, 64, 128), BF),
        in_specs=[
            pl.BlockSpec((64, 64, 128), lambda k: (k, 0, 0)),
            pl.BlockSpec((8, 2, 1, 32, 128), lambda k: (0, 0, k, 2, 0)),
            pl.BlockSpec((4, 24, 1024), lambda k: (k, 0, 0)),
            const(8, 128),
        ],
        out_specs=pl.BlockSpec((64, 64, 128), lambda k: (k, 0, 0)),
        scratch_shapes=[pltpu.VMEM((8, 32, 128), F32)],
        compiler_params=VMEM,
        name="pair_backward",
    )(pair, gd, saved, proj)
    alignment_gradient = pl.pallas_call(
        msa_backward,
        out_shape=shape((32, 64, 64), BF),
        in_specs=[vm] * 7,
        out_specs=vm,
        scratch_shapes=[pltpu.VMEM((1024, 1024), BF)] * 2,
        compiler_params=VMEM,
        name="msa_backward",
    )(msa, gain, wc, ws, gd, cb, tail)
    return (alignment_gradient, pair_gradient)


def solution(mesh):
    inner = Mesh(mesh.devices.reshape(8, 2, 4, 4), ("row", "d", "b", "a"))
    res = ("d", "b", "a")
    split = P("row", res, None)
    return jax.shard_map(
        shards,
        mesh=inner,
        in_specs=(split, split, split, P("row")) + (P(),) * 9,
        out_specs=(split, split),
        check_vma=False,
    )
```

time: 454 us -> 185 us (0.41)
  the two profiles are of different devices: /device:TPU:32 before, /device:TPU:1 now
where the time goes in v1:
time: 185 us; the launch traced here: 183 us
  waiting for transfers between devices  59.4 us (32%)
  Pallas kernels  34.8 us (19%)
  blocking collectives  34.6 us (19%)
  starting transfers between devices  29.6 us (16%)
  local copies, waits for them, and re-layouts  23.6 us (13%)
    all_to_all x4, waiting for transfers between devices, exchange(): return lax.all_to_all(x, axes, 0, 0, tiled=True)  59.4 us
    all_to_all x1, blocking collectives, exchange(): return lax.all_to_all(x, axes, 0, 0, tiled=True)  34.6 us
    all_to_all x4, starting transfers between devices, exchange(): return lax.all_to_all(x, axes, 0, 0, tiled=True)  29.6 us
    unnamed x56, local copies, waits for them, and re-layouts  18.4 us
    pallas_call x1, Pallas kernels, shards(): pl.pallas_call(pair_forward, grid=(4,), out_shape=(shape((8, 2, 4, 112, 1...  11.3 us
    pallas_call x1, Pallas kernels, shards(): pl.pallas_call(msa_backward, out_shape=shape((32, 64, 64), BF), in_specs=...  8.57 us
    pallas_call x1, Pallas kernels, shards(): pl.pallas_call(pair_backward, grid=(4,), out_shape=shape((256, 64, 128),...  6.41 us
    pallas_call x1, Pallas kernels, shards(): pl.pallas_call(msa_forward, out_shape=(shape((8, 2, 4, 64, 128), BF), sha...  4.38 us
  transfers between devices with their start and end apart: 4, of which 4 were waited for; matrix products, arithmetic and copies ran while one was open for 3% of the time, Pallas kernels for 10%

profile of v1, /device:TPU:1, one launch (start us, length us, event | category | flops | bytes accessed | tf_op | source)
XLA Modules:
  0.0 183.2 jit_solution(14228098981646278532)
XLA Ops:
  0.6 1.0 copy-done.3
  1.7 1.0 copy-done.11
  2.7 0.7 copy-done.15
  3.4 0.7 copy-done.17
  4.2 0.7 copy-done.21
  4.9 0.7 copy-done.22
  5.5 0.7 copy-done.24
  6.2 4.4 %msa_forward.1 = (bf16[8,2,4,64,128]{4,3,2,1,0:T(8,128)(2,1)}, bf16[8,2,64,128]{3,2,1,0:T(8,128)(2,1)S(1)}, f32[8,2,64,128]{3,2,1,0:T(8,128)S(1)}) custom-call(s32[32]{0:T(128)S(1)} %copy-done.24, bf16[32,64,64]{2,1,0:T(8,128)(2,1)S(1)} %copy-done.3, bf16[32,64,64]{2,1,0:T(8,128)(2,1)S(1)} %copy-done.11, f32[1,64]{1,0:T(1,128)S(1)} %bitcast.28, ...), custom_call_target="tpu_custom_call" | custom-call | tf_op jit(solution)/shard_map/msa_forward/pallas_call | solution.py:307
  10.6 0.8 copy-done.9
  11.4 15.2 %all-to-all-start = ((bf16[64,64,128]{2,1,0:T(8,128)(2,1)}), bf16[64,64,128]{2,1,0:T(8,128)(2,1)S(1)}, u32[]{:S(2)}, u32[]{:S(2)}) async-start(bf16[64,64,128]{2,1,0:T(8,128)(2,1)} %bitcast.1), calls=%async_computation | async-start | bytes 2097152 | tf_op jit(solution)/shard_map/all_to_all | solution.py:294
  26.6 0.8 dynamic_slice.13
  27.4 0.8 dynamic_slice.15
  28.2 0.8 dynamic_slice.12
  28.9 0.8 dynamic_slice.14
  30.0 0.2 copy.15
  30.2 0.2 copy.16
  30.4 0.2 sub.36
  30.6 0.1 sub.37
  30.7 0.2 eq.26
  30.9 0.1 eq.27
  31.5 0.4 copy-done.19
  31.9 11.3 %pair_forward.1 = (bf16[8,2,4,112,128]{4,3,2,1,0:T(8,128)(2,1)S(1)}, f32[16,24,1024]{2,1,0:T(8,128)S(1)}) custom-call(bf16[256,64,128]{2,1,0:T(8,128)(2,1)} %pair.3, s32[16,1,1024]{2,1,0:T(1,128)S(1)} %compare_select_fusion.bins, f32[8,128]{1,0:T(8,128)S(1)} %subtract_bitcast_fusion.proj, f32[8,128]{1,0:T(8,128)S(1)} %pad.4.table, ...), custom_call_target="tpu_custom_call" | custom-call | tf_op jit(solution)/shard_map/pair_forward/pallas_call | solution.py:337
  43.2 1.2 copy-done.5
  44.5 1.2 copy-done.7
  45.6 9.9 %all-to-all-done = bf16[64,64,128]{2,1,0:T(8,128)(2,1)S(1)} async-done(((bf16[64,64,128]{2,1,0:T(8,128)(2,1)}), bf16[64,64,128]{2,1,0:T(8,128)(2,1)S(1)}, u32[]{:S(2)}, u32[]{:S(2)}) %all-to-all-start) | async-done | bytes 1048608 | tf_op jit(solution)/shard_map/all_to_all | solution.py:294
  55.6 34.6 %all_to_all.25 = bf16[64,112,128]{2,1,0:T(8,128)(2,1)S(1)} all-to-all(bf16[64,112,128]{2,1,0:T(8,128)(2,1)} %bitcast.26), channel_id=1, replica_groups=mesh['row'=8,'d'=2,'b'=4,'a'=4] {'row','d','a'}, dimensions={0} | all-to-all | bytes 3670016 | tf_op jit(solution)/shard_map/all_to_all | solution.py:294
  90.2 1.6 merge_products.1
  91.7 0.7 copy-done.14
  92.4 3.4 %all-to-all-start.2 = ((f32[8,8,512]{2,1,0:T(8,128)}), f32[8,8,512]{2,1,0:T(8,128)S(1)}, u32[]{:S(2)}, u32[]{:S(2)}) async-start(f32[8,8,512]{2,1,0:T(8,128)} %copy-done.14), calls=%async_computation.2 | async-start | bytes 262144 | tf_op jit(solution)/shard_map/all_to_all | solution.py:294
  95.8 0.7 score_products.1.scores
  96.5 1.0 copy-done.1
  97.5 0.7 slice_bitcast_fusion.own
  98.2 5.7 %all-to-all-done.2.stats = f32[8,8,512]{2,1,0:T(8,128)S(1)} async-done(((f32[8,8,512]{2,1,0:T(8,128)}), f32[8,8,512]{2,1,0:T(8,128)S(1)}, u32[]{:S(2)}, u32[]{:S(2)}) %all-to-all-start.2) | async-done | bytes 131104 | tf_op jit(solution)/shard_map/all_to_all | solution.py:294
  103.9 1.2 copy-done.2
  105.1 1.1 gradients.1
  106.2 0.8 copy-done.12
  107.0 1.1 copy-done.6
  108.1 6.1 %all-to-all-start.3 = ((bf16[64,96,128]{2,1,0:T(8,128)(2,1)}), bf16[64,96,128]{2,1,0:T(8,128)(2,1)S(1)}, u32[]{:S(2)}, u32[]{:S(2)}) async-start(bf16[64,96,128]{2,1,0:T(8,128)(2,1)} %bitcast.27), calls=%async_computation.3 | async-start | bytes 3145728 | tf_op jit(solution)/shard_map/all_to_all | solution.py:294
  114.3 1.0 copy-done.13
  115.3 0.7 context_products.1
  116.1 1.0 copy-done
  117.1 21.2 %all-to-all-done.3 = bf16[64,96,128]{2,1,0:T(8,128)(2,1)S(1)} async-done(((bf16[64,96,128]{2,1,0:T(8,128)(2,1)}), bf16[64,96,128]{2,1,0:T(8,128)(2,1)S(1)}, u32[]{:S(2)}, u32[]{:S(2)}) %all-to-all-start.3) | async-done | bytes 1572896 | tf_op jit(solution)/shard_map/all_to_all | solution.py:294
  138.3 4.8 %all-to-all-start.4 = ((bf16[64,64,128]{2,1,0:T(8,128)(2,1)}), bf16[64,64,128]{2,1,0:T(8,128)(2,1)S(1)}, u32[]{:S(2)}, u32[]{:S(2)}) async-start(bf16[64,64,128]{2,1,0:T(8,128)(2,1)} %bitcast.25), calls=%async_computation.4 | async-start | bytes 2097152 | tf_op jit(solution)/shard_map/all_to_all | solution.py:294
  143.1 1.4 copy-done.8
  144.5 6.4 %pair_backward.1 = bf16[256,64,128]{2,1,0:T(8,128)(2,1)} custom-call(bf16[256,64,128]{2,1,0:T(8,128)(2,1)} %pair.3, bf16[8,2,4,96,128]{4,3,2,1,0:T(8,128)(2,1)S(1)} %bitcast.22, f32[16,24,1024]{2,1,0:T(8,128)S(1)} %copy-done.8, f32[8,128]{1,0:T(8,128)S(1)} %copy-done.20), custom_call_target="tpu_custom_call" | custom-call | tf_op jit(solution)/shard_map/pair_backward/pallas_call | solution.py:394
  151.0 22.6 %all-to-all-done.4 = bf16[64,64,128]{2,1,0:T(8,128)(2,1)S(1)} async-done(((bf16[64,64,128]{2,1,0:T(8,128)(2,1)}), bf16[64,64,128]{2,1,0:T(8,128)(2,1)S(1)}, u32[]{:S(2)}, u32[]{:S(2)}) %all-to-all-start.4) | async-done | bytes 1048608 | tf_op jit(solution)/shard_map/all_to_all | solution.py:294
  173.6 1.0 copy-done.10
  174.6 8.6 %msa_backward.1 = bf16[32,64,64]{2,1,0:T(8,128)(2,1)} custom-call(bf16[32,64,64]{2,1,0:T(8,128)(2,1)S(1)} %copy-done.4, f32[1,64]{1,0:T(1,128)S(1)} %bitcast.29, bf16[64,64]{1,0:T(8,128)(2,1)S(1)} %copy-done.16, bf16[64,64]{1,0:T(8,128)(2,1)S(1)} %copy-done.18, bf16[8,2,4,96,128]{4,3,2,1,0:T(8,128)(2,1)S(1)} %bitcast.23, ...), custom_call_target="tpu_custom_call" | custom-call | tf_op jit(solution)/shard_map/msa_backward/pallas_call | solution.py:409
  (47 shorter events, 0.8 us)
Async XLA Ops:
  0.6 1.0 copy-start.3
  1.7 1.0 copy-start.11
  2.7 0.7 copy-start.15
  3.4 0.7 copy-start.17
  4.2 0.7 copy-start.21
  4.9 0.7 copy-start.22
  5.5 0.7 copy-start.24
  10.6 0.8 copy-start.9
  11.4 19.7 %copy-start.26 = (f32[66,8]{0,1:T(8,128)S(1)}, f32[66,8]{0,1:T(8,128)}, u32[]{:S(2)}) copy-start(f32[66,8]{0,1:T(8,128)} %param.25) | copy-start | bytes 6340
  11.4 19.8 %copy-start.25 = (f32[128,8]{0,1:T(8,128)S(1)}, f32[128,8]{0,1:T(8,128)}, u32[]{:S(2)}) copy-start(f32[128,8]{0,1:T(8,128)} %param.24) | copy-start | bytes 12292
  11.4 19.8 %copy-start.27 = (f32[128]{0:T(128)S(1)}, f32[128]{0:T(128)}, u32[]{:S(2)}) copy-start(f32[128]{0:T(128)} %param.20) | copy-start | bytes 1540
  11.4 44.2 %all-to-all-start = ((bf16[64,64,128]{2,1,0:T(8,128)(2,1)}), bf16[64,64,128]{2,1,0:T(8,128)(2,1)S(1)}, u32[]{:S(2)}, u32[]{:S(2)}) async-start(bf16[64,64,128]{2,1,0:T(8,128)(2,1)} %bitcast.1), calls=%async_computation | async-start | bytes 2097152 | tf_op jit(solution)/shard_map/all_to_all | solution.py:294
  31.3 0.6 copy-start.19
  43.2 1.2 copy-start.5
  44.5 1.2 copy-start.7
  91.7 0.7 copy-start.14
  92.4 11.5 %all-to-all-start.2 = ((f32[8,8,512]{2,1,0:T(8,128)}), f32[8,8,512]{2,1,0:T(8,128)S(1)}, u32[]{:S(2)}, u32[]{:S(2)}) async-start(f32[8,8,512]{2,1,0:T(8,128)} %copy-done.14), calls=%async_computation.2 | async-start | bytes 262144 | tf_op jit(solution)/shard_map/all_to_all | solution.py:294
  96.5 1.0 copy-start.1
  103.9 1.2 copy-start.2
  106.2 0.8 copy-start.12
  107.0 1.1 copy-start.6
  108.1 30.1 %all-to-all-start.3 = ((bf16[64,96,128]{2,1,0:T(8,128)(2,1)}), bf16[64,96,128]{2,1,0:T(8,128)(2,1)S(1)}, u32[]{:S(2)}, u32[]{:S(2)}) async-start(bf16[64,96,128]{2,1,0:T(8,128)(2,1)} %bitcast.27), calls=%async_computation.3 | async-start | bytes 3145728 | tf_op jit(solution)/shard_map/all_to_all | solution.py:294
  114.3 1.0 copy-start.13
  116.1 1.0 copy-start
  117.1 26.1 %copy-start.20 = (f32[8,128]{1,0:T(8,128)S(1)}, f32[8,128]{1,0:T(8,128)}, u32[]{:S(2)}) copy-start(f32[8,128]{1,0:T(8,128)} %copy-done.19) | copy-start | bytes 12292
  138.3 35.3 %all-to-all-start.4 = ((bf16[64,64,128]{2,1,0:T(8,128)(2,1)}), bf16[64,64,128]{2,1,0:T(8,128)(2,1)S(1)}, u32[]{:S(2)}, u32[]{:S(2)}) async-start(bf16[64,64,128]{2,1,0:T(8,128)(2,1)} %bitcast.25), calls=%async_computation.4 | async-start | bytes 2097152 | tf_op jit(solution)/shard_map/all_to_all | solution.py:294
  143.1 1.4 copy-start.8
  144.5 29.0 %copy-start.4 = (bf16[32,64,64]{2,1,0:T(8,128)(2,1)S(1)}, bf16[32,64,64]{2,1,0:T(8,128)(2,1)}, u32[]{:S(2)}) copy-start(bf16[32,64,64]{2,1,0:T(8,128)(2,1)} %msa.3) | copy-start | bytes 786436
  144.5 29.0 %copy-start.16 = (bf16[64,64]{1,0:T(8,128)(2,1)S(1)}, bf16[64,64]{1,0:T(8,128)(2,1)}, u32[]{:S(2)}) copy-start(bf16[64,64]{1,0:T(8,128)(2,1)} %wc.3) | copy-start | bytes 24580
  144.5 29.0 %copy-start.18 = (bf16[64,64]{1,0:T(8,128)(2,1)S(1)}, bf16[64,64]{1,0:T(8,128)(2,1)}, u32[]{:S(2)}) copy-start(bf16[64,64]{1,0:T(8,128)(2,1)} %ws.3) | copy-start | bytes 24580
  144.5 29.0 %copy-start.23 = (f32[64]{0:T(128)S(1)}, f32[64]{0:T(128)}, u32[]{:S(2)}) copy-start(f32[64]{0:T(128)} %param.19) | copy-start | bytes 772
  173.6 1.0 copy-start.10

commit v2 on v1

--- a/solution.py
+++ b/solution.py
@@ -13,6 +13,7 @@
 BF = jnp.bfloat16
 F32 = jnp.float32
 VMEM = pltpu.CompilerParams(vmem_limit_bytes=48 * 1024 * 1024)
+WHOLE = pltpu.CompilerParams(vmem_limit_bytes=60 * 1024 * 1024)
 HALF = 64
 
 
@@ -47,37 +48,60 @@
         out_ref[s * 64 : (s + 1) * 64, :] = jnp.where(owner == s, wide, 0.0).astype(BF)
 
 
-def standardize(x):
-    center = x - jnp.mean(x, -1, keepdims=True)
-    scale = lax.rsqrt(jnp.mean(center * center, -1, keepdims=True) + EPS)
+def averager():
+    half = (iota((128, 128), 0) < 64) == (iota((128, 128), 1) < 64)
+    return jnp.where(half, 1.0 / 64, 0.0).astype(BF)
+
+
+def half_means(x, ones):
+    hi = x.astype(BF)
+    return mm(hi, ones) + mm((x - hi.astype(F32)).astype(BF), ones)
+
+
+def paired(x):
+    return jnp.concatenate([jnp.concatenate([x(2 * k), x(2 * k + 1)], axis=1) for k in range(16)], axis=0)
+
+
+def beside(x, d):
+    return jnp.concatenate([x[(d * 8 + k) * 64 : (d * 8 + k + 1) * 64] for k in range(8)], axis=1)
+
+
+def standardize(x, ones):
+    center = x.astype(F32) - mm(x, ones)
+    scale = lax.rsqrt(half_means(center * center, ones) + EPS)
     return center * scale, scale
 
 
-def msa_forward(flags, msa, adj, gain, wc, ws, wf, u_out, v_out, t_out, bdc, bds, bdf):
-    spread(wc[...], False, bdc)
+def twice(gain):
+    return jnp.concatenate([gain[...], gain[...]], axis=1)
+
+
+def msa_updates(flags, msa, adj, gain, ws, wf, u_out, t_out, bds, bdf):
     spread(ws[...], False, bds)
     spread(wf[...], True, bdf)
-    g = gain[...]
+    normed, _ = standardize(paired(lambda s: msa[s]), averager())
+    normed = (normed * twice(gain)).astype(BF)
+    masked = paired(lambda s: (adj[s].astype(F32) * flags[s].astype(F32)).astype(BF))
     for d in range(2):
-        normed, masked = [], []
-        for s in range(16):
-            row = d * 16 + s
-            normed.append((standardize(msa[row].astype(F32))[0] * g).astype(BF))
-            masked.append((adj[row].astype(F32) * flags[row].astype(F32)).astype(BF))
-        x = jnp.concatenate(normed, axis=1)
-        y = jnp.concatenate(masked, axis=1)
-        values = mm(x, bdc[...]).astype(BF)
-        gate = jax.nn.sigmoid(mm(x, bds[...]))
-        upstream = mm(y, bdf[...])
-        moved = gate * upstream
+        gate = jax.nn.sigmoid(mm(beside(normed, d), bds[...]))
+        moved = gate * mm(beside(masked, d), bdf[...])
         update = moved.astype(BF)
         tail = moved * (1.0 - gate)
         for h in range(8):
             cols = slice(h * 128, (h + 1) * 128)
-            v_out[h, d] = values[:, cols]
             t_out[h, d] = tail[:, cols]
             for b in range(4):
                 u_out[h, d, b] = update[:, cols]
+
+
+def msa_values(msa, gain, wc, v_out, bdc):
+    spread(wc[...], False, bdc)
+    normed, _ = standardize(paired(lambda s: msa[s]), averager())
+    normed = (normed * twice(gain)).astype(BF)
+    for d in range(2):
+        values = mm(beside(normed, d), bdc[...]).astype(BF)
+        for h in range(8):
+            v_out[h, d] = values[:, h * 128 : (h + 1) * 128]
 
 
 def partner(x, k, lane):
@@ -89,7 +113,7 @@
     ones8 = jnp.full((8, 128), 1.0 / 128, F32)
     lhs = jnp.concatenate([w_hi, w_mid, w_lo, ones8], axis=0).astype(BF)
     ones8 = ones8.astype(BF)
-    averager = jnp.full((128, 128), 1.0 / 128, F32).astype(BF)
+    mean = jnp.full((128, 128), 1.0 / 128, F32).astype(BF)
     b_lhs = jnp.concatenate(list(split3(table[...])) + [jnp.zeros((8, 128), F32)], axis=0).astype(BF)
     lane = iota((8, 128), 1)
     klass = iota((128, 1024), 0)
@@ -97,7 +121,7 @@
         x = jnp.concatenate(
             [pair[e * 32 + g * 8 + rho] for rho in range(8) for e in range(2)], axis=0
         )
-        center = x.astype(F32) - mm(x, averager)
+        center = x.astype(F32) - mm(x, mean)
         square = center * center
         s_hi = square.astype(BF)
         s_lo = (square - s_hi.astype(F32)).astype(BF)
@@ -136,7 +160,7 @@
             out[h, d, 0, 96:112, :] = packed
 
 
-def merge_products(ub, vw, p_out, stats, m_s):
+def merge_products(block, ub, vw, p_out, stats, c0, c1, c2, c3, m_s, c_s):
     lane = iota((128, 128), 1)
     quarter = lane // 32
     left = lane < HALF
@@ -171,7 +195,9 @@
         v = jnp.concatenate([vw[r + k, :, 0:64, :].reshape(512, 128) for k in range(2)], axis=1)
         c = mm(p, v)
         for k in range(2):
-            acc += ub[r + k].reshape(512, 128).astype(F32) * c[:, k * 128 : (k + 1) * 128]
+            part = c[:, k * 128 : (k + 1) * 128]
+            acc += ub[r + k].reshape(512, 128).astype(F32) * part
+            c_s[r + k] = part.astype(BF)
     score = jnp.sum(acc, axis=1, keepdims=True)
     column = iota((512, 128), 1)
     mixed = jnp.where(
@@ -179,9 +205,12 @@
         m_s[...].reshape(512, 128),
         jnp.where(column == 1, total, jnp.where(column == 2, score, 0.0)),
     )
-    rows = jnp.transpose(mixed)[0:8]
-    for k in range(8):
-        stats[k] = rows
+    stats[...] = jnp.transpose(mixed)[0:8]
+    for k, out in enumerate((c0, c1, c2, c3)):
+        for d in range(2):
+            start = pl.multiple_of(d * 256 + (block[0] ^ k) * 64, 64)
+            for r in range(8):
+                out[r, d] = c_s[r, pl.ds(start, 64), :]
 
 
 def score_products(ub, vw, out):
@@ -193,17 +222,21 @@
     out[...] = acc
 
 
-def gradients(stats, own, p_in, ub, scores, p_out, out):
-    tops, totals, sums = stats[:, 0, :], stats[:, 1, :], stats[:, 2, :]
-    peak = jnp.max(tops, axis=0, keepdims=True)
-    factor = jnp.exp(tops - peak)
-    total = 0.5 * jnp.sum(factor * totals, axis=0, keepdims=True)
-    row_total = jnp.sum(factor * sums, axis=0, keepdims=True) / total
-    mine = jnp.exp(own[0:1, :] - peak) / total
+def streamed(stats):
+    rows = [x[...] for x in stats]
+    peak = functools.reduce(jnp.maximum, [x[0:1] for x in rows])
+    factor = [jnp.exp(x[0:1] - peak) for x in rows]
+    total = sum(f * x[1:2] for f, x in zip(factor, rows))
+    return [f / total for f in factor], rows
+
+
+def gradients(own, first, second, third, p_in, ub, scores, *rest):
+    out = rest[-1]
+    share, rows = streamed((own, first, second, third))
+    row_total = sum(f * x[2:3] for f, x in zip(share, rows))
     which = iota((8, 512), 0)
-    columns = jnp.transpose(jnp.where(which == 0, mine, jnp.where(which == 1, 0.5 * row_total, 0.0)))
+    columns = jnp.transpose(jnp.where(which == 0, share[0], jnp.where(which == 1, row_total, 0.0)))
     p = (p_in[...].reshape(512, 512).astype(F32) * columns[:, 0:1]).astype(BF)
-    p_out[...] = p
     grad = (p.astype(F32) * (scores[...] - columns[:, 1:2])).reshape(8, 2, 32, 512)
     left = iota((256, 128), 1) < HALF
     for cp in range(4):
@@ -221,12 +254,18 @@
             out[r + k, :, 0:64, :] = grad_v[:, k * 128 : (k + 1) * 128].reshape(8, 64, 128)
 
 
-def context_products(p, vw, out):
-    for r in range(0, 8, 2):
-        v = jnp.concatenate([vw[r + k, :, 0:64, :].reshape(512, 128) for k in range(2)], axis=1)
-        c = mm(p[...], v).astype(BF)
-        for k in range(2):
-            out[r + k] = c[:, k * 128 : (k + 1) * 128].reshape(8, 64, 128)
+def context_sum(block, own, first, second, third, c0, c1, c2, c3, out, f_s):
+    share, _ = streamed((own, first, second, third))
+    which = iota((8, 512), 0)
+    mixed = jnp.zeros((8, 512), F32)
+    for k in range(4):
+        mixed = jnp.where(which == k, share[k], mixed)
+    f_s[...] = jnp.transpose(mixed)
+    for d in range(2):
+        f = f_s[pl.ds(pl.multiple_of(d * 256 + block[0] * 64, 64), 64), :]
+        for r in range(8):
+            parts = [c[r, d].astype(F32) * f[:, k : k + 1] for k, c in enumerate((c0, c1, c2, c3))]
+            out[r, d] = ((parts[0] + parts[1]) + (parts[2] + parts[3])).astype(BF)
 
 
 def pair_backward(pair, grads, saved, proj, out, g_s):
@@ -260,59 +299,76 @@
                 out[i] = (base[rows] - steep[rows] * pair[i].astype(F32)).astype(BF)
 
 
-def msa_backward(msa, gain, wc, ws, gb, cb, tail, out, bdc, bds):
+def msa_partial(msa, wc, gb, normed_out, scale_out, grad_out, bdc):
     spread(wc[...], False, bdc)
-    spread(ws[...], False, bds)
-    g = gain[...]
+    normed, scale = standardize(paired(lambda s: msa[s]), averager())
+    normed_out[...] = normed
+    scale_out[...] = scale
     for d in range(2):
-        value_grad, gate_grad = [], []
+        value_grad = []
         for h in range(8):
             total = gb[h, d, 0, 0:64, :].astype(F32)
-            context = cb[h, d, 0].astype(F32)
             for k in range(1, 4):
                 total += gb[h, d, k, 0:64, :].astype(F32)
-                context += cb[h, d, k].astype(F32)
             value_grad.append(total.astype(BF))
-            gate_grad.append((tail[h, d] * context).astype(BF))
-        grad = mm_nt(jnp.concatenate(value_grad, axis=1), bdc[...])
-        grad += mm_nt(jnp.concatenate(gate_grad, axis=1), bds[...])
-        for s in range(16):
-            row = d * 16 + s
-            normed, scale = standardize(msa[row].astype(F32))
-            scaled = grad[:, s * 64 : (s + 1) * 64] * g
-            out[row] = (
-                scale
-                * (
-                    scaled
-                    - jnp.mean(scaled, -1, keepdims=True)
-                    - normed * jnp.mean(scaled * normed, -1, keepdims=True)
-                )
-            ).astype(BF)
+        grad_out[d] = mm_nt(jnp.concatenate(value_grad, axis=1), bdc[...])
+
+
+def msa_backward(gain, ws, context, tail, normed, scale, partial, out, bds):
+    spread(ws[...], False, bds)
+    grads = []
+    for d in range(2):
+        gate_grad = [(tail[h, d] * context[h, d].astype(F32)).astype(BF) for h in range(8)]
+        grad = partial[d] + mm_nt(jnp.concatenate(gate_grad, axis=1), bds[...])
+        grads += [grad[:, k * 128 : (k + 1) * 128] for k in range(8)]
+    ones = averager()
+    scaled = jnp.concatenate(grads, axis=0) * twice(gain)
+    xhat = normed[...]
+    result = scale[...] * (
+        scaled - half_means(scaled, ones) - xhat * half_means(scaled * xhat, ones)
+    )
+    for k in range(16):
+        rows = result[k * 64 : (k + 1) * 64]
+        out[2 * k] = rows[:, 0:64].astype(BF)
+        out[2 * k + 1] = rows[:, 64:128].astype(BF)
 
 
 def exchange(x, axes):
     return lax.all_to_all(x, axes, 0, 0, tiled=True)
 
 
+def swap(x, k):
+    return lax.ppermute(x, "b", [(i, i ^ k) for i in range(4)])
+
+
 def shape(dims, dtype):
     return jax.ShapeDtypeStruct(dims, dtype)
 
 
 def shards(msa, pair, adj, flags, chains, positions, msa_gain, pair_gain, wc, ws, wf, wp, table):
-    vm = pl.BlockSpec(memory_space=pltpu.VMEM)
+    vm = pl.BlockSpec()
     sm = pl.BlockSpec(memory_space=pltpu.SMEM)
     gp, gq = ("row", "d", "a"), ("row", "d", "b")
     gain = msa_gain.reshape(1, 64)
 
-    u_send, values, tail = pl.pallas_call(
-        msa_forward,
-        out_shape=(shape((8, 2, 4, 64, 128), BF), shape((8, 2, 64, 128), BF), shape((8, 2, 64, 128), F32)),
-        in_specs=[sm] + [vm] * 6,
-        out_specs=(vm, vm, vm),
-        scratch_shapes=[pltpu.VMEM((1024, 1024), BF)] * 3,
-        compiler_params=VMEM,
-        name="msa_forward",
-    )(flags, msa, adj, gain, wc, ws, wf)
+    u_send, tail = pl.pallas_call(
+        msa_updates,
+        out_shape=(shape((8, 2, 4, 64, 128), BF), shape((8, 2, 64, 128), F32)),
+        in_specs=[sm] + [vm] * 5,
+        out_specs=(vm, vm),
+        scratch_shapes=[pltpu.VMEM((1024, 1024), BF)] * 2,
+        compiler_params=WHOLE,
+        name="msa_updates",
+    )(flags, msa, adj, gain, ws, wf)
+    values = pl.pallas_call(
+        msa_values,
+        out_shape=shape((8, 2, 64, 128), BF),
+        in_specs=[vm] * 3,
+        out_specs=vm,
+        scratch_shapes=[pltpu.VMEM((1024, 1024), BF)],
+        compiler_params=WHOLE,
+        name="msa_values",
+    )(msa, gain, wc)
     ub = exchange(u_send.reshape(64, 64, 128), gq).reshape(8, 8, 64, 128)
 
     row = lax.axis_index("row")
@@ -355,16 +411,19 @@
     )(pair, bins, proj, table_t, values)
     vw = exchange(vw_send.reshape(64, 112, 128), gp).reshape(8, 8, 112, 128)
 
-    p_raw, stats = pl.pallas_call(
+    block = lax.axis_index("b").reshape(1)
+    piece = shape((8, 2, 64, 128), BF)
+    p_raw, stats, *pieces = pl.pallas_call(
         merge_products,
-        out_shape=(shape((8, 2, 2, 16, 512), BF), shape((8, 8, 512), F32)),
-        in_specs=[vm, vm],
-        out_specs=(vm, vm),
-        scratch_shapes=[pltpu.VMEM((8, 2, 2, 16, 128), F32)],
+        out_shape=(shape((8, 2, 2, 16, 512), BF), shape((8, 512), F32)) + (piece,) * 4,
+        in_specs=[sm, vm, vm],
+        out_specs=(vm,) * 6,
+        scratch_shapes=[pltpu.VMEM((8, 2, 2, 16, 128), F32), pltpu.VMEM((8, 512, 128), BF)],
         compiler_params=VMEM,
         name="merge_products",
-    )(ub, vw)
-    all_stats = exchange(stats, ("d", "b"))
+    )(block, ub, vw)
+    shares = [stats] + [swap(stats, k) for k in (1, 2, 3)]
+    pieces = pieces[:1] + [swap(pieces[k], k) for k in (1, 2, 3)]
     scores = pl.pallas_call(
         score_products,
         out_shape=shape((512, 512), F32),
@@ -373,24 +432,25 @@
         compiler_params=VMEM,
         name="score_products",
     )(ub, vw)
-    p, gd_send = pl.pallas_call(
+    gd_send = pl.pallas_call(
         gradients,
-        out_shape=(shape((512, 512), BF), shape((8, 8, 96, 128), BF)),
-        in_specs=[vm] * 5,
-        out_specs=(vm, vm),
+        out_shape=shape((8, 8, 96, 128), BF),
+        in_specs=[vm] * 7 + [pl.BlockSpec(memory_space=pl.ANY)] * 2,
+        out_specs=vm,
         compiler_params=VMEM,
         name="gradients",
-    )(all_stats, stats[0], p_raw, ub, scores)
+    )(*shares, p_raw, ub, scores, pieces[1], pieces[3])
     gd = exchange(gd_send.reshape(64, 96, 128), gp).reshape(8, 2, 4, 96, 128)
-    c_send = pl.pallas_call(
-        context_products,
-        out_shape=shape((8, 8, 64, 128), BF),
-        in_specs=[vm, vm],
+    context_send = pl.pallas_call(
+        context_sum,
+        out_shape=piece,
+        in_specs=[sm] + [vm] * 8,
         out_specs=vm,
-        compiler_params=VMEM,
-        name="context_products",
-    )(p, vw)
-    cb = exchange(c_send.reshape(64, 64, 128), gq).reshape(8, 2, 4, 64, 128)
+        scratch_shapes=[pltpu.VMEM((512, 8), F32)],
+        compiler_params=VMEM,
+        name="context_sum",
+    )(block, *shares, *pieces)
+    context = exchange(context_send.reshape(16, 64, 128), ("row", "d")).reshape(8, 2, 64, 128)
     pair_gradient = pl.pallas_call(
         pair_backward,
         grid=(4,),
@@ -406,15 +466,24 @@
         compiler_params=VMEM,
         name="pair_backward",
     )(pair, gd, saved, proj)
+    partial = pl.pallas_call(
+        msa_partial,
+        out_shape=(shape((1024, 128), F32), shape((1024, 128), F32), shape((2, 64, 1024), F32)),
+        in_specs=[vm] * 3,
+        out_specs=(vm, vm, vm),
+        scratch_shapes=[pltpu.VMEM((1024, 1024), BF)],
+        compiler_params=VMEM,
+        name="msa_partial",
+    )(msa, wc, gd)
     alignment_gradient = pl.pallas_call(
         msa_backward,
         out_shape=shape((32, 64, 64), BF),
         in_specs=[vm] * 7,
         out_specs=vm,
-        scratch_shapes=[pltpu.VMEM((1024, 1024), BF)] * 2,
+        scratch_shapes=[pltpu.VMEM((1024, 1024), BF)],
         compiler_params=VMEM,
         name="msa_backward",
-    )(msa, gain, wc, ws, gd, cb, tail)
+    )(gain, ws, context, tail, *partial)
     return (alignment_gradient, pair_gradient)
 
 

time: 185 us -> 161 us (0.87)
  the two profiles are of different devices: /device:TPU:1 before, /device:TPU:32 now
where the time goes in v2:
time: 161 us; the launch traced here: 159 us
  waiting for transfers between devices  45.9 us (29%)
  starting transfers between devices  38 us (24%)
  Pallas kernels  35.5 us (22%)
  blocking collectives  30.1 us (19%)
  local copies, waits for them, and re-layouts  8.4 us (5%)
    ppermute x6, waiting for transfers between devices, swap(): return lax.ppermute(x, 'b', [(i, i ^ k) for i in range(4)])  36.1 us
    all_to_all x1, blocking collectives, exchange(): return lax.all_to_all(x, axes, 0, 0, tiled=True)  30.1 us
    all_to_all x3, starting transfers between devices, exchange(): return lax.all_to_all(x, axes, 0, 0, tiled=True)  26.7 us
    ppermute x6, starting transfers between devices, swap(): return lax.ppermute(x, 'b', [(i, i ^ k) for i in range(4)])  11.3 us
    pallas_call x1, Pallas kernels, shards(): pl.pallas_call(pair_forward, grid=(4,), out_shape=(shape((8, 2, 4, 112, 1...  11.3 us
    all_to_all x3, waiting for transfers between devices, exchange(): return lax.all_to_all(x, axes, 0, 0, tiled=True)  9.8 us
    pallas_call x1, Pallas kernels, shards(): pl.pallas_call(pair_backward, grid=(4,), out_shape=shape((256, 64, 128),...  6.38 us
    pallas_call x1, Pallas kernels, shards(): pl.pallas_call(msa_updates, out_shape=(shape((8, 2, 4, 64, 128), BF), sha...  4.55 us
  transfers between devices with their start and end apart: 9, of which 4 were waited for; matrix products, arithmetic and copies ran while one was open for 3% of the time, Pallas kernels for 15%

profile of v2, /device:TPU:32, one launch (start us, length us, event | category | flops | bytes accessed | tf_op | source)
XLA Modules:
  0.0 159.1 jit_solution(13294289821153572532)
XLA Ops:
  0.6 4.5 %msa_updates.1 = (bf16[8,2,4,64,128]{4,3,2,1,0:T(8,128)(2,1)}, f32[8,2,64,128]{3,2,1,0:T(8,128)}) custom-call(s32[32]{0:T(128)} %flags.1, bf16[32,64,64]{2,1,0:T(8,128)(2,1)} %msa.5, bf16[32,64,64]{2,1,0:T(8,128)(2,1)} %adj.1, f32[1,64]{1,0:T(1,128)} %bitcast.24, bf16[64,64]{1,0:T(8,128)(2,1)} %ws.3, bf16[64,64]{1,0:T(8,128)(2,1)} %wf.1), custom_call_target="tpu_custom_call" | custom-call | tf_op jit(solution)/shard_map/msa_updates/pallas_call | solution.py:354
  5.2 13.8 %all-to-all-start = ((bf16[64,64,128]{2,1,0:T(8,128)(2,1)}), bf16[64,64,128]{2,1,0:T(8,128)(2,1)S(1)}, u32[]{:S(2)}, u32[]{:S(2)}) async-start(bf16[64,64,128]{2,1,0:T(8,128)(2,1)} %bitcast.27), calls=%async_computation | async-start | bytes 2097152 | tf_op jit(solution)/shard_map/all_to_all | solution.py:337
  19.0 0.8 dynamic_slice.13
  19.8 0.8 dynamic_slice.15
  20.5 0.8 dynamic_slice.12
  21.3 0.8 dynamic_slice.14
  22.1 0.1 sub.39
  22.1 0.1 eq.29
  22.2 0.1 reshape.132
  22.3 0.1 reshape.131
  22.4 0.2 copy.15
  22.6 0.2 copy.16
  22.8 0.2 sub.36
  23.0 0.1 sub.37
  23.1 0.2 eq.26
  23.3 0.1 eq.27
  23.5 3.2 %msa_values.1.v_in = bf16[8,2,64,128]{3,2,1,0:T(8,128)(2,1)} custom-call(bf16[32,64,64]{2,1,0:T(8,128)(2,1)} %msa.5, f32[1,64]{1,0:T(1,128)} %bitcast.25, bf16[64,64]{1,0:T(8,128)(2,1)} %wc.3), custom_call_target="tpu_custom_call" | custom-call | tf_op jit(solution)/shard_map/msa_values/pallas_call | solution.py:363
  26.7 0.1 multiply_reduce_fusion
  26.8 0.1 subtract_bitcast_fusion.proj
  26.9 0.1 compare_select_fusion.bins
  27.0 0.9 copy-done.3
  28.0 11.3 %pair_forward.1 = (bf16[8,2,4,112,128]{4,3,2,1,0:T(8,128)(2,1)S(1)}, f32[16,24,1024]{2,1,0:T(8,128)S(1)}) custom-call(bf16[256,64,128]{2,1,0:T(8,128)(2,1)} %pair.3, s32[16,1,1024]{2,1,0:T(1,128)S(1)} %compare_select_fusion.bins, f32[8,128]{1,0:T(8,128)S(1)} %subtract_bitcast_fusion.proj, f32[8,128]{1,0:T(8,128)S(1)} %pad.4.table, ...), custom_call_target="tpu_custom_call" | custom-call | tf_op jit(solution)/shard_map/pair_forward/pallas_call | solution.py:393
  39.3 1.2 copy-done.1
  40.4 9.8 %all-to-all-done = bf16[64,64,128]{2,1,0:T(8,128)(2,1)S(1)} async-done(((bf16[64,64,128]{2,1,0:T(8,128)(2,1)}), bf16[64,64,128]{2,1,0:T(8,128)(2,1)S(1)}, u32[]{:S(2)}, u32[]{:S(2)}) %all-to-all-start) | async-done | bytes 1048608 | tf_op jit(solution)/shard_map/all_to_all | solution.py:337
  50.2 30.1 %all_to_all.20 = bf16[64,112,128]{2,1,0:T(8,128)(2,1)S(1)} all-to-all(bf16[64,112,128]{2,1,0:T(8,128)(2,1)S(1)} %bitcast.22), channel_id=1, replica_groups=mesh['row'=8,'d'=2,'b'=4,'a'=4] {'row','d','a'}, dimensions={0} | all-to-all | bytes 3670016 | tf_op jit(solution)/shard_map/all_to_all | solution.py:337
  80.3 1.6 %merge_products.1 = (bf16[8,2,2,16,512]{4,3,2,1,0:T(8,128)(2,1)S(1)}, f32[8,512]{1,0:T(8,128)S(1)}, bf16[8,2,64,128]{3,2,1,0:T(8,128)(2,1)S(1)}, bf16[8,2,64,128...) custom-call(s32[1]{0:T(128)} %bitcast.1.block, ...), custom_call_target="tpu_custom_call" | custom-call | tf_op jit(solution)/shard_map/merge_products/pallas_call | solution.py:416
  82.0 1.7 %collective-permute-start.3 = (bf16[8,2,64,128]{3,2,1,0:T(8,128)(2,1)S(1)}, bf16[8,2,64,128]{3,2,1,0:T(8,128)(2,1)S(1)}, u32[]{:S(2)}, u32[]{:S(2)}) collective-permute-start(bf16[8,2,64,128]{3,2,1,0:T(8,128)(2,1)S(1)} %get-tuple-element.19), channel_id=1, source_target_pairs={{0,4},{4,0},{8,12},{12,8},{1,5},{5,1},{9,13},{13,9},{2,6},{6,2},{1... | collective-permute-start | bytes 786440 | tf_op jit(solution)/shard_map/ppermute | solution.py:341
  83.6 0.9 collective-permute-start.5
  84.5 3.2 %collective-permute-start.2 = (f32[8,512]{1,0:T(8,128)S(1)}, f32[8,512]{1,0:T(8,128)S(1)}, u32[]{:S(2)}, u32[]{:S(2)}) collective-permute-start(f32[8,512]{1,0:T(8,128)S(1)} %get-tuple-element.17.own), channel_id=1, source_target_pairs={{0,12},{4,8},{8,4},{12,0},{1,13},{5,9},{9,5},{13,1},{2,14},{6,10},... | collective-permute-start | bytes 49160 | tf_op jit(solution)/shard_map/ppermute | solution.py:341
  87.8 2.7 %collective-permute-start.1 = (f32[8,512]{1,0:T(8,128)S(1)}, f32[8,512]{1,0:T(8,128)S(1)}, u32[]{:S(2)}, u32[]{:S(2)}) collective-permute-start(f32[8,512]{1,0:T(8,128)S(1)} %get-tuple-element.17.own), channel_id=1, source_target_pairs={{0,8},{4,12},{8,0},{12,4},{1,9},{5,13},{9,1},{13,5},{2,10},{6,14},... | collective-permute-start | bytes 49160 | tf_op jit(solution)/shard_map/ppermute | solution.py:341
  90.5 0.6 collective-permute-start
  91.0 0.7 score_products.1.scores
  91.8 7.7 %collective-permute-done.2.third = f32[8,512]{1,0:T(8,128)S(1)} collective-permute-done((f32[8,512]{1,0:T(8,128)S(1)}, f32[8,512]{1,0:T(8,128)S(1)}, u32[]{:S(2)}, u32[]{:S(2)}) %collective-permute-start.2) | collective-permute-done | bytes 16416 | tf_op jit(solution)/shard_map/ppermute | solution.py:341
  99.4 0.9 collective-permute-done.1.second
  100.3 0.0 collective-permute-done.first
  100.3 0.0 collective-permute-done.3.c1.rest_0_
  100.4 0.0 collective-permute-done.5.c3.rest_1_
  100.4 2.2 %gradients.1 = bf16[8,8,96,128]{3,2,1,0:T(8,128)(2,1)} custom-call(f32[8,512]{1,0:T(8,128)S(1)} %get-tuple-element.17.own, f32[8,512]{1,0:T(8,128)S(1)} %collective-permute-done.first, f32[8,512]{1,0:T(8,128)S(1)} %collective-permute-done.1.second, f32[8,512]{1,0:T(8,128)S(1)} %collective-permute-done.2.third, ...), custom_call_target="tpu_custom_call" | custom-call | tf_op jit(solution)/shard_map/gradients/pallas_call | solution.py:435
  102.6 6.0 %all-to-all-start.3 = ((bf16[64,96,128]{2,1,0:T(8,128)(2,1)}), bf16[64,96,128]{2,1,0:T(8,128)(2,1)S(1)}, u32[]{:S(2)}, u32[]{:S(2)}) async-start(bf16[64,96,128]{2,1,0:T(8,128)(2,1)} %bitcast.12), calls=%async_computation.3 | async-start | bytes 3145728 | tf_op jit(solution)/shard_map/all_to_all | solution.py:337
  108.6 2.3 %collective-permute-start.4 = (bf16[8,2,64,128]{3,2,1,0:T(8,128)(2,1)S(1)}, bf16[8,2,64,128]{3,2,1,0:T(8,128)(2,1)S(1)}, u32[]{:S(2)}, u32[]{:S(2)}) collective-permute-start(bf16[8,2,64,128]{3,2,1,0:T(8,128)(2,1)S(1)} %get-tuple-element.20), channel_id=1, source_target_pairs={{0,8},{4,12},{8,0},{12,4},{1,9},{5,13},{9,1},{13,5},{2,10},{6,14},... | collective-permute-start | bytes 786440 | tf_op jit(solution)/shard_map/ppermute | solution.py:341
  110.8 27.5 %collective-permute-done.4.c2 = bf16[8,2,64,128]{3,2,1,0:T(8,128)(2,1)S(1)} collective-permute-done((bf16[8,2,64,128]{3,2,1,0:T(8,128)(2,1)S(1)}, bf16[8,2,64,128]{3,2,1,0:T(8,128)(2,1)S(1)}, u32[]{:S(2)}, u32[]{:S(2)}) %collective-permute-start.4) | collective-permute-done | bytes 262176 | tf_op jit(solution)/shard_map/ppermute | solution.py:341
  138.3 1.2 context_sum.1
  139.5 6.9 %all-to-all-start.2 = ((bf16[16,64,128]{2,1,0:T(8,128)(2,1)}), bf16[16,64,128]{2,1,0:T(8,128)(2,1)S(1)}, u32[]{:S(2)}, u32[]{:S(2)}) async-start(bf16[16,64,128]{2,1,0:T(8,128)(2,1)} %bitcast.10), calls=%async_computation.2 | async-start | bytes 524288 | tf_op jit(solution)/shard_map/all_to_all | solution.py:337
  146.4 1.7 %msa_partial.1 = (f32[1024,128]{1,0:T(8,128)S(1)}, f32[1024,128]{1,0:T(8,128)S(1)}, f32[2,64,1024]{2,1,0:T(8,128)S(1)}) custom-call(bf16[32,64,64]{2,1,0:T(8,128)(2,1)S(1)} %copy-done, bf16[64,64]{1,0:T(8,128)(2,1)S(1)} %copy-done.8, bf16[8,2,4,96,128]{4,3,2,1,0:T(8,128)(2,1)S(1)} %bitcast.20), custom_call_target="tpu_custom_call" | custom-call | tf_op jit(solution)/shard_map/msa_partial/pallas_call | solution.py:469
  148.2 0.8 copy-done.5
  149.0 6.4 %pair_backward.1 = bf16[256,64,128]{2,1,0:T(8,128)(2,1)} custom-call(bf16[256,64,128]{2,1,0:T(8,128)(2,1)} %pair.3, bf16[8,2,4,96,128]{4,3,2,1,0:T(8,128)(2,1)S(1)} %bitcast.21, f32[16,24,1024]{2,1,0:T(8,128)S(1)} %copy-done.2, f32[8,128]{1,0:T(8,128)S(1)} %subtract_bitcast_fusion.proj), custom_call_target="tpu_custom_call" | custom-call | tf_op jit(solution)/shard_map/pair_backward/pallas_call | solution.py:454
  155.4 1.0 copy-done.6
  156.4 2.7 %msa_backward.1 = bf16[32,64,64]{2,1,0:T(8,128)(2,1)} custom-call(f32[1,64]{1,0:T(1,128)S(1)} %bitcast.26, bf16[64,64]{1,0:T(8,128)(2,1)S(1)} %copy-done.7, bf16[8,2,64,128]{3,2,1,0:T(8,128)(2,1)S(1)} %bitcast.23, f32[8,2,64,128]{3,2,1,0:T(8,128)S(1)} %copy-done.4, f32[1024,128]{1,0:T(8,128)S(1)} %get-tuple-element.24.normed, ...), custom_call_target="tpu_custom_call" | custom-call | tf_op jit(solution)/shard_map/msa_backward/pallas_call | solution.py:478
  (28 shorter events, 0.1 us)
Async XLA Ops:
  5.2 21.5 %copy-start.11 = (f32[66,8]{0,1:T(8,128)S(1)}, f32[66,8]{0,1:T(8,128)}, u32[]{:S(2)}) copy-start(f32[66,8]{0,1:T(8,128)} %param.25) | copy-start | bytes 6340
  5.2 21.5 %copy-start.10 = (f32[128,8]{0,1:T(8,128)S(1)}, f32[128,8]{0,1:T(8,128)}, u32[]{:S(2)}) copy-start(f32[128,8]{0,1:T(8,128)} %param.24) | copy-start | bytes 12292
  5.2 21.5 %copy-start.12 = (f32[128]{0:T(128)S(1)}, f32[128]{0:T(128)}, u32[]{:S(2)}) copy-start(f32[128]{0:T(128)} %param.20) | copy-start | bytes 1540
  5.2 45.1 %all-to-all-start = ((bf16[64,64,128]{2,1,0:T(8,128)(2,1)}), bf16[64,64,128]{2,1,0:T(8,128)(2,1)S(1)}, u32[]{:S(2)}, u32[]{:S(2)}) async-start(bf16[64,64,128]{2,1,0:T(8,128)(2,1)} %bitcast.27), calls=%async_computation | async-start | bytes 2097152 | tf_op jit(solution)/shard_map/all_to_all | solution.py:337
  27.0 1.0 copy-start.3
  39.3 1.2 copy-start.1
  82.0 18.4 %collective-permute-start.3 = (bf16[8,2,64,128]{3,2,1,0:T(8,128)(2,1)S(1)}, bf16[8,2,64,128]{3,2,1,0:T(8,128)(2,1)S(1)}, u32[]{:S(2)}, u32[]{:S(2)}) collective-permute-start(bf16[8,2,64,128]{3,2,1,0:T(8,128)(2,1)S(1)} %get-tuple-element.19), channel_id=1, source_target_pairs={{0,4},{4,0},{8,12},{12,8},{1,5},{5,1},{9,13},{13,9},{2,6},{6,2},{1... | collective-permute-start | bytes 786440 | tf_op jit(solution)/shard_map/ppermute | solution.py:341
  83.6 16.7 %collective-permute-start.5 = (bf16[8,2,64,128]{3,2,1,0:T(8,128)(2,1)S(1)}, bf16[8,2,64,128]{3,2,1,0:T(8,128)(2,1)S(1)}, u32[]{:S(2)}, u32[]{:S(2)}) collective-permute-start(bf16[8,2,64,128]{3,2,1,0:T(8,128)(2,1)S(1)} %get-tuple-element.21), channel_id=1, source_target_pairs={{0,12},{4,8},{8,4},{12,0},{1,13},{5,9},{9,5},{13,1},{2,14},{6,10},... | collective-permute-start | bytes 786440 | tf_op jit(solution)/shard_map/ppermute | solution.py:341
  84.5 14.9 %collective-permute-start.2 = (f32[8,512]{1,0:T(8,128)S(1)}, f32[8,512]{1,0:T(8,128)S(1)}, u32[]{:S(2)}, u32[]{:S(2)}) collective-permute-start(f32[8,512]{1,0:T(8,128)S(1)} %get-tuple-element.17.own), channel_id=1, source_target_pairs={{0,12},{4,8},{8,4},{12,0},{1,13},{5,9},{9,5},{13,1},{2,14},{6,10},... | collective-permute-start | bytes 49160 | tf_op jit(solution)/shard_map/ppermute | solution.py:341
  87.8 12.6 %collective-permute-start.1 = (f32[8,512]{1,0:T(8,128)S(1)}, f32[8,512]{1,0:T(8,128)S(1)}, u32[]{:S(2)}, u32[]{:S(2)}) collective-permute-start(f32[8,512]{1,0:T(8,128)S(1)} %get-tuple-element.17.own), channel_id=1, source_target_pairs={{0,8},{4,12},{8,0},{12,4},{1,9},{5,13},{9,1},{13,5},{2,10},{6,14},... | collective-permute-start | bytes 49160 | tf_op jit(solution)/shard_map/ppermute | solution.py:341
  90.5 9.9 %collective-permute-start = (f32[8,512]{1,0:T(8,128)S(1)}, f32[8,512]{1,0:T(8,128)S(1)}, u32[]{:S(2)}, u32[]{:S(2)}) collective-permute-start(f32[8,512]{1,0:T(8,128)S(1)} %get-tuple-element.17.own), channel_id=1, source_target_pairs={{0,4},{4,0},{8,12},{12,8},{1,5},{5,1},{9,13},{13,9},{2,6},{6,2},{1... | collective-permute-start | bytes 49160 | tf_op jit(solution)/shard_map/ppermute | solution.py:341
  102.6 43.9 %copy-start = (bf16[32,64,64]{2,1,0:T(8,128)(2,1)S(1)}, bf16[32,64,64]{2,1,0:T(8,128)(2,1)}, u32[]{:S(2)}) copy-start(bf16[32,64,64]{2,1,0:T(8,128)(2,1)} %msa.5) | copy-start | bytes 786436
  102.6 43.9 %copy-start.8 = (bf16[64,64]{1,0:T(8,128)(2,1)S(1)}, bf16[64,64]{1,0:T(8,128)(2,1)}, u32[]{:S(2)}) copy-start(bf16[64,64]{1,0:T(8,128)(2,1)} %wc.3) | copy-start | bytes 24580
  102.6 36.9 %all-to-all-start.3 = ((bf16[64,96,128]{2,1,0:T(8,128)(2,1)}), bf16[64,96,128]{2,1,0:T(8,128)(2,1)S(1)}, u32[]{:S(2)}, u32[]{:S(2)}) async-start(bf16[64,96,128]{2,1,0:T(8,128)(2,1)} %bitcast.12), calls=%async_computation.3 | async-start | bytes 3145728 | tf_op jit(solution)/shard_map/all_to_all | solution.py:337
  108.6 29.7 %collective-permute-start.4 = (bf16[8,2,64,128]{3,2,1,0:T(8,128)(2,1)S(1)}, bf16[8,2,64,128]{3,2,1,0:T(8,128)(2,1)S(1)}, u32[]{:S(2)}, u32[]{:S(2)}) collective-permute-start(bf16[8,2,64,128]{3,2,1,0:T(8,128)(2,1)S(1)} %get-tuple-element.20), channel_id=1, source_target_pairs={{0,8},{4,12},{8,0},{12,4},{1,9},{5,13},{9,1},{13,5},{2,10},{6,14},... | collective-permute-start | bytes 786440 | tf_op jit(solution)/shard_map/ppermute | solution.py:341
  139.5 15.9 %all-to-all-start.2 = ((bf16[16,64,128]{2,1,0:T(8,128)(2,1)}), bf16[16,64,128]{2,1,0:T(8,128)(2,1)S(1)}, u32[]{:S(2)}, u32[]{:S(2)}) async-start(bf16[16,64,128]{2,1,0:T(8,128)(2,1)} %bitcast.10), calls=%async_computation.2 | async-start | bytes 524288 | tf_op jit(solution)/shard_map/all_to_all | solution.py:337
  146.4 2.6 %copy-start.2 = (f32[16,24,1024]{2,1,0:T(8,128)S(1)}, f32[16,24,1024]{2,1,0:T(8,128)}, u32[]{:S(2)}) copy-start(f32[16,24,1024]{2,1,0:T(8,128)} %copy-done.1) | copy-start | bytes 4718596
  148.2 0.8 copy-start.5
  149.0 6.4 %copy-start.4 = (f32[8,2,64,128]{3,2,1,0:T(8,128)S(1)}, f32[8,2,64,128]{3,2,1,0:T(8,128)}, u32[]{:S(2)}) copy-start(f32[8,2,64,128]{3,2,1,0:T(8,128)} %get-tuple-element.22.tail) | copy-start | bytes 1572868
  149.0 6.4 %copy-start.7 = (bf16[64,64]{1,0:T(8,128)(2,1)S(1)}, bf16[64,64]{1,0:T(8,128)(2,1)}, u32[]{:S(2)}) copy-start(bf16[64,64]{1,0:T(8,128)(2,1)} %ws.3) | copy-start | bytes 24580
  149.0 6.4 %copy-start.9 = (f32[64]{0:T(128)S(1)}, f32[64]{0:T(128)}, u32[]{:S(2)}) copy-start(f32[64]{0:T(128)} %param.19) | copy-start | bytes 772
  155.4 1.0 copy-start.6

commit v3 on v2

--- a/solution.py
+++ b/solution.py
@@ -76,47 +76,56 @@
     return jnp.concatenate([gain[...], gain[...]], axis=1)
 
 
-def msa_updates(flags, msa, adj, gain, ws, wf, u_out, t_out, bds, bdf):
+def msa_forward(flags, msa, adj, gain, wc, ws, wf, u_out, v_out, t_out, bdc, bds, bdf):
+    spread(wc[...], False, bdc)
     spread(ws[...], False, bds)
     spread(wf[...], True, bdf)
     normed, _ = standardize(paired(lambda s: msa[s]), averager())
     normed = (normed * twice(gain)).astype(BF)
     masked = paired(lambda s: (adj[s].astype(F32) * flags[s].astype(F32)).astype(BF))
     for d in range(2):
-        gate = jax.nn.sigmoid(mm(beside(normed, d), bds[...]))
+        x = beside(normed, d)
+        values = mm(x, bdc[...]).astype(BF)
+        gate = jax.nn.sigmoid(mm(x, bds[...]))
         moved = gate * mm(beside(masked, d), bdf[...])
         update = moved.astype(BF)
         tail = moved * (1.0 - gate)
         for h in range(8):
             cols = slice(h * 128, (h + 1) * 128)
+            u_out[h, d] = update[:, cols]
+            v_out[h, d] = values[:, cols]
             t_out[h, d] = tail[:, cols]
-            for b in range(4):
-                u_out[h, d, b] = update[:, cols]
-
-
-def msa_values(msa, gain, wc, v_out, bdc):
-    spread(wc[...], False, bdc)
-    normed, _ = standardize(paired(lambda s: msa[s]), averager())
-    normed = (normed * twice(gain)).astype(BF)
-    for d in range(2):
-        values = mm(beside(normed, d), bdc[...]).astype(BF)
-        for h in range(8):
-            v_out[h, d] = values[:, h * 128 : (h + 1) * 128]
 
 
 def partner(x, k, lane):
     return jnp.where(lane & k == 0, pltpu.roll(x, 128 - k, 1), pltpu.roll(x, k, 1))
 
 
-def pair_forward(pair, bins, proj, table, v_in, out, saved, p_s, m_s):
-    w_hi, w_mid, w_lo = split3(proj[...])
+def pair_forward(
+    row, col, chain, position, chains, positions, pair, gain, wp, table, v_in, after,
+    out, saved, proj, p_s, m_s, w_s,
+):
+    w_s[...] = jnp.zeros((8, 128), F32)
+    w_s[:, 0 : table.shape[1]] = table[...]
+    scaled = wp[...] * gain[...]
+    scaled = scaled - jnp.mean(scaled, -1, keepdims=True)
+    proj[...] = scaled
+    w_hi, w_mid, w_lo = split3(scaled)
     ones8 = jnp.full((8, 128), 1.0 / 128, F32)
     lhs = jnp.concatenate([w_hi, w_mid, w_lo, ones8], axis=0).astype(BF)
     ones8 = ones8.astype(BF)
     mean = jnp.full((128, 128), 1.0 / 128, F32).astype(BF)
-    b_lhs = jnp.concatenate(list(split3(table[...])) + [jnp.zeros((8, 128), F32)], axis=0).astype(BF)
+    b_lhs = jnp.concatenate(list(split3(w_s[...])) + [jnp.zeros((8, 128), F32)], axis=0).astype(BF)
     lane = iota((8, 128), 1)
     klass = iota((128, 1024), 0)
+    left = iota((1, 128), 1) < HALF
+
+    def own_columns(ref):
+        both = ref[pl.ds(col[0] // 2, 1), :]
+        return jnp.where(left == (col[0] % 2 == 0), both, pltpu.roll(both, 64, 1))
+
+    chain_j, position_j = own_columns(chains), own_columns(positions)
+    begin = row[0] * 256 + pl.program_id(0) * 64
     for g in range(4):
         x = jnp.concatenate(
             [pair[e * 32 + g * 8 + rho] for rho in range(8) for e in range(2)], axis=0
@@ -132,7 +141,14 @@
         saved[g, 0:8, :] = t
         saved[g, 8:16, :] = scale
         saved[g, 16:24, :] = z[24:32]
-        onehot = jnp.where(klass == bins[g], 1.0, 0.0).astype(BF)
+        bins = []
+        for rho in range(8):
+            i = begin + g * 8 + rho
+            offset = jnp.where(left, position[i], position[i + 32]) - position_j
+            near = jnp.clip(offset + RMAX, 0, 2 * RMAX)
+            same = jnp.where(left, chain[i], chain[i + 32]) == chain_j
+            bins.append(jnp.where(same, near, 2 * RMAX + 1))
+        onehot = jnp.where(klass == jnp.concatenate(bins, axis=1), 1.0, 0.0).astype(BF)
         zb = mm(b_lhs, onehot)
         logits = t + (zb[0:8] + zb[8:16] + zb[16:24])
         for rho in range(8):
@@ -160,7 +176,19 @@
             out[h, d, 0, 96:112, :] = packed
 
 
-def merge_products(block, ub, vw, p_out, stats, c0, c1, c2, c3, m_s, c_s):
+def rows_at(d, block):
+    return pl.ds(pl.multiple_of(d * 256 + block * 64, 64), 64)
+
+
+def gather_updates(block, mine, first, second_a, second_b, third, out):
+    for r in range(8):
+        second = second_a.at[r] if r < 4 else second_b.at[r - 4]
+        for d in range(2):
+            for k, x in enumerate((mine.at[r], first.at[r], second, third.at[r])):
+                out[r, rows_at(d, block[0] ^ k), :] = x[d]
+
+
+def merge_products(block, ub, vw, p_out, stats, own, first, third, m_s, c_s):
     lane = iota((128, 128), 1)
     quarter = lane // 32
     left = lane < HALF
@@ -200,40 +228,49 @@
             c_s[r + k] = part.astype(BF)
     score = jnp.sum(acc, axis=1, keepdims=True)
     column = iota((512, 128), 1)
-    mixed = jnp.where(
-        column == 0,
-        m_s[...].reshape(512, 128),
-        jnp.where(column == 1, total, jnp.where(column == 2, score, 0.0)),
-    )
-    stats[...] = jnp.transpose(mixed)[0:8]
-    for k, out in enumerate((c0, c1, c2, c3)):
-        for d in range(2):
-            start = pl.multiple_of(d * 256 + (block[0] ^ k) * 64, 64)
-            for r in range(8):
-                out[r, d] = c_s[r, pl.ds(start, 64), :]
-
-
-def score_products(ub, vw, out):
+    mixed = m_s[...].reshape(512, 128)
+    for at, value in enumerate(split3(total)[:2] + split3(jnp.broadcast_to(score, (512, 128)))):
+        mixed = jnp.where(column == at + 1, value, mixed)
+    rows = jnp.transpose(mixed)[0:8]
+    rows = jnp.concatenate([rows[:, q * 128 : (q + 1) * 128] for q in range(4)], axis=0).astype(BF)
+    stats[...] = rows
+    first[1024:1056, :] = rows
+    third[1024:1056, :] = rows
+    for d in range(2):
+        for r in range(8):
+            zero, one, two, three = [c_s[r, rows_at(d, block[0] ^ k), :] for k in range(4)]
+            own[0, r, d] = zero
+            at = ((r % 4) * 2 + d) * 64
+            out, direct, passed = (first, one, two) if r < 4 else (third, three, two)
+            own[1, r, d] = three if r < 4 else one
+            out[at : at + 64, :] = direct
+            out[512 + at : 576 + at, :] = passed
+
+
+def score_products(msa, ub, vw, out, normed_out, scale_out):
     acc = jnp.zeros((512, 512), F32)
     for r in range(0, 8, 2):
         u = jnp.concatenate([ub[r + k].reshape(512, 128) for k in range(2)], axis=1)
         v = jnp.concatenate([vw[r + k, :, 0:64, :].reshape(512, 128) for k in range(2)], axis=1)
         acc += mm_nt(u, v)
     out[...] = acc
+    normed_out[...], scale_out[...] = standardize(paired(lambda s: msa[s]), averager())
 
 
 def streamed(stats):
-    rows = [x[...] for x in stats]
+    rows = []
+    for ref in stats:
+        x = ref[-32:, :].astype(F32)
+        rows.append(jnp.concatenate([x[q * 8 : q * 8 + 8] for q in range(4)], axis=1))
     peak = functools.reduce(jnp.maximum, [x[0:1] for x in rows])
     factor = [jnp.exp(x[0:1] - peak) for x in rows]
-    total = sum(f * x[1:2] for f, x in zip(factor, rows))
-    return [f / total for f in factor], rows
-
-
-def gradients(own, first, second, third, p_in, ub, scores, *rest):
-    out = rest[-1]
+    total = sum(f * (x[1:2] + x[2:3]) for f, x in zip(factor, rows))
+    return [f / total for f in factor], [x[3:4] + x[4:5] + x[5:6] for x in rows]
+
+
+def gradients(own, first, second, third, p_in, ub, scores, out):
     share, rows = streamed((own, first, second, third))
-    row_total = sum(f * x[2:3] for f, x in zip(share, rows))
+    row_total = sum(f * x for f, x in zip(share, rows))
     which = iota((8, 512), 0)
     columns = jnp.transpose(jnp.where(which == 0, share[0], jnp.where(which == 1, row_total, 0.0)))
     p = (p_in[...].reshape(512, 512).astype(F32) * columns[:, 0:1]).astype(BF)
@@ -254,18 +291,41 @@
             out[r + k, :, 0:64, :] = grad_v[:, k * 128 : (k + 1) * 128].reshape(8, 64, 128)
 
 
-def context_sum(block, own, first, second, third, c0, c1, c2, c3, out, f_s):
-    share, _ = streamed((own, first, second, third))
+def share_columns(stats, f_s):
+    share, _ = streamed(stats)
     which = iota((8, 512), 0)
     mixed = jnp.zeros((8, 512), F32)
     for k in range(4):
         mixed = jnp.where(which == k, share[k], mixed)
     f_s[...] = jnp.transpose(mixed)
+
+
+def context_on_the_way(block, s0, s2, c, first, third, to_third, to_first, f_s):
+    share_columns((s0, first, s2, third), f_s)
     for d in range(2):
-        f = f_s[pl.ds(pl.multiple_of(d * 256 + block[0] * 64, 64), 64), :]
+        f_3, f_1 = f_s[rows_at(d, block[0] ^ 3), :], f_s[rows_at(d, block[0] ^ 1), :]
+        for r in range(4):
+            at = (r * 2 + d) * 64
+            to_third[r, d] = (
+                c[1, r, d].astype(F32) * f_3[:, 0:1] + first[512 + at : 576 + at, :].astype(F32) * f_3[:, 1:2]
+            ).astype(BF)
+            to_first[r, d] = (
+                c[1, r + 4, d].astype(F32) * f_1[:, 0:1] + third[512 + at : 576 + at, :].astype(F32) * f_1[:, 3:4]
+            ).astype(BF)
+
+
+def context_sum(block, s0, s2, c, first, third, from_third, from_first, out, f_s):
+    share_columns((s0, first, s2, third), f_s)
+    for d in range(2):
+        f = f_s[rows_at(d, block[0]), :]
         for r in range(8):
-            parts = [c[r, d].astype(F32) * f[:, k : k + 1] for k, c in enumerate((c0, c1, c2, c3))]
-            out[r, d] = ((parts[0] + parts[1]) + (parts[2] + parts[3])).astype(BF)
+            rows = slice(((r % 4) * 2 + d) * 64, ((r % 4) * 2 + d + 1) * 64)
+            near, at, far = (
+                (first[rows, :], 1, from_third[r, d]) if r < 4 else (third[rows, :], 3, from_first[r - 4, d])
+            )
+            out[r, d] = (
+                c[0, r, d].astype(F32) * f[:, 0:1] + near.astype(F32) * f[:, at : at + 1] + far.astype(F32)
+            ).astype(BF)
 
 
 def pair_backward(pair, grads, saved, proj, out, g_s):
@@ -299,11 +359,8 @@
                 out[i] = (base[rows] - steep[rows] * pair[i].astype(F32)).astype(BF)
 
 
-def msa_partial(msa, wc, gb, normed_out, scale_out, grad_out, bdc):
+def msa_partial(wc, gb, grad_out, bdc):
     spread(wc[...], False, bdc)
-    normed, scale = standardize(paired(lambda s: msa[s]), averager())
-    normed_out[...] = normed
-    scale_out[...] = scale
     for d in range(2):
         value_grad = []
         for h in range(8):
@@ -348,109 +405,136 @@
 def shards(msa, pair, adj, flags, chains, positions, msa_gain, pair_gain, wc, ws, wf, wp, table):
     vm = pl.BlockSpec()
     sm = pl.BlockSpec(memory_space=pltpu.SMEM)
-    gp, gq = ("row", "d", "a"), ("row", "d", "b")
+    gp, rd = ("row", "d", "a"), ("row", "d")
     gain = msa_gain.reshape(1, 64)
-
-    u_send, tail = pl.pallas_call(
-        msa_updates,
-        out_shape=(shape((8, 2, 4, 64, 128), BF), shape((8, 2, 64, 128), F32)),
+    block = lax.axis_index("b").reshape(1)
+    piece = shape((8, 2, 64, 128), BF)
+
+    u_send, values, tail = pl.pallas_call(
+        msa_forward,
+        out_shape=(piece, piece, shape((8, 2, 64, 128), F32)),
+        in_specs=[sm] + [vm] * 6,
+        out_specs=(vm, vm, vm),
+        scratch_shapes=[pltpu.VMEM((1024, 1024), BF)] * 3,
+        compiler_params=WHOLE,
+        name="msa_forward",
+    )(flags, msa, adj, gain, wc, ws, wf)
+    mine = exchange(u_send.reshape(16, 64, 128), rd).reshape(8, 2, 64, 128)
+    first, third = swap(mine, 1), swap(mine, 3)
+    second = swap(first[:4], 3), swap(third[4:], 1)
+    ub = pl.pallas_call(
+        gather_updates,
+        out_shape=shape((8, 512, 128), BF),
         in_specs=[sm] + [vm] * 5,
-        out_specs=(vm, vm),
-        scratch_shapes=[pltpu.VMEM((1024, 1024), BF)] * 2,
-        compiler_params=WHOLE,
-        name="msa_updates",
-    )(flags, msa, adj, gain, ws, wf)
-    values = pl.pallas_call(
-        msa_values,
-        out_shape=shape((8, 2, 64, 128), BF),
-        in_specs=[vm] * 3,
         out_specs=vm,
-        scratch_shapes=[pltpu.VMEM((1024, 1024), BF)],
-        compiler_params=WHOLE,
-        name="msa_values",
-    )(msa, gain, wc)
-    ub = exchange(u_send.reshape(64, 64, 128), gq).reshape(8, 8, 64, 128)
-
-    row = lax.axis_index("row")
+        compiler_params=VMEM,
+        name="gather_updates",
+    )(block, mine, first, *second, third)
+
     col = lax.axis_index("d") * 16 + lax.axis_index("b") * 4 + lax.axis_index("a")
-
-    def rows_of(x):
-        return lax.dynamic_slice_in_dim(x, row * 256, 256).reshape(4, 2, 4, 8).transpose(0, 2, 3, 1)
-
-    def cols_of(x):
-        return lax.dynamic_slice_in_dim(x, col * 64, 64)
-
-    offset = jnp.clip(rows_of(positions)[..., None] - cols_of(positions) + RMAX, 0, 2 * RMAX)
-    bins = jnp.where(rows_of(chains)[..., None] == cols_of(chains), offset, 2 * RMAX + 1)
-    bins = bins.reshape(16, 1, 1024)
-    scaled = (wp * pair_gain[:, None]).T
-    proj = scaled - jnp.mean(scaled, -1, keepdims=True)
-    table_t = jnp.pad(table.T, ((0, 0), (0, 128 - table.shape[0])))
-
     def const(*dims):
         return pl.BlockSpec(dims, lambda k: (0,) * len(dims))
 
-    vw_send, saved = pl.pallas_call(
+    anywhere = pl.BlockSpec(memory_space=pl.ANY)
+    vw_send, saved, proj = pl.pallas_call(
         pair_forward,
         grid=(4,),
-        out_shape=(shape((8, 2, 4, 112, 128), BF), shape((16, 24, 1024), F32)),
+        out_shape=(shape((8, 2, 4, 112, 128), BF), shape((16, 24, 1024), F32), shape((8, 128), F32)),
         in_specs=[
+            sm,
+            sm,
+            sm,
+            sm,
+            const(16, 128),
+            const(16, 128),
             pl.BlockSpec((64, 64, 128), lambda k: (k, 0, 0)),
-            pl.BlockSpec((4, 1, 1024), lambda k: (k, 0, 0)),
+            const(1, 128),
             const(8, 128),
-            const(8, 128),
+            const(8, table.shape[0]),
             const(8, 2, 64, 128),
+            anywhere,
         ],
         out_specs=(
             pl.BlockSpec((8, 2, 1, 112, 128), lambda k: (0, 0, k, 0, 0)),
             pl.BlockSpec((4, 24, 1024), lambda k: (k, 0, 0)),
+            const(8, 128),
         ),
-        scratch_shapes=[pltpu.VMEM((8, 32, 128), F32)] * 2,
-        compiler_params=VMEM,
+        scratch_shapes=[pltpu.VMEM((8, 32, 128), F32)] * 2 + [pltpu.VMEM((8, 128), F32)],
+        compiler_params=WHOLE,
         name="pair_forward",
-    )(pair, bins, proj, table_t, values)
+    )(
+        lax.axis_index("row").reshape(1),
+        col.reshape(1),
+        chains,
+        positions,
+        chains.reshape(16, 128),
+        positions.reshape(16, 128),
+        pair,
+        pair_gain.reshape(1, 128),
+        wp.T,
+        table.T,
+        values,
+        mine,
+    )
+    vw_send = pl.pallas_call(
+        lambda *refs: None,
+        out_shape=shape((8, 2, 4, 112, 128), BF),
+        in_specs=[anywhere] * 3,
+        out_specs=anywhere,
+        input_output_aliases={0: 0},
+        compiler_params=WHOLE,
+        name="in_order",
+    )(vw_send, first, third)
     vw = exchange(vw_send.reshape(64, 112, 128), gp).reshape(8, 8, 112, 128)
 
-    block = lax.axis_index("b").reshape(1)
-    piece = shape((8, 2, 64, 128), BF)
-    p_raw, stats, *pieces = pl.pallas_call(
+    halves = shape((1056, 128), BF)
+    p_raw, stats, own, first, third = pl.pallas_call(
         merge_products,
-        out_shape=(shape((8, 2, 2, 16, 512), BF), shape((8, 512), F32)) + (piece,) * 4,
+        out_shape=(shape((8, 2, 2, 16, 512), BF), shape((32, 128), BF), shape((2, 8, 2, 64, 128), BF), halves, halves),
         in_specs=[sm, vm, vm],
-        out_specs=(vm,) * 6,
+        out_specs=(vm,) * 5,
         scratch_shapes=[pltpu.VMEM((8, 2, 2, 16, 128), F32), pltpu.VMEM((8, 512, 128), BF)],
         compiler_params=VMEM,
         name="merge_products",
     )(block, ub, vw)
-    shares = [stats] + [swap(stats, k) for k in (1, 2, 3)]
-    pieces = pieces[:1] + [swap(pieces[k], k) for k in (1, 2, 3)]
-    scores = pl.pallas_call(
+    far, first, third = swap(stats, 2), swap(first, 1), swap(third, 3)
+    scores, normed, scale = pl.pallas_call(
         score_products,
-        out_shape=shape((512, 512), F32),
-        in_specs=[vm, vm],
-        out_specs=vm,
+        out_shape=(shape((512, 512), F32), shape((1024, 128), F32), shape((1024, 128), F32)),
+        in_specs=[vm] * 3,
+        out_specs=(vm,) * 3,
         compiler_params=VMEM,
         name="score_products",
-    )(ub, vw)
+    )(msa, ub, vw)
     gd_send = pl.pallas_call(
         gradients,
         out_shape=shape((8, 8, 96, 128), BF),
-        in_specs=[vm] * 7 + [pl.BlockSpec(memory_space=pl.ANY)] * 2,
+        in_specs=[vm] * 7,
         out_specs=vm,
         compiler_params=VMEM,
         name="gradients",
-    )(*shares, p_raw, ub, scores, pieces[1], pieces[3])
+    )(stats, first, far, third, p_raw, ub, scores)
     gd = exchange(gd_send.reshape(64, 96, 128), gp).reshape(8, 2, 4, 96, 128)
+    half = shape((4, 2, 64, 128), BF)
+    to_third, to_first = pl.pallas_call(
+        context_on_the_way,
+        out_shape=(half, half),
+        in_specs=[sm] + [vm] * 5,
+        out_specs=(vm, vm),
+        scratch_shapes=[pltpu.VMEM((512, 8), F32)],
+        compiler_params=WHOLE,
+        name="context_on_the_way",
+    )(block, stats, far, own, first, third)
     context_send = pl.pallas_call(
         context_sum,
         out_shape=piece,
-        in_specs=[sm] + [vm] * 8,
+        in_specs=[sm] + [vm] * 7,
         out_specs=vm,
         scratch_shapes=[pltpu.VMEM((512, 8), F32)],
-        compiler_params=VMEM,
+        compiler_params=WHOLE,
         name="context_sum",
-    )(block, *shares, *pieces)
-    context = exchange(context_send.reshape(16, 64, 128), ("row", "d")).reshape(8, 2, 64, 128)
+    )(block, stats, far, own, first, third, swap(to_third, 3), swap(to_first, 1))
+    context = exchange(context_send.reshape(16, 64, 128), rd).reshape(8, 2, 64, 128)
     pair_gradient = pl.pallas_call(
         pair_backward,
         grid=(4,),
@@ -468,22 +552,22 @@
     )(pair, gd, saved, proj)
     partial = pl.pallas_call(
         msa_partial,
-        out_shape=(shape((1024, 128), F32), shape((1024, 128), F32), shape((2, 64, 1024), F32)),
-        in_specs=[vm] * 3,
-        out_specs=(vm, vm, vm),
+        out_shape=shape((2, 64, 1024), F32),
+        in_specs=[vm] * 2,
+        out_specs=vm,
         scratch_shapes=[pltpu.VMEM((1024, 1024), BF)],
         compiler_params=VMEM,
         name="msa_partial",
-    )(msa, wc, gd)
+    )(wc, gd)
     alignment_gradient = pl.pallas_call(
         msa_backward,
         out_shape=shape((32, 64, 64), BF),
         in_specs=[vm] * 7,
         out_specs=vm,
         scratch_shapes=[pltpu.VMEM((1024, 1024), BF)],
-        compiler_params=VMEM,
+        compiler_params=WHOLE,
         name="msa_backward",
-    )(gain, ws, context, tail, *partial)
+    )(gain, ws, context, tail, normed, scale, partial)
     return (alignment_gradient, pair_gradient)
 
 

time: 161 us -> 157 us (0.975)
  blocking collectives: 30.1 us -> 15.7 us
  waiting for transfers between devices: 45.9 us -> 52.7 us
  Pallas kernels: 35.5 us -> 39.3 us
  local copies, waits for them, and re-layouts: 8.4 us -> 6.31 us
  starting transfers between devices: 38 us -> 40 us
    ppermute x6 -> x9, waiting for transfers between devices: 36.1 us -> 52.7 us  [swap(): return lax.ppermute(x, 'b', [(i, i ^ k) for i in range(4)])]
    all_to_all x1, blocking collectives: 30.1 us -> 15.7 us  [exchange(): return lax.all_to_all(x, axes, 0, 0, tiled=True)]
    all_to_all x3, waiting for transfers between devices: 9.8 us -> 0.05 us  [exchange(): return lax.all_to_all(x, axes, 0, 0, tiled=True)]
    ppermute x6 -> x9, starting transfers between devices: 11.3 us -> 18.9 us  [swap(): return lax.ppermute(x, 'b', [(i, i ^ k) for i in range(4)])]
    all_to_all x3, starting transfers between devices: 26.7 us -> 21.1 us  [exchange(): return lax.all_to_all(x, axes, 0, 0, tiled=True)]
    dynamic_slice x4 -> x0, local copies, waits for them, and re-layouts: 3.04 us -> none  [the longest x2 1.52 us: cols_of(): return lax.dynamic_slice_in_dim(x, col * 64, 64)]
    unnamed x26 -> x44, local copies, waits for them, and re-layouts: 3.98 us -> 6.29 us
    pallas_call x1, Pallas kernels: 2.71 us -> 4.33 us  [shards(): pl.pallas_call(msa_backward, out_shape=shape((32, 64, 64), BF), in_specs=...]
  transfers between devices with their start and end apart: 9 -> 12, of which waited for: 4 -> 5; matrix products, arithmetic and copies ran while one was open for 3% -> 0% of each run, Pallas kernels for 15% -> 17%
where the time goes in v3:
time: 157 us; the launch traced here: 155 us
  waiting for transfers between devices  52.7 us (34%)
  starting transfers between devices  40 us (25%)
  Pallas kernels  39.3 us (25%)
  blocking collectives  15.7 us (10%)
  local copies, waits for them, and re-layouts  6.31 us (4%)
    ppermute x9, waiting for transfers between devices, swap(): return lax.ppermute(x, 'b', [(i, i ^ k) for i in range(4)])  52.7 us
    all_to_all x3, starting transfers between devices, exchange(): return lax.all_to_all(x, axes, 0, 0, tiled=True)  21.1 us
    ppermute x9, starting transfers between devices, swap(): return lax.ppermute(x, 'b', [(i, i ^ k) for i in range(4)])  18.9 us
    all_to_all x1, blocking collectives, exchange(): return lax.all_to_all(x, axes, 0, 0, tiled=True)  15.7 us
    pallas_call x1, Pallas kernels, shards(): pl.pallas_call(pair_forward, grid=(4,), out_shape=(shape((8, 2, 4, 112, 1...  12.3 us
    pallas_call x1, Pallas kernels, shards(): pl.pallas_call(pair_backward, grid=(4,), out_shape=shape((256, 64, 128),...  6.32 us
    unnamed x44, local copies, waits for them, and re-layouts  6.29 us
    pallas_call x1, Pallas kernels, shards(): pl.pallas_call(msa_forward, out_shape=(piece, piece, shape((8, 2, 64, 128...  5.07 us
  transfers between devices with their start and end apart: 12, of which 5 were waited for; matrix products, arithmetic and copies ran while one was open for 0% of the time, Pallas kernels for 17%

profile of v3, /device:TPU:32, one launch (start us, length us, event | category | flops | bytes accessed | tf_op | source)
XLA Modules:
  0.0 154.9 jit_solution(6286630209399925936)
XLA Ops:
  0.6 5.1 %msa_forward.1 = (bf16[8,2,64,128]{3,2,1,0:T(8,128)(2,1)}, bf16[8,2,64,128]{3,2,1,0:T(8,128)(2,1)}, f32[8,2,64,128]{3,2,1,0:T(8,128)}) custom-call(s32[32]{0:T(128)} %flags.1, bf16[32,64,64]{2,1,0:T(8,128)(2,1)} %msa.3, bf16[32,64,64]{2,1,0:T(8,128)(2,1)} %adj.1, f32[1,64]{1,0:T(1,128)} %bitcast.33, bf16[64,64]{1,0:T(8,128)(2,1)} %wc.3, bf16[64,64]{1,0:T(8,128)(2,1)} %ws.3, ...), custom_call_target="tpu_custom_call" | custom-call | tf_op jit(solution)/shard_map/msa_forward/pallas_call | solution.py:413
  5.7 15.7 %all_to_all.20 = bf16[16,64,128]{2,1,0:T(8,128)(2,1)S(1)} all-to-all(bf16[16,64,128]{2,1,0:T(8,128)(2,1)} %bitcast.28), channel_id=1, replica_groups=mesh['row'=8,'d'=2,'b'=4,'a'=4] {'row','d'}, dimensions={0} | all-to-all | bytes 524288 | tf_op jit(solution)/shard_map/all_to_all | solution.py:394
  21.4 3.3 %collective-permute-start = (bf16[8,2,64,128]{3,2,1,0:T(8,128)(2,1)S(1)}, bf16[8,2,64,128]{3,2,1,0:T(8,128)(2,1)S(1)}, u32[]{:S(2)}, u32[]{:S(2)}) collective-permute-start(bf16[8,2,64,128]{3,2,1,0:T(8,128)(2,1)S(1)} %bitcast.21), channel_id=1, source_target_pairs={{0,4},{4,0},{8,12},{12,8},{1,5},{5,1},{9,13},{13,9},{2,6},{6,2},{1... | collective-permute-start | bytes 786440 | tf_op jit(solution)/shard_map/ppermute | solution.py:398
  24.7 3.6 %collective-permute-start.2 = (bf16[8,2,64,128]{3,2,1,0:T(8,128)(2,1)S(1)}, bf16[8,2,64,128]{3,2,1,0:T(8,128)(2,1)S(1)}, u32[]{:S(2)}, u32[]{:S(2)}) collective-permute-start(bf16[8,2,64,128]{3,2,1,0:T(8,128)(2,1)S(1)} %bitcast.22), channel_id=1, source_target_pairs={{0,12},{4,8},{8,4},{12,0},{1,13},{5,9},{9,5},{13,1},{2,14},{6,10},... | collective-permute-start | bytes 786440 | tf_op jit(solution)/shard_map/ppermute | solution.py:398
  28.3 0.0 copy-done.2
  28.3 12.3 %pair_forward.1 = (bf16[8,2,4,112,128]{4,3,2,1,0:T(8,128)(2,1)}, f32[16,24,1024]{2,1,0:T(8,128)}, f32[8,128]{1,0:T(8,128)}) custom-call(s32[1]{0:T(128)} %bitcast.4.row, s32[1]{0:T(128)} %bitcast.5.col, s32[2048]{0:T(1024)} %chain.1, s32[2048]{0:T(1024)} %position.1, s32[16,128]{1,0:T(8,128)} %bitcast.29, s32[16,128]{1,0:T(8,128)} %bitcast.30, ...), custom_call_target="tpu_custom_call" | custom-call | tf_op jit(solution)/shard_map/pair_forward/pallas_call | solution.py:439
  40.6 0.0 collective-permute-done.first.refs_1_
  40.6 0.0 collective-permute-done.2.third.refs_2_
  40.7 0.7 copy-done.7
  41.3 0.1 copy-done.9
  41.4 5.3 %all-to-all-start.1 = ((bf16[64,112,128]{2,1,0:T(8,128)(2,1)}), bf16[64,112,128]{2,1,0:T(8,128)(2,1)S(1)}, u32[]{:S(2)}, u32[]{:S(2)}) async-start(bf16[64,112,128]{2,1,0:T(8,128)(2,1)} %bitcast.25), calls=%async_computation.1 | async-start | bytes 3670016 | tf_op jit(solution)/shard_map/all_to_all | solution.py:394
  46.7 1.7 %collective-permute-start.1 = (bf16[4,2,64,128]{3,2,1,0:T(8,128)(2,1)S(1)}, bf16[4,2,64,128]{3,2,1,0:T(8,128)(2,1)S(1)}, u32[]{:S(2)}, u32[]{:S(2)}) collective-permute-start(bf16[4,2,64,128]{3,2,1,0:T(8,128)(2,1)S(1)} %slice.8), channel_id=1, source_target_pairs={{0,12},{4,8},{8,4},{12,0},{1,13},{5,9},{9,5},{13,1},{2,14},{6,10},... | collective-permute-start | bytes 393224 | tf_op jit(solution)/shard_map/ppermute | solution.py:398
  48.5 1.5 collective-permute-start.3
  49.9 22.4 %collective-permute-done.1.second_a = bf16[4,2,64,128]{3,2,1,0:T(8,128)(2,1)S(1)} collective-permute-done((bf16[4,2,64,128]{3,2,1,0:T(8,128)(2,1)S(1)}, bf16[4,2,64,128]{3,2,1,0:T(8,128)(2,1)S(1)}, u32[]{:S(2)}, u32[]{:S(2)}) %collective-permute-start.1) | collective-permute-done | bytes 131104 | tf_op jit(solution)/shard_map/ppermute | solution.py:398
  72.4 1.9 %collective-permute-done.3.second_b = bf16[4,2,64,128]{3,2,1,0:T(8,128)(2,1)S(1)} collective-permute-done((bf16[4,2,64,128]{3,2,1,0:T(8,128)(2,1)S(1)}, bf16[4,2,64,128]{3,2,1,0:T(8,128)(2,1)S(1)}, u32[]{:S(2)}, u32[]{:S(2)}) %collective-permute-start.3) | collective-permute-done | bytes 131104 | tf_op jit(solution)/shard_map/ppermute | solution.py:398
  74.3 0.9 copy-done.11
  75.3 0.1 gather_updates.1.ub
  75.3 0.0 all-to-all-done.1
  75.4 0.0 copy-start.4
  75.4 1.6 %merge_products.1 = (bf16[8,2,2,16,512]{4,3,2,1,0:T(8,128)(2,1)S(1)}, bf16[32,128]{1,0:T(8,128)(2,1)S(1)}, bf16[2,8,2,64,128]{4,3,2,1,0:T(8,128)(2,1)S(1)}, bf16...) custom-call(s32[1]{0:T(128)} %bitcast.1.block, bf16[8,512,128]{2,1,0:T(8,128)(2,1)S(1)} %gather_updates.1.ub, ...), custom_call_target="tpu_custom_call" | custom-call | tf_op jit(solution)/shard_map/merge_products/pallas_call | solution.py:491
  76.9 0.8 copy-done.5
  77.7 1.5 collective-permute-start.5
  79.3 1.5 collective-permute-start.6
  80.8 3.4 %collective-permute-start.4 = (bf16[32,128]{1,0:T(8,128)(2,1)S(1)}, bf16[32,128]{1,0:T(8,128)(2,1)S(1)}, u32[]{:S(2)}, u32[]{:S(2)}) collective-permute-start(bf16[32,128]{1,0:T(8,128)(2,1)S(1)} %get-tuple-element.21.s0.own), channel_id=1, source_target_pairs={{0,8},{4,12},{8,0},{12,4},{1,9},{5,13},{9,1},{13,5},{2,10},{6,14},... | collective-permute-start | bytes 24584 | tf_op jit(solution)/shard_map/ppermute | solution.py:398
  84.2 1.2 score_products.1
  85.5 0.8 copy-done.13
  86.2 0.8 copy-done.14
  87.0 9.1 %collective-permute-done.4.s2.second = bf16[32,128]{1,0:T(8,128)(2,1)S(1)} collective-permute-done((bf16[32,128]{1,0:T(8,128)(2,1)S(1)}, bf16[32,128]{1,0:T(8,128)(2,1)S(1)}, u32[]{:S(2)}, u32[]{:S(2)}) %collective-permute-start.4) | collective-permute-done | bytes 8224 | tf_op jit(solution)/shard_map/ppermute | solution.py:398
  96.1 0.0 collective-permute-done.5.first
  96.1 0.0 collective-permute-done.6.third
  96.1 2.2 %gradients.1 = bf16[8,8,96,128]{3,2,1,0:T(8,128)(2,1)} custom-call(bf16[32,128]{1,0:T(8,128)(2,1)S(1)} %get-tuple-element.21.s0.own, bf16[1056,128]{1,0:T(8,128)(2,1)S(1)} %collective-permute-done.5.first, bf16[32,128]{1,0:T(8,128)(2,1)S(1)} %collective-permute-done.4.s2.second, bf16[1056,128]{1,0:T(8,128)(2,1)S(1)} %collective-permute-done.6.third, ...), custom_call_target="tpu_custom_call" | custom-call | tf_op jit(solution)/shard_map/gradients/pallas_call | solution.py:509
  98.4 8.9 %all-to-all-start.3 = ((bf16[64,96,128]{2,1,0:T(8,128)(2,1)}), bf16[64,96,128]{2,1,0:T(8,128)(2,1)S(1)}, u32[]{:S(2)}, u32[]{:S(2)}) async-start(bf16[64,96,128]{2,1,0:T(8,128)(2,1)} %bitcast.15), calls=%async_computation.3 | async-start | bytes 3145728 | tf_op jit(solution)/shard_map/all_to_all | solution.py:394
  107.2 0.0 copy-start.17
  107.2 2.3 %context_on_the_way.1 = (bf16[4,2,64,128]{3,2,1,0:T(8,128)(2,1)}, bf16[4,2,64,128]{3,2,1,0:T(8,128)(2,1)}) custom-call(s32[1]{0:T(128)} %bitcast.1.block, bf16[32,128]{1,0:T(8,128)(2,1)} %copy-done.15, bf16[32,128]{1,0:T(8,128)(2,1)} %copy-done.16, bf16[2,8,2,64,128]{4,3,2,1,0:T(8,128)(2,1)} %copy-done.5, bf16[1056,128]{1,0:T(8,128)(2,1)} %copy-done, ...), custom_call_target="tpu_custom_call" | custom-call | tf_op jit(solution)/shard_map/context_on_the_way/pallas_call | solution.py:519
  109.5 0.7 collective-permute-start.7
  110.3 1.7 %collective-permute-start.8 = (bf16[4,2,64,128]{3,2,1,0:T(8,128)(2,1)}, bf16[4,2,64,128]{3,2,1,0:T(8,128)(2,1)S(1)}, u32[]{:S(2)}, u32[]{:S(2)}) collective-permute-start(bf16[4,2,64,128]{3,2,1,0:T(8,128)(2,1)} %get-tuple-element.26), channel_id=1, source_target_pairs={{0,4},{4,0},{8,12},{12,8},{1,5},{5,1},{9,13},{13,9},{2,6},{6,2},{1... | collective-permute-start | bytes 393224 | tf_op jit(solution)/shard_map/ppermute | solution.py:398
  111.9 18.3 %collective-permute-done.7.from_third = bf16[4,2,64,128]{3,2,1,0:T(8,128)(2,1)S(1)} collective-permute-done((bf16[4,2,64,128]{3,2,1,0:T(8,128)(2,1)}, bf16[4,2,64,128]{3,2,1,0:T(8,128)(2,1)S(1)}, u32[]{:S(2)}, u32[]{:S(2)}) %collective-permute-start.7) | collective-permute-done | bytes 131104 | tf_op jit(solution)/shard_map/ppermute | solution.py:398
  130.2 1.0 collective-permute-done.8.from_first
  131.2 0.6 copy-done.21
  131.8 2.4 %context_sum.1 = bf16[8,2,64,128]{3,2,1,0:T(8,128)(2,1)} custom-call(s32[1]{0:T(128)} %bitcast.1.block, bf16[32,128]{1,0:T(8,128)(2,1)} %copy-done.15, bf16[32,128]{1,0:T(8,128)(2,1)} %copy-done.16, bf16[2,8,2,64,128]{4,3,2,1,0:T(8,128)(2,1)} %copy-done.5, bf16[1056,128]{1,0:T(8,128)(2,1)} %copy-done, bf16[1056,128]{1,0:T(8,128)(2,1)} %copy-done.1, ...), custom_call_target="tpu_custom_call" | custom-call | tf_op jit(solution)/shard_map/context_sum/pallas_call | solution.py:528
  134.2 0.0 all-to-all-done.3
  134.2 6.9 %all-to-all-start.2 = ((bf16[16,64,128]{2,1,0:T(8,128)(2,1)}), bf16[16,64,128]{2,1,0:T(8,128)(2,1)S(1)}, u32[]{:S(2)}, u32[]{:S(2)}) async-start(bf16[16,64,128]{2,1,0:T(8,128)(2,1)} %bitcast.27), calls=%async_computation.2 | async-start | bytes 524288 | tf_op jit(solution)/shard_map/all_to_all | solution.py:394
  141.2 1.5 msa_partial.1.partial
  142.7 0.8 copy-done.6
  143.5 6.3 %pair_backward.1 = bf16[256,64,128]{2,1,0:T(8,128)(2,1)} custom-call(bf16[256,64,128]{2,1,0:T(8,128)(2,1)} %pair.3, bf16[8,2,4,96,128]{4,3,2,1,0:T(8,128)(2,1)S(1)} %bitcast.20, f32[16,24,1024]{2,1,0:T(8,128)S(1)} %copy-done.12, f32[8,128]{1,0:T(8,128)S(1)} %copy-done.18), custom_call_target="tpu_custom_call" | custom-call | tf_op jit(solution)/shard_map/pair_backward/pallas_call | solution.py:538
  149.8 0.0 all-to-all-done.2
  149.8 0.7 copy-done.19
  150.5 4.3 %msa_backward.1 = bf16[32,64,64]{2,1,0:T(8,128)(2,1)} custom-call(f32[1,64]{1,0:T(1,128)} %bitcast.34, bf16[64,64]{1,0:T(8,128)(2,1)} %ws.3, bf16[8,2,64,128]{3,2,1,0:T(8,128)(2,1)} %bitcast.26, f32[8,2,64,128]{3,2,1,0:T(8,128)} %get-tuple-element.27.tail, f32[1024,128]{1,0:T(8,128)} %copy-done.13, f32[1024,128]{1,0:T(8,128)} %copy-done.14, ...), custom_call_target="tpu_custom_call" | custom-call | tf_op jit(solution)/shard_map/msa_backward/pallas_call | solution.py:562
  (35 shorter events, 0.1 us)
Async XLA Ops:
  21.4 6.9 %copy-start.2 = (bf16[16,64,128]{2,1,0:T(8,128)(2,1)}, bf16[16,64,128]{2,1,0:T(8,128)(2,1)S(1)}, u32[]{:S(2)}) copy-start(bf16[16,64,128]{2,1,0:T(8,128)(2,1)S(1)} %all_to_all.20) | copy-start | bytes 786436
  21.4 19.2 %collective-permute-start = (bf16[8,2,64,128]{3,2,1,0:T(8,128)(2,1)S(1)}, bf16[8,2,64,128]{3,2,1,0:T(8,128)(2,1)S(1)}, u32[]{:S(2)}, u32[]{:S(2)}) collective-permute-start(bf16[8,2,64,128]{3,2,1,0:T(8,128)(2,1)S(1)} %bitcast.21), channel_id=1, source_target_pairs={{0,4},{4,0},{8,12},{12,8},{1,5},{5,1},{9,13},{13,9},{2,6},{6,2},{1... | collective-permute-start | bytes 786440 | tf_op jit(solution)/shard_map/ppermute | solution.py:398
  24.7 15.9 %collective-permute-start.2 = (bf16[8,2,64,128]{3,2,1,0:T(8,128)(2,1)S(1)}, bf16[8,2,64,128]{3,2,1,0:T(8,128)(2,1)S(1)}, u32[]{:S(2)}, u32[]{:S(2)}) collective-permute-start(bf16[8,2,64,128]{3,2,1,0:T(8,128)(2,1)S(1)} %bitcast.22), channel_id=1, source_target_pairs={{0,12},{4,8},{8,4},{12,0},{1,13},{5,9},{9,5},{13,1},{2,14},{6,10},... | collective-permute-start | bytes 786440 | tf_op jit(solution)/shard_map/ppermute | solution.py:398
  40.6 0.7 copy-start.7
  40.7 0.8 copy-start.9
  41.4 5.3 %copy-start.8 = (bf16[8,2,64,128]{3,2,1,0:T(8,128)(2,1)S(1)}, bf16[8,2,64,128]{3,2,1,0:T(8,128)(2,1)}, u32[]{:S(2)}) copy-start(bf16[8,2,64,128]{3,2,1,0:T(8,128)(2,1)} %copy-done.7) | copy-start | bytes 786436
  41.4 7.0 %copy-start.10 = (bf16[8,2,64,128]{3,2,1,0:T(8,128)(2,1)S(1)}, bf16[8,2,64,128]{3,2,1,0:T(8,128)(2,1)}, u32[]{:S(2)}) copy-start(bf16[8,2,64,128]{3,2,1,0:T(8,128)(2,1)} %copy-done.9) | copy-start | bytes 786436
  41.4 32.9 %copy-start.3 = (bf16[16,64,128]{2,1,0:T(8,128)(2,1)S(1)}, bf16[16,64,128]{2,1,0:T(8,128)(2,1)}, u32[]{:S(2)}) copy-start(bf16[16,64,128]{2,1,0:T(8,128)(2,1)} %copy-done.2) | copy-start | bytes 786436
  41.4 33.9 %all-to-all-start.1 = ((bf16[64,112,128]{2,1,0:T(8,128)(2,1)}), bf16[64,112,128]{2,1,0:T(8,128)(2,1)S(1)}, u32[]{:S(2)}, u32[]{:S(2)}) async-start(bf16[64,112,128]{2,1,0:T(8,128)(2,1)} %bitcast.25), calls=%async_computation.1 | async-start | bytes 3670016 | tf_op jit(solution)/shard_map/all_to_all | solution.py:394
  46.7 25.6 %collective-permute-start.1 = (bf16[4,2,64,128]{3,2,1,0:T(8,128)(2,1)S(1)}, bf16[4,2,64,128]{3,2,1,0:T(8,128)(2,1)S(1)}, u32[]{:S(2)}, u32[]{:S(2)}) collective-permute-start(bf16[4,2,64,128]{3,2,1,0:T(8,128)(2,1)S(1)} %slice.8), channel_id=1, source_target_pairs={{0,12},{4,8},{8,4},{12,0},{1,13},{5,9},{9,5},{13,1},{2,14},{6,10},... | collective-permute-start | bytes 393224 | tf_op jit(solution)/shard_map/ppermute | solution.py:398
  48.5 25.8 %collective-permute-start.3 = (bf16[4,2,64,128]{3,2,1,0:T(8,128)(2,1)S(1)}, bf16[4,2,64,128]{3,2,1,0:T(8,128)(2,1)S(1)}, u32[]{:S(2)}, u32[]{:S(2)}) collective-permute-start(bf16[4,2,64,128]{3,2,1,0:T(8,128)(2,1)S(1)} %slice.9), channel_id=1, source_target_pairs={{0,4},{4,0},{8,12},{12,8},{1,5},{5,1},{9,13},{13,9},{2,6},{6,2},{1... | collective-permute-start | bytes 393224 | tf_op jit(solution)/shard_map/ppermute | solution.py:398
  74.3 1.0 copy-start.11
  75.4 8.9 %copy-start.4 = (bf16[32,64,64]{2,1,0:T(8,128)(2,1)S(1)}, bf16[32,64,64]{2,1,0:T(8,128)(2,1)}, u32[]{:S(2)}) copy-start(bf16[32,64,64]{2,1,0:T(8,128)(2,1)} %msa.3) | copy-start | bytes 786436
  76.9 0.8 copy-start.5
  77.7 20.6 %copy-start.15 = (bf16[32,128]{1,0:T(8,128)(2,1)}, bf16[32,128]{1,0:T(8,128)(2,1)S(1)}, u32[]{:S(2)}) copy-start(bf16[32,128]{1,0:T(8,128)(2,1)S(1)} %get-tuple-element.21.s0.own) | copy-start | bytes 24580
  77.7 18.4 %collective-permute-start.5 = (bf16[1056,128]{1,0:T(8,128)(2,1)S(1)}, bf16[1056,128]{1,0:T(8,128)(2,1)S(1)}, u32[]{:S(2)}, u32[]{:S(2)}) collective-permute-start(bf16[1056,128]{1,0:T(8,128)(2,1)S(1)} %get-tuple-element.23), channel_id=1, source_target_pairs={{0,4},{4,0},{8,12},{12,8},{1,5},{5,1},{9,13},{13,9},{2,6},{6,2},{1... | collective-permute-start | bytes 811016 | tf_op jit(solution)/shard_map/ppermute | solution.py:398
  79.3 16.9 %collective-permute-start.6 = (bf16[1056,128]{1,0:T(8,128)(2,1)S(1)}, bf16[1056,128]{1,0:T(8,128)(2,1)S(1)}, u32[]{:S(2)}, u32[]{:S(2)}) collective-permute-start(bf16[1056,128]{1,0:T(8,128)(2,1)S(1)} %get-tuple-element.24), channel_id=1, source_target_pairs={{0,12},{4,8},{8,4},{12,0},{1,13},{5,9},{9,5},{13,1},{2,14},{6,10},... | collective-permute-start | bytes 811016 | tf_op jit(solution)/shard_map/ppermute | solution.py:398
  80.8 15.3 %collective-permute-start.4 = (bf16[32,128]{1,0:T(8,128)(2,1)S(1)}, bf16[32,128]{1,0:T(8,128)(2,1)S(1)}, u32[]{:S(2)}, u32[]{:S(2)}) collective-permute-start(bf16[32,128]{1,0:T(8,128)(2,1)S(1)} %get-tuple-element.21.s0.own), channel_id=1, source_target_pairs={{0,8},{4,12},{8,0},{12,4},{1,9},{5,13},{9,1},{13,5},{2,10},{6,14},... | collective-permute-start | bytes 24584 | tf_op jit(solution)/shard_map/ppermute | solution.py:398
  85.4 0.8 copy-start.13
  86.2 0.8 copy-start.14
  96.1 2.2 %copy-start.16 = (bf16[32,128]{1,0:T(8,128)(2,1)}, bf16[32,128]{1,0:T(8,128)(2,1)S(1)}, u32[]{:S(2)}) copy-start(bf16[32,128]{1,0:T(8,128)(2,1)S(1)} %collective-permute-done.4.s2.second) | copy-start | bytes 24580
  96.1 2.2 %copy-start = (bf16[1056,128]{1,0:T(8,128)(2,1)}, bf16[1056,128]{1,0:T(8,128)(2,1)S(1)}, u32[]{:S(2)}) copy-start(bf16[1056,128]{1,0:T(8,128)(2,1)S(1)} %collective-permute-done.5.first) | copy-start | bytes 811012
  96.1 2.2 %copy-start.1 = (bf16[1056,128]{1,0:T(8,128)(2,1)}, bf16[1056,128]{1,0:T(8,128)(2,1)S(1)}, u32[]{:S(2)}) copy-start(bf16[1056,128]{1,0:T(8,128)(2,1)S(1)} %collective-permute-done.6.third) | copy-start | bytes 811012
  98.4 35.9 %all-to-all-start.3 = ((bf16[64,96,128]{2,1,0:T(8,128)(2,1)}), bf16[64,96,128]{2,1,0:T(8,128)(2,1)S(1)}, u32[]{:S(2)}, u32[]{:S(2)}) async-start(bf16[64,96,128]{2,1,0:T(8,128)(2,1)} %bitcast.15), calls=%async_computation.3 | async-start | bytes 3145728 | tf_op jit(solution)/shard_map/all_to_all | solution.py:394
  107.2 33.9 %copy-start.17 = (bf16[64,64]{1,0:T(8,128)(2,1)S(1)}, bf16[64,64]{1,0:T(8,128)(2,1)}, u32[]{:S(2)}) copy-start(bf16[64,64]{1,0:T(8,128)(2,1)} %wc.3) | copy-start | bytes 24580
  109.5 20.7 %collective-permute-start.7 = (bf16[4,2,64,128]{3,2,1,0:T(8,128)(2,1)}, bf16[4,2,64,128]{3,2,1,0:T(8,128)(2,1)S(1)}, u32[]{:S(2)}, u32[]{:S(2)}) collective-permute-start(bf16[4,2,64,128]{3,2,1,0:T(8,128)(2,1)} %get-tuple-element.25), channel_id=1, source_target_pairs={{0,12},{4,8},{8,4},{12,0},{1,13},{5,9},{9,5},{13,1},{2,14},{6,10},... | collective-permute-start | bytes 393224 | tf_op jit(solution)/shard_map/ppermute | solution.py:398
  110.3 33.2 %copy-start.12 = (f32[16,24,1024]{2,1,0:T(8,128)S(1)}, f32[16,24,1024]{2,1,0:T(8,128)}, u32[]{:S(2)}) copy-start(f32[16,24,1024]{2,1,0:T(8,128)} %get-tuple-element.32.saved) | copy-start | bytes 4718596
  110.3 33.2 %copy-start.18 = (f32[8,128]{1,0:T(8,128)S(1)}, f32[8,128]{1,0:T(8,128)}, u32[]{:S(2)}) copy-start(f32[8,128]{1,0:T(8,128)} %get-tuple-element.33.proj) | copy-start | bytes 12292
  110.3 20.9 %collective-permute-start.8 = (bf16[4,2,64,128]{3,2,1,0:T(8,128)(2,1)}, bf16[4,2,64,128]{3,2,1,0:T(8,128)(2,1)S(1)}, u32[]{:S(2)}, u32[]{:S(2)}) collective-permute-start(bf16[4,2,64,128]{3,2,1,0:T(8,128)(2,1)} %get-tuple-element.26), channel_id=1, source_target_pairs={{0,4},{4,0},{8,12},{12,8},{1,5},{5,1},{9,13},{13,9},{2,6},{6,2},{1... | collective-permute-start | bytes 393224 | tf_op jit(solution)/shard_map/ppermute | solution.py:398
  130.2 1.0 copy-start.20
  131.2 0.6 copy-start.21
  134.2 15.6 %all-to-all-start.2 = ((bf16[16,64,128]{2,1,0:T(8,128)(2,1)}), bf16[16,64,128]{2,1,0:T(8,128)(2,1)S(1)}, u32[]{:S(2)}, u32[]{:S(2)}) async-start(bf16[16,64,128]{2,1,0:T(8,128)(2,1)} %bitcast.27), calls=%async_computation.2 | async-start | bytes 524288 | tf_op jit(solution)/shard_map/all_to_all | solution.py:394
  142.7 0.8 copy-start.6
  149.8 0.7 copy-start.19

commit v4 on v3

--- a/solution.py
+++ b/solution.py
@@ -300,32 +300,28 @@
     f_s[...] = jnp.transpose(mixed)
 
 
-def context_on_the_way(block, s0, s2, c, first, third, to_third, to_first, f_s):
+def context_on_the_way(block, s0, s2, c, first, third, to_third, to_first, base, f_s):
     share_columns((s0, first, s2, third), f_s)
     for d in range(2):
-        f_3, f_1 = f_s[rows_at(d, block[0] ^ 3), :], f_s[rows_at(d, block[0] ^ 1), :]
+        f_0, f_1, f_3 = [f_s[rows_at(d, block[0] ^ k), :] for k in (0, 1, 3)]
         for r in range(4):
             at = (r * 2 + d) * 64
+            near, far = slice(at, at + 64), slice(512 + at, 576 + at)
             to_third[r, d] = (
-                c[1, r, d].astype(F32) * f_3[:, 0:1] + first[512 + at : 576 + at, :].astype(F32) * f_3[:, 1:2]
+                c[1, r, d].astype(F32) * f_3[:, 0:1] + first[far, :].astype(F32) * f_3[:, 1:2]
             ).astype(BF)
             to_first[r, d] = (
-                c[1, r + 4, d].astype(F32) * f_1[:, 0:1] + third[512 + at : 576 + at, :].astype(F32) * f_1[:, 3:4]
+                c[1, r + 4, d].astype(F32) * f_1[:, 0:1] + third[far, :].astype(F32) * f_1[:, 3:4]
             ).astype(BF)
-
-
-def context_sum(block, s0, s2, c, first, third, from_third, from_first, out, f_s):
-    share_columns((s0, first, s2, third), f_s)
-    for d in range(2):
-        f = f_s[rows_at(d, block[0]), :]
-        for r in range(8):
-            rows = slice(((r % 4) * 2 + d) * 64, ((r % 4) * 2 + d + 1) * 64)
-            near, at, far = (
-                (first[rows, :], 1, from_third[r, d]) if r < 4 else (third[rows, :], 3, from_first[r - 4, d])
+            base[r, d] = c[0, r, d].astype(F32) * f_0[:, 0:1] + first[near, :].astype(F32) * f_0[:, 1:2]
+            base[r + 4, d] = (
+                c[0, r + 4, d].astype(F32) * f_0[:, 0:1] + third[near, :].astype(F32) * f_0[:, 3:4]
             )
-            out[r, d] = (
-                c[0, r, d].astype(F32) * f[:, 0:1] + near.astype(F32) * f[:, at : at + 1] + far.astype(F32)
-            ).astype(BF)
+
+
+def context_sum(base, from_third, from_first, out):
+    out[0:4] = (base[0:4] + from_third[...].astype(F32)).astype(BF)
+    out[4:8] = (base[4:8] + from_first[...].astype(F32)).astype(BF)
 
 
 def pair_backward(pair, grads, saved, proj, out, g_s):
@@ -359,24 +355,18 @@
                 out[i] = (base[rows] - steep[rows] * pair[i].astype(F32)).astype(BF)
 
 
-def msa_partial(wc, gb, grad_out, bdc):
+def msa_backward(gain, wc, ws, gb, context, tail, normed, scale, out, bdc, bds):
     spread(wc[...], False, bdc)
-    for d in range(2):
-        value_grad = []
-        for h in range(8):
-            total = gb[h, d, 0, 0:64, :].astype(F32)
-            for k in range(1, 4):
-                total += gb[h, d, k, 0:64, :].astype(F32)
-            value_grad.append(total.astype(BF))
-        grad_out[d] = mm_nt(jnp.concatenate(value_grad, axis=1), bdc[...])
-
-
-def msa_backward(gain, ws, context, tail, normed, scale, partial, out, bds):
     spread(ws[...], False, bds)
     grads = []
     for d in range(2):
-        gate_grad = [(tail[h, d] * context[h, d].astype(F32)).astype(BF) for h in range(8)]
-        grad = partial[d] + mm_nt(jnp.concatenate(gate_grad, axis=1), bds[...])
+        value_grad, gate_grad = [], []
+        for h in range(8):
+            parts = [gb[h, d, k].astype(F32) for k in range(4)]
+            value_grad.append(((parts[0] + parts[1]) + (parts[2] + parts[3])).astype(BF))
+            gate_grad.append((tail[h, d] * context[h, d].astype(F32)).astype(BF))
+        grad = mm_nt(jnp.concatenate(value_grad, axis=1), bdc[...])
+        grad += mm_nt(jnp.concatenate(gate_grad, axis=1), bds[...])
         grads += [grad[:, k * 128 : (k + 1) * 128] for k in range(8)]
     ones = averager()
     scaled = jnp.concatenate(grads, axis=0) * twice(gain)
@@ -516,11 +506,11 @@
     )(stats, first, far, third, p_raw, ub, scores)
     gd = exchange(gd_send.reshape(64, 96, 128), gp).reshape(8, 2, 4, 96, 128)
     half = shape((4, 2, 64, 128), BF)
-    to_third, to_first = pl.pallas_call(
+    to_third, to_first, base = pl.pallas_call(
         context_on_the_way,
-        out_shape=(half, half),
+        out_shape=(half, half, shape((8, 2, 64, 128), F32)),
         in_specs=[sm] + [vm] * 5,
-        out_specs=(vm, vm),
+        out_specs=(vm, vm, vm),
         scratch_shapes=[pltpu.VMEM((512, 8), F32)],
         compiler_params=WHOLE,
         name="context_on_the_way",
@@ -528,12 +518,11 @@
     context_send = pl.pallas_call(
         context_sum,
         out_shape=piece,
-        in_specs=[sm] + [vm] * 7,
+        in_specs=[vm] * 3,
         out_specs=vm,
-        scratch_shapes=[pltpu.VMEM((512, 8), F32)],
         compiler_params=WHOLE,
         name="context_sum",
-    )(block, stats, far, own, first, third, swap(to_third, 3), swap(to_first, 1))
+    )(base, swap(to_third, 3), swap(to_first, 1))
     context = exchange(context_send.reshape(16, 64, 128), rd).reshape(8, 2, 64, 128)
     pair_gradient = pl.pallas_call(
         pair_backward,
@@ -550,24 +539,25 @@
         compiler_params=VMEM,
         name="pair_backward",
     )(pair, gd, saved, proj)
-    partial = pl.pallas_call(
-        msa_partial,
-        out_shape=shape((2, 64, 1024), F32),
-        in_specs=[vm] * 2,
-        out_specs=vm,
-        scratch_shapes=[pltpu.VMEM((1024, 1024), BF)],
-        compiler_params=VMEM,
-        name="msa_partial",
-    )(wc, gd)
     alignment_gradient = pl.pallas_call(
         msa_backward,
+        grid=(1,),
         out_shape=shape((32, 64, 64), BF),
-        in_specs=[vm] * 7,
-        out_specs=vm,
-        scratch_shapes=[pltpu.VMEM((1024, 1024), BF)],
+        in_specs=[
+            const(1, 64),
+            const(64, 64),
+            const(64, 64),
+            const(8, 2, 4, 64, 128),
+            const(8, 2, 64, 128),
+            const(8, 2, 64, 128),
+            const(1024, 128),
+            const(1024, 128),
+        ],
+        out_specs=const(32, 64, 64),
+        scratch_shapes=[pltpu.VMEM((1024, 1024), BF)] * 2,
         compiler_params=WHOLE,
         name="msa_backward",
-    )(gain, ws, context, tail, normed, scale, partial)
+    )(gain, wc, ws, gd, context, tail, normed, scale)
     return (alignment_gradient, pair_gradient)
 
 

time: 157 us -> 156 us (level)
  waiting for transfers between devices: 52.7 us -> 56.5 us
  local copies, waits for them, and re-layouts: 6.31 us -> 3.96 us
    unnamed x44 -> x42, local copies, waits for them, and re-layouts: 6.29 us -> 3.94 us
    all_to_all x3, waiting for transfers between devices: 0.05 us -> 2.34 us  [exchange(): return lax.all_to_all(x, axes, 0, 0, tiled=True)]
    pallas_call x4 -> x3, Pallas kernels: 10.5 us -> 10.3 us  [the longest x1 5.8 us: shards(): pl.pallas_call(msa_backward, grid=(1,), out_shape=shape((32, 64, 64), BF)...]
  transfers between devices with their start and end apart: 12 -> 12, of which waited for: 5 -> 5; matrix products, arithmetic and copies ran while one was open for 0% -> 0% of each run, Pallas kernels for 17% -> 16%
where the time goes in v4:
time: 156 us; the launch traced here: 155 us
  waiting for transfers between devices  56.5 us (36%)
  Pallas kernels  39.1 us (25%)
  starting transfers between devices  39 us (25%)
  blocking collectives  15.7 us (10%)
  local copies, waits for them, and re-layouts  3.96 us (3%)
    ppermute x9, waiting for transfers between devices, swap(): return lax.ppermute(x, 'b', [(i, i ^ k) for i in range(4)])  54.1 us
    all_to_all x3, starting transfers between devices, exchange(): return lax.all_to_all(x, axes, 0, 0, tiled=True)  21.1 us
    ppermute x9, starting transfers between devices, swap(): return lax.ppermute(x, 'b', [(i, i ^ k) for i in range(4)])  17.9 us
    all_to_all x1, blocking collectives, exchange(): return lax.all_to_all(x, axes, 0, 0, tiled=True)  15.7 us
    pallas_call x1, Pallas kernels, shards(): pl.pallas_call(pair_forward, grid=(4,), out_shape=(shape((8, 2, 4, 112, 1...  12.4 us
    pallas_call x1, Pallas kernels, shards(): pl.pallas_call(pair_backward, grid=(4,), out_shape=shape((256, 64, 128),...  6.33 us
    pallas_call x1, Pallas kernels, shards(): pl.pallas_call(msa_backward, grid=(1,), out_shape=shape((32, 64, 64), BF)...  5.8 us
    pallas_call x1, Pallas kernels, shards(): pl.pallas_call(msa_forward, out_shape=(piece, piece, shape((8, 2, 64, 128...  5.05 us
  transfers between devices with their start and end apart: 12, of which 5 were waited for; matrix products, arithmetic and copies ran while one was open for 0% of the time, Pallas kernels for 16%

profile of v4, /device:TPU:32, one launch (start us, length us, event | category | flops | bytes accessed | tf_op | source)
XLA Modules:
  0.0 155.1 jit_solution(5611706077488372329)
XLA Ops:
  0.6 5.0 %msa_forward.1 = (bf16[8,2,64,128]{3,2,1,0:T(8,128)(2,1)}, bf16[8,2,64,128]{3,2,1,0:T(8,128)(2,1)}, f32[8,2,64,128]{3,2,1,0:T(8,128)}) custom-call(s32[32]{0:T(128)} %flags.1, bf16[32,64,64]{2,1,0:T(8,128)(2,1)} %msa.3, bf16[32,64,64]{2,1,0:T(8,128)(2,1)} %adj.1, f32[1,64]{1,0:T(1,128)} %bitcast.33, bf16[64,64]{1,0:T(8,128)(2,1)} %wc.3, bf16[64,64]{1,0:T(8,128)(2,1)} %ws.3, ...), custom_call_target="tpu_custom_call" | custom-call | tf_op jit(solution)/shard_map/msa_forward/pallas_call | solution.py:403
  5.7 15.7 %all_to_all.20 = bf16[16,64,128]{2,1,0:T(8,128)(2,1)S(1)} all-to-all(bf16[16,64,128]{2,1,0:T(8,128)(2,1)} %bitcast.28), channel_id=1, replica_groups=mesh['row'=8,'d'=2,'b'=4,'a'=4] {'row','d'}, dimensions={0} | all-to-all | bytes 524288 | tf_op jit(solution)/shard_map/all_to_all | solution.py:384
  21.4 5.4 %collective-permute-start.2 = (bf16[8,2,64,128]{3,2,1,0:T(8,128)(2,1)S(1)}, bf16[8,2,64,128]{3,2,1,0:T(8,128)(2,1)S(1)}, u32[]{:S(2)}, u32[]{:S(2)}) collective-permute-start(bf16[8,2,64,128]{3,2,1,0:T(8,128)(2,1)S(1)} %bitcast.21), channel_id=1, source_target_pairs={{0,12},{4,8},{8,4},{12,0},{1,13},{5,9},{9,5},{13,1},{2,14},{6,10},... | collective-permute-start | bytes 786440 | tf_op jit(solution)/shard_map/ppermute | solution.py:388
  26.8 1.4 collective-permute-start
  28.3 0.0 copy-done.1
  28.3 12.4 %pair_forward.1 = (bf16[8,2,4,112,128]{4,3,2,1,0:T(8,128)(2,1)}, f32[16,24,1024]{2,1,0:T(8,128)}, f32[8,128]{1,0:T(8,128)}) custom-call(s32[1]{0:T(128)} %bitcast.4.row, s32[1]{0:T(128)} %bitcast.5.col, s32[2048]{0:T(1024)} %chain.1, s32[2048]{0:T(1024)} %position.1, s32[16,128]{1,0:T(8,128)} %bitcast.29, s32[16,128]{1,0:T(8,128)} %bitcast.30, ...), custom_call_target="tpu_custom_call" | custom-call | tf_op jit(solution)/shard_map/pair_forward/pallas_call | solution.py:429
  40.6 0.0 collective-permute-done.2.third.refs_2_
  40.6 0.0 copy-start.4
  40.6 0.0 collective-permute-done.first.refs_1_
  40.6 0.0 copy-start.6
  40.7 0.7 copy-done.4
  41.3 0.1 copy-done.6
  41.4 5.3 %all-to-all-start.1 = ((bf16[64,112,128]{2,1,0:T(8,128)(2,1)}), bf16[64,112,128]{2,1,0:T(8,128)(2,1)S(1)}, u32[]{:S(2)}, u32[]{:S(2)}) async-start(bf16[64,112,128]{2,1,0:T(8,128)(2,1)} %bitcast.25), calls=%async_computation.1 | async-start | bytes 3670016 | tf_op jit(solution)/shard_map/all_to_all | solution.py:384
  46.7 0.0 copy-done.5
  46.7 1.6 %collective-permute-start.3 = (bf16[4,2,64,128]{3,2,1,0:T(8,128)(2,1)S(1)}, bf16[4,2,64,128]{3,2,1,0:T(8,128)(2,1)S(1)}, u32[]{:S(2)}, u32[]{:S(2)}) collective-permute-start(bf16[4,2,64,128]{3,2,1,0:T(8,128)(2,1)S(1)} %slice.9), channel_id=1, source_target_pairs={{0,4},{4,0},{8,12},{12,8},{1,5},{5,1},{9,13},{13,9},{2,6},{6,2},{1... | collective-permute-start | bytes 393224 | tf_op jit(solution)/shard_map/ppermute | solution.py:388
  48.3 0.8 collective-permute-start.1
  49.1 25.2 %collective-permute-done.3.second_b = bf16[4,2,64,128]{3,2,1,0:T(8,128)(2,1)S(1)} collective-permute-done((bf16[4,2,64,128]{3,2,1,0:T(8,128)(2,1)S(1)}, bf16[4,2,64,128]{3,2,1,0:T(8,128)(2,1)S(1)}, u32[]{:S(2)}, u32[]{:S(2)}) %collective-permute-start.3) | collective-permute-done | bytes 131104 | tf_op jit(solution)/shard_map/ppermute | solution.py:388
  74.3 0.0 collective-permute-done.1.second_a
  74.3 0.9 copy-done.8
  75.3 0.1 gather_updates.1.ub
  75.3 0.0 copy-start.3
  75.4 0.0 all-to-all-done.1
  75.4 1.6 %merge_products.1 = (bf16[8,2,2,16,512]{4,3,2,1,0:T(8,128)(2,1)S(1)}, bf16[32,128]{1,0:T(8,128)(2,1)S(1)}, bf16[2,8,2,64,128]{4,3,2,1,0:T(8,128)(2,1)S(1)}, bf16...) custom-call(s32[1]{0:T(128)} %bitcast.1.block, bf16[8,512,128]{2,1,0:T(8,128)(2,1)S(1)} %gather_updates.1.ub, ...), custom_call_target="tpu_custom_call" | custom-call | tf_op jit(solution)/shard_map/merge_products/pallas_call | solution.py:481
  76.9 1.2 collective-permute-start.4
  78.2 1.6 %collective-permute-start.6 = (bf16[1056,128]{1,0:T(8,128)(2,1)S(1)}, bf16[1056,128]{1,0:T(8,128)(2,1)S(1)}, u32[]{:S(2)}, u32[]{:S(2)}) collective-permute-start(bf16[1056,128]{1,0:T(8,128)(2,1)S(1)} %get-tuple-element.24), channel_id=1, source_target_pairs={{0,12},{4,8},{8,4},{12,0},{1,13},{5,9},{9,5},{13,1},{2,14},{6,10},... | collective-permute-start | bytes 811016 | tf_op jit(solution)/shard_map/ppermute | solution.py:388
  79.8 3.7 %collective-permute-start.5 = (bf16[32,128]{1,0:T(8,128)(2,1)S(1)}, bf16[32,128]{1,0:T(8,128)(2,1)S(1)}, u32[]{:S(2)}, u32[]{:S(2)}) collective-permute-start(bf16[32,128]{1,0:T(8,128)(2,1)S(1)} %get-tuple-element.22.own.s0), channel_id=1, source_target_pairs={{0,8},{4,12},{8,0},{12,4},{1,9},{5,13},{9,1},{13,5},{2,10},{6,14},... | collective-permute-start | bytes 24584 | tf_op jit(solution)/shard_map/ppermute | solution.py:388
  83.5 1.2 score_products.1
  84.7 0.8 copy-done.13
  85.5 9.8 %collective-permute-done.5.second.s2 = bf16[32,128]{1,0:T(8,128)(2,1)S(1)} collective-permute-done((bf16[32,128]{1,0:T(8,128)(2,1)S(1)}, bf16[32,128]{1,0:T(8,128)(2,1)S(1)}, u32[]{:S(2)}, u32[]{:S(2)}) %collective-permute-start.5) | collective-permute-done | bytes 8224 | tf_op jit(solution)/shard_map/ppermute | solution.py:388
  95.4 0.0 collective-permute-done.4.first
  95.4 0.0 collective-permute-done.6.third
  95.4 2.2 %gradients.1 = bf16[8,8,96,128]{3,2,1,0:T(8,128)(2,1)} custom-call(bf16[32,128]{1,0:T(8,128)(2,1)S(1)} %get-tuple-element.22.own.s0, bf16[1056,128]{1,0:T(8,128)(2,1)S(1)} %collective-permute-done.4.first, bf16[32,128]{1,0:T(8,128)(2,1)S(1)} %collective-permute-done.5.second.s2, bf16[1056,128]{1,0:T(8,128)(2,1)S(1)} %collective-permute-done.6.third, ...), custom_call_target="tpu_custom_call" | custom-call | tf_op jit(solution)/shard_map/gradients/pallas_call | solution.py:499
  97.6 0.0 copy-done.16
  97.7 8.9 %all-to-all-start.2 = ((bf16[64,96,128]{2,1,0:T(8,128)(2,1)}), bf16[64,96,128]{2,1,0:T(8,128)(2,1)S(1)}, u32[]{:S(2)}, u32[]{:S(2)}) async-start(bf16[64,96,128]{2,1,0:T(8,128)(2,1)} %bitcast.13), calls=%async_computation.2 | async-start | bytes 3145728 | tf_op jit(solution)/shard_map/all_to_all | solution.py:384
  106.6 2.6 %context_on_the_way.1 = (bf16[4,2,64,128]{3,2,1,0:T(8,128)(2,1)}, bf16[4,2,64,128]{3,2,1,0:T(8,128)(2,1)}, f32[8,2,64,128]{3,2,1,0:T(8,128)}) custom-call(s32[1]{0:T(128)} %bitcast.1.block, bf16[32,128]{1,0:T(8,128)(2,1)} %copy-done.15, bf16[32,128]{1,0:T(8,128)(2,1)} %copy-done.16, bf16[2,8,2,64,128]{4,3,2,1,0:T(8,128)(2,1)} %copy-done.14, ...), custom_call_target="tpu_custom_call" | custom-call | tf_op jit(solution)/shard_map/context_on_the_way/pallas_call | solution.py:509
  109.2 0.7 collective-permute-start.7
  109.9 1.5 collective-permute-start.8
  111.4 18.1 %collective-permute-done.7.from_third = bf16[4,2,64,128]{3,2,1,0:T(8,128)(2,1)S(1)} collective-permute-done((bf16[4,2,64,128]{3,2,1,0:T(8,128)(2,1)}, bf16[4,2,64,128]{3,2,1,0:T(8,128)(2,1)S(1)}, u32[]{:S(2)}, u32[]{:S(2)}) %collective-permute-start.7) | collective-permute-done | bytes 131104 | tf_op jit(solution)/shard_map/ppermute | solution.py:388
  129.5 0.9 collective-permute-done.8.from_first
  130.5 0.0 copy-done.19
  130.5 0.6 copy-done.20
  131.1 1.9 %context_sum.1 = bf16[8,2,64,128]{3,2,1,0:T(8,128)(2,1)} custom-call(f32[8,2,64,128]{3,2,1,0:T(8,128)} %get-tuple-element.28.base, bf16[4,2,64,128]{3,2,1,0:T(8,128)(2,1)} %copy-done.19, bf16[4,2,64,128]{3,2,1,0:T(8,128)(2,1)} %copy-done.20), custom_call_target="tpu_custom_call" | custom-call | tf_op jit(solution)/shard_map/context_sum/pallas_call | solution.py:518
  133.0 0.0 all-to-all-done.2
  133.0 6.9 %all-to-all-start.3 = ((bf16[16,64,128]{2,1,0:T(8,128)(2,1)}), bf16[16,64,128]{2,1,0:T(8,128)(2,1)S(1)}, u32[]{:S(2)}, u32[]{:S(2)}) async-start(bf16[16,64,128]{2,1,0:T(8,128)(2,1)} %bitcast.27), calls=%async_computation.3 | async-start | bytes 524288 | tf_op jit(solution)/shard_map/all_to_all | solution.py:384
  139.9 6.3 %pair_backward.1 = bf16[256,64,128]{2,1,0:T(8,128)(2,1)} custom-call(bf16[256,64,128]{2,1,0:T(8,128)(2,1)} %pair.3, bf16[8,2,4,96,128]{4,3,2,1,0:T(8,128)(2,1)S(1)} %bitcast.19, f32[16,24,1024]{2,1,0:T(8,128)S(1)} %copy-done.9, f32[8,128]{1,0:T(8,128)S(1)} %copy-done.17), custom_call_target="tpu_custom_call" | custom-call | tf_op jit(solution)/shard_map/pair_backward/pallas_call | solution.py:527
  146.3 2.3 %all-to-all-done.3 = bf16[16,64,128]{2,1,0:T(8,128)(2,1)S(1)} async-done(((bf16[16,64,128]{2,1,0:T(8,128)(2,1)}), bf16[16,64,128]{2,1,0:T(8,128)(2,1)S(1)}, u32[]{:S(2)}, u32[]{:S(2)}) %all-to-all-start.3) | async-done | bytes 262176 | tf_op jit(solution)/shard_map/all_to_all | solution.py:384
  148.6 0.7 copy-done.18
  149.3 5.8 %msa_backward.1 = bf16[32,64,64]{2,1,0:T(8,128)(2,1)} custom-call(f32[1,64]{1,0:T(1,128)} %bitcast.34, bf16[64,64]{1,0:T(8,128)(2,1)} %wc.3, bf16[64,64]{1,0:T(8,128)(2,1)} %ws.3, bf16[8,2,4,96,128]{4,3,2,1,0:T(8,128)(2,1)} %bitcast.20, bf16[8,2,64,128]{3,2,1,0:T(8,128)(2,1)} %bitcast.26, f32[8,2,64,128]{3,2,1,0:T(8,128)} %get-tuple-element.31.tail, ...), custom_call_target="tpu_custom_call" | custom-call | tf_op jit(solution)/shard_map/msa_backward/pallas_call | solution.py:542
  (32 shorter events, 0.1 us)
Async XLA Ops:
  21.4 6.9 %copy-start.1 = (bf16[16,64,128]{2,1,0:T(8,128)(2,1)}, bf16[16,64,128]{2,1,0:T(8,128)(2,1)S(1)}, u32[]{:S(2)}) copy-start(bf16[16,64,128]{2,1,0:T(8,128)(2,1)S(1)} %all_to_all.20) | copy-start | bytes 786436
  21.4 19.2 %collective-permute-start.2 = (bf16[8,2,64,128]{3,2,1,0:T(8,128)(2,1)S(1)}, bf16[8,2,64,128]{3,2,1,0:T(8,128)(2,1)S(1)}, u32[]{:S(2)}, u32[]{:S(2)}) collective-permute-start(bf16[8,2,64,128]{3,2,1,0:T(8,128)(2,1)S(1)} %bitcast.21), channel_id=1, source_target_pairs={{0,12},{4,8},{8,4},{12,0},{1,13},{5,9},{9,5},{13,1},{2,14},{6,10},... | collective-permute-start | bytes 786440 | tf_op jit(solution)/shard_map/ppermute | solution.py:388
  26.8 13.8 %collective-permute-start = (bf16[8,2,64,128]{3,2,1,0:T(8,128)(2,1)S(1)}, bf16[8,2,64,128]{3,2,1,0:T(8,128)(2,1)S(1)}, u32[]{:S(2)}, u32[]{:S(2)}) collective-permute-start(bf16[8,2,64,128]{3,2,1,0:T(8,128)(2,1)S(1)} %bitcast.22), channel_id=1, source_target_pairs={{0,4},{4,0},{8,12},{12,8},{1,5},{5,1},{9,13},{13,9},{2,6},{6,2},{1... | collective-permute-start | bytes 786440 | tf_op jit(solution)/shard_map/ppermute | solution.py:388
  40.6 0.7 copy-start.4
  40.6 0.8 copy-start.6
  41.4 5.3 %copy-start.5 = (bf16[8,2,64,128]{3,2,1,0:T(8,128)(2,1)S(1)}, bf16[8,2,64,128]{3,2,1,0:T(8,128)(2,1)}, u32[]{:S(2)}) copy-start(bf16[8,2,64,128]{3,2,1,0:T(8,128)(2,1)} %copy-done.4) | copy-start | bytes 786436
  41.4 6.9 %copy-start.7 = (bf16[8,2,64,128]{3,2,1,0:T(8,128)(2,1)S(1)}, bf16[8,2,64,128]{3,2,1,0:T(8,128)(2,1)}, u32[]{:S(2)}) copy-start(bf16[8,2,64,128]{3,2,1,0:T(8,128)(2,1)} %copy-done.6) | copy-start | bytes 786436
  41.4 32.9 %copy-start.2 = (bf16[16,64,128]{2,1,0:T(8,128)(2,1)S(1)}, bf16[16,64,128]{2,1,0:T(8,128)(2,1)}, u32[]{:S(2)}) copy-start(bf16[16,64,128]{2,1,0:T(8,128)(2,1)} %copy-done.1) | copy-start | bytes 786436
  41.4 33.9 %all-to-all-start.1 = ((bf16[64,112,128]{2,1,0:T(8,128)(2,1)}), bf16[64,112,128]{2,1,0:T(8,128)(2,1)S(1)}, u32[]{:S(2)}, u32[]{:S(2)}) async-start(bf16[64,112,128]{2,1,0:T(8,128)(2,1)} %bitcast.25), calls=%async_computation.1 | async-start | bytes 3670016 | tf_op jit(solution)/shard_map/all_to_all | solution.py:384
  46.7 27.6 %collective-permute-start.3 = (bf16[4,2,64,128]{3,2,1,0:T(8,128)(2,1)S(1)}, bf16[4,2,64,128]{3,2,1,0:T(8,128)(2,1)S(1)}, u32[]{:S(2)}, u32[]{:S(2)}) collective-permute-start(bf16[4,2,64,128]{3,2,1,0:T(8,128)(2,1)S(1)} %slice.9), channel_id=1, source_target_pairs={{0,4},{4,0},{8,12},{12,8},{1,5},{5,1},{9,13},{13,9},{2,6},{6,2},{1... | collective-permute-start | bytes 393224 | tf_op jit(solution)/shard_map/ppermute | solution.py:388
  48.3 26.0 %collective-permute-start.1 = (bf16[4,2,64,128]{3,2,1,0:T(8,128)(2,1)S(1)}, bf16[4,2,64,128]{3,2,1,0:T(8,128)(2,1)S(1)}, u32[]{:S(2)}, u32[]{:S(2)}) collective-permute-start(bf16[4,2,64,128]{3,2,1,0:T(8,128)(2,1)S(1)} %slice.8), channel_id=1, source_target_pairs={{0,12},{4,8},{8,4},{12,0},{1,13},{5,9},{9,5},{13,1},{2,14},{6,10},... | collective-permute-start | bytes 393224 | tf_op jit(solution)/shard_map/ppermute | solution.py:388
  74.3 1.0 copy-start.8
  75.3 8.2 %copy-start.3 = (bf16[32,64,64]{2,1,0:T(8,128)(2,1)S(1)}, bf16[32,64,64]{2,1,0:T(8,128)(2,1)}, u32[]{:S(2)}) copy-start(bf16[32,64,64]{2,1,0:T(8,128)(2,1)} %msa.3) | copy-start | bytes 786436
  76.9 18.4 %copy-start.14 = (bf16[2,8,2,64,128]{4,3,2,1,0:T(8,128)(2,1)}, bf16[2,8,2,64,128]{4,3,2,1,0:T(8,128)(2,1)S(1)}, u32[]{:S(2)}) copy-start(bf16[2,8,2,64,128]{4,3,2,1,0:T(8,128)(2,1)S(1)} %get-tuple-element.27.c) | copy-start | bytes 1572868
  76.9 20.7 %copy-start.15 = (bf16[32,128]{1,0:T(8,128)(2,1)}, bf16[32,128]{1,0:T(8,128)(2,1)S(1)}, u32[]{:S(2)}) copy-start(bf16[32,128]{1,0:T(8,128)(2,1)S(1)} %get-tuple-element.22.own.s0) | copy-start | bytes 24580
  76.9 18.4 %collective-permute-start.4 = (bf16[1056,128]{1,0:T(8,128)(2,1)S(1)}, bf16[1056,128]{1,0:T(8,128)(2,1)S(1)}, u32[]{:S(2)}, u32[]{:S(2)}) collective-permute-start(bf16[1056,128]{1,0:T(8,128)(2,1)S(1)} %get-tuple-element.23), channel_id=1, source_target_pairs={{0,4},{4,0},{8,12},{12,8},{1,5},{5,1},{9,13},{13,9},{2,6},{6,2},{1... | collective-permute-start | bytes 811016 | tf_op jit(solution)/shard_map/ppermute | solution.py:388
  78.2 17.2 %collective-permute-start.6 = (bf16[1056,128]{1,0:T(8,128)(2,1)S(1)}, bf16[1056,128]{1,0:T(8,128)(2,1)S(1)}, u32[]{:S(2)}, u32[]{:S(2)}) collective-permute-start(bf16[1056,128]{1,0:T(8,128)(2,1)S(1)} %get-tuple-element.24), channel_id=1, source_target_pairs={{0,12},{4,8},{8,4},{12,0},{1,13},{5,9},{9,5},{13,1},{2,14},{6,10},... | collective-permute-start | bytes 811016 | tf_op jit(solution)/shard_map/ppermute | solution.py:388
  79.8 15.6 %collective-permute-start.5 = (bf16[32,128]{1,0:T(8,128)(2,1)S(1)}, bf16[32,128]{1,0:T(8,128)(2,1)S(1)}, u32[]{:S(2)}, u32[]{:S(2)}) collective-permute-start(bf16[32,128]{1,0:T(8,128)(2,1)S(1)} %get-tuple-element.22.own.s0), channel_id=1, source_target_pairs={{0,8},{4,12},{8,0},{12,4},{1,9},{5,13},{9,1},{13,5},{2,10},{6,14},... | collective-permute-start | bytes 24584 | tf_op jit(solution)/shard_map/ppermute | solution.py:388
  84.7 0.8 copy-start.13
  85.5 12.1 %copy-start.12 = (f32[1024,128]{1,0:T(8,128)}, f32[1024,128]{1,0:T(8,128)S(1)}, u32[]{:S(2)}) copy-start(f32[1024,128]{1,0:T(8,128)S(1)} %get-tuple-element.32.normed) | copy-start | bytes 1572868
  95.4 2.3 %copy-start.16 = (bf16[32,128]{1,0:T(8,128)(2,1)}, bf16[32,128]{1,0:T(8,128)(2,1)S(1)}, u32[]{:S(2)}) copy-start(bf16[32,128]{1,0:T(8,128)(2,1)S(1)} %collective-permute-done.5.second.s2) | copy-start | bytes 24580
  95.4 2.3 %copy-start.10 = (bf16[1056,128]{1,0:T(8,128)(2,1)}, bf16[1056,128]{1,0:T(8,128)(2,1)S(1)}, u32[]{:S(2)}) copy-start(bf16[1056,128]{1,0:T(8,128)(2,1)S(1)} %collective-permute-done.4.first) | copy-start | bytes 811012
  95.4 2.3 %copy-start.11 = (bf16[1056,128]{1,0:T(8,128)(2,1)}, bf16[1056,128]{1,0:T(8,128)(2,1)S(1)}, u32[]{:S(2)}) copy-start(bf16[1056,128]{1,0:T(8,128)(2,1)S(1)} %collective-permute-done.6.third) | copy-start | bytes 811012
  97.7 35.3 %all-to-all-start.2 = ((bf16[64,96,128]{2,1,0:T(8,128)(2,1)}), bf16[64,96,128]{2,1,0:T(8,128)(2,1)S(1)}, u32[]{:S(2)}, u32[]{:S(2)}) async-start(bf16[64,96,128]{2,1,0:T(8,128)(2,1)} %bitcast.13), calls=%async_computation.2 | async-start | bytes 3145728 | tf_op jit(solution)/shard_map/all_to_all | solution.py:384
  106.6 33.3 %copy-start.9 = (f32[16,24,1024]{2,1,0:T(8,128)S(1)}, f32[16,24,1024]{2,1,0:T(8,128)}, u32[]{:S(2)}) copy-start(f32[16,24,1024]{2,1,0:T(8,128)} %get-tuple-element.34.saved) | copy-start | bytes 4718596
  106.6 33.3 %copy-start.17 = (f32[8,128]{1,0:T(8,128)S(1)}, f32[8,128]{1,0:T(8,128)}, u32[]{:S(2)}) copy-start(f32[8,128]{1,0:T(8,128)} %get-tuple-element.35.proj) | copy-start | bytes 12292
  109.2 20.3 %collective-permute-start.7 = (bf16[4,2,64,128]{3,2,1,0:T(8,128)(2,1)}, bf16[4,2,64,128]{3,2,1,0:T(8,128)(2,1)S(1)}, u32[]{:S(2)}, u32[]{:S(2)}) collective-permute-start(bf16[4,2,64,128]{3,2,1,0:T(8,128)(2,1)} %get-tuple-element.29), channel_id=1, source_target_pairs={{0,12},{4,8},{8,4},{12,0},{1,13},{5,9},{9,5},{13,1},{2,14},{6,10},... | collective-permute-start | bytes 393224 | tf_op jit(solution)/shard_map/ppermute | solution.py:388
  109.9 20.5 %collective-permute-start.8 = (bf16[4,2,64,128]{3,2,1,0:T(8,128)(2,1)}, bf16[4,2,64,128]{3,2,1,0:T(8,128)(2,1)S(1)}, u32[]{:S(2)}, u32[]{:S(2)}) collective-permute-start(bf16[4,2,64,128]{3,2,1,0:T(8,128)(2,1)} %get-tuple-element.30), channel_id=1, source_target_pairs={{0,4},{4,0},{8,12},{12,8},{1,5},{5,1},{9,13},{13,9},{2,6},{6,2},{1... | collective-permute-start | bytes 393224 | tf_op jit(solution)/shard_map/ppermute | solution.py:388
  129.5 0.9 copy-start.19
  130.5 0.7 copy-start.20
  133.0 13.3 %copy-start = (bf16[64,96,128]{2,1,0:T(8,128)(2,1)}, bf16[64,96,128]{2,1,0:T(8,128)(2,1)S(1)}, u32[]{:S(2)}) copy-start(bf16[64,96,128]{2,1,0:T(8,128)(2,1)S(1)} %all-to-all-done.2) | copy-start | bytes 4718596
  133.0 15.6 %all-to-all-start.3 = ((bf16[16,64,128]{2,1,0:T(8,128)(2,1)}), bf16[16,64,128]{2,1,0:T(8,128)(2,1)S(1)}, u32[]{:S(2)}, u32[]{:S(2)}) async-start(bf16[16,64,128]{2,1,0:T(8,128)(2,1)} %bitcast.27), calls=%async_computation.3 | async-start | bytes 524288 | tf_op jit(solution)/shard_map/all_to_all | solution.py:384
  148.6 0.7 copy-start.18

commit v5 on v4

--- a/solution.py
+++ b/solution.py
@@ -319,11 +319,6 @@
             )
 
 
-def context_sum(base, from_third, from_first, out):
-    out[0:4] = (base[0:4] + from_third[...].astype(F32)).astype(BF)
-    out[4:8] = (base[4:8] + from_first[...].astype(F32)).astype(BF)
-
-
 def pair_backward(pair, grads, saved, proj, out, g_s):
     w_hi, w_mid, _ = split3(proj[...])
     row = iota((8, 128), 0)
@@ -515,14 +510,8 @@
         compiler_params=WHOLE,
         name="context_on_the_way",
     )(block, stats, far, own, first, third)
-    context_send = pl.pallas_call(
-        context_sum,
-        out_shape=piece,
-        in_specs=[vm] * 3,
-        out_specs=vm,
-        compiler_params=WHOLE,
-        name="context_sum",
-    )(base, swap(to_third, 3), swap(to_first, 1))
+    far = jnp.concatenate([swap(to_third, 3), swap(to_first, 1)], axis=0)
+    context_send = (base + far.astype(F32)).astype(BF)
     context = exchange(context_send.reshape(16, 64, 128), rd).reshape(8, 2, 64, 128)
     pair_gradient = pl.pallas_call(
         pair_backward,

time: 156 us -> 155 us (level)
  Pallas kernels: 39.1 us -> 37.2 us
  other arithmetic: 0 us -> 1.82 us
    pallas_call x1 -> x0, Pallas kernels: 1.88 us -> none  [shards(): pl.pallas_call(context_sum, out_shape=piece, in_specs=[vm] * 3, out_specs...]
    convert_element_type x0 -> x1, other arithmetic: none -> 1.82 us  [shards(): context_send = (base + far.astype(F32)).astype(BF)]
    unnamed x42 -> x38, local copies, waits for them, and re-layouts: 3.94 us -> 3.28 us
  transfers between devices with their start and end apart: 12 -> 12, of which waited for: 5 -> 5; matrix products, arithmetic and copies ran while one was open for 0% -> 1% of each run, Pallas kernels for 16% -> 15%
where the time goes in v5:
time: 155 us; the launch traced here: 154 us
  waiting for transfers between devices  56.5 us (36%)
  starting transfers between devices  39 us (25%)
  Pallas kernels  37.2 us (24%)
  blocking collectives  15.7 us (10%)
  local copies, waits for them, and re-layouts  3.3 us (2%)
  other arithmetic  1.82 us (1%)
    ppermute x9, waiting for transfers between devices, swap(): return lax.ppermute(x, 'b', [(i, i ^ k) for i in range(4)])  54.1 us
    all_to_all x3, starting transfers between devices, exchange(): return lax.all_to_all(x, axes, 0, 0, tiled=True)  21.1 us
    ppermute x9, starting transfers between devices, swap(): return lax.ppermute(x, 'b', [(i, i ^ k) for i in range(4)])  17.9 us
    all_to_all x1, blocking collectives, exchange(): return lax.all_to_all(x, axes, 0, 0, tiled=True)  15.7 us
    pallas_call x1, Pallas kernels, shards(): pl.pallas_call(pair_forward, grid=(4,), out_shape=(shape((8, 2, 4, 112, 1...  12.3 us
    pallas_call x1, Pallas kernels, shards(): pl.pallas_call(pair_backward, grid=(4,), out_shape=shape((256, 64, 128),...  6.33 us
    pallas_call x1, Pallas kernels, shards(): pl.pallas_call(msa_backward, grid=(1,), out_shape=shape((32, 64, 64), BF)...  5.8 us
    pallas_call x1, Pallas kernels, shards(): pl.pallas_call(msa_forward, out_shape=(piece, piece, shape((8, 2, 64, 128...  5.05 us
  transfers between devices with their start and end apart: 12, of which 5 were waited for; matrix products, arithmetic and copies ran while one was open for 1% of the time, Pallas kernels for 15%

profile of v5, /device:TPU:32, one launch (start us, length us, event | category | flops | bytes accessed | tf_op | source)
XLA Modules:
  0.0 154.4 jit_solution(14341772219658523803)
XLA Ops:
  0.6 5.1 %msa_forward.1 = (bf16[8,2,64,128]{3,2,1,0:T(8,128)(2,1)}, bf16[8,2,64,128]{3,2,1,0:T(8,128)(2,1)}, f32[8,2,64,128]{3,2,1,0:T(8,128)}) custom-call(s32[32]{0:T(128)} %flags.1, bf16[32,64,64]{2,1,0:T(8,128)(2,1)} %msa.3, bf16[32,64,64]{2,1,0:T(8,128)(2,1)} %adj.1, f32[1,64]{1,0:T(1,128)} %bitcast.33, bf16[64,64]{1,0:T(8,128)(2,1)} %wc.3, bf16[64,64]{1,0:T(8,128)(2,1)} %ws.3, ...), custom_call_target="tpu_custom_call" | custom-call | tf_op jit(solution)/shard_map/msa_forward/pallas_call | solution.py:398
  5.7 15.7 %all_to_all.20 = bf16[16,64,128]{2,1,0:T(8,128)(2,1)S(1)} all-to-all(bf16[16,64,128]{2,1,0:T(8,128)(2,1)} %bitcast.28), channel_id=1, replica_groups=mesh['row'=8,'d'=2,'b'=4,'a'=4] {'row','d'}, dimensions={0} | all-to-all | bytes 524288 | tf_op jit(solution)/shard_map/all_to_all | solution.py:379
  21.4 5.4 %collective-permute-start.2 = (bf16[8,2,64,128]{3,2,1,0:T(8,128)(2,1)S(1)}, bf16[8,2,64,128]{3,2,1,0:T(8,128)(2,1)S(1)}, u32[]{:S(2)}, u32[]{:S(2)}) collective-permute-start(bf16[8,2,64,128]{3,2,1,0:T(8,128)(2,1)S(1)} %bitcast.21), channel_id=1, source_target_pairs={{0,12},{4,8},{8,4},{12,0},{1,13},{5,9},{9,5},{13,1},{2,14},{6,10},... | collective-permute-start | bytes 786440 | tf_op jit(solution)/shard_map/ppermute | solution.py:383
  26.8 1.4 collective-permute-start
  28.3 0.0 copy-done.1
  28.3 12.3 %pair_forward.1 = (bf16[8,2,4,112,128]{4,3,2,1,0:T(8,128)(2,1)}, f32[16,24,1024]{2,1,0:T(8,128)}, f32[8,128]{1,0:T(8,128)}) custom-call(s32[1]{0:T(128)} %bitcast.4.row, s32[1]{0:T(128)} %bitcast.5.col, s32[2048]{0:T(1024)} %chain.1, s32[2048]{0:T(1024)} %position.1, s32[16,128]{1,0:T(8,128)} %bitcast.29, s32[16,128]{1,0:T(8,128)} %bitcast.30, ...), custom_call_target="tpu_custom_call" | custom-call | tf_op jit(solution)/shard_map/pair_forward/pallas_call | solution.py:424
  40.6 0.0 collective-permute-done.2.third.refs_2_
  40.6 0.0 copy-start.4
  40.6 0.0 collective-permute-done.first.refs_1_
  40.6 0.0 copy-start.6
  40.7 0.7 copy-done.4
  41.3 0.1 copy-done.6
  41.4 5.3 %all-to-all-start.1 = ((bf16[64,112,128]{2,1,0:T(8,128)(2,1)}), bf16[64,112,128]{2,1,0:T(8,128)(2,1)S(1)}, u32[]{:S(2)}, u32[]{:S(2)}) async-start(bf16[64,112,128]{2,1,0:T(8,128)(2,1)} %bitcast.25), calls=%async_computation.1 | async-start | bytes 3670016 | tf_op jit(solution)/shard_map/all_to_all | solution.py:379
  46.7 0.0 copy-done.5
  46.7 1.6 %collective-permute-start.3 = (bf16[4,2,64,128]{3,2,1,0:T(8,128)(2,1)S(1)}, bf16[4,2,64,128]{3,2,1,0:T(8,128)(2,1)S(1)}, u32[]{:S(2)}, u32[]{:S(2)}) collective-permute-start(bf16[4,2,64,128]{3,2,1,0:T(8,128)(2,1)S(1)} %slice.9), channel_id=1, source_target_pairs={{0,4},{4,0},{8,12},{12,8},{1,5},{5,1},{9,13},{13,9},{2,6},{6,2},{1... | collective-permute-start | bytes 393224 | tf_op jit(solution)/shard_map/ppermute | solution.py:383
  48.3 0.8 collective-permute-start.1
  49.1 25.2 %collective-permute-done.3.second_b = bf16[4,2,64,128]{3,2,1,0:T(8,128)(2,1)S(1)} collective-permute-done((bf16[4,2,64,128]{3,2,1,0:T(8,128)(2,1)S(1)}, bf16[4,2,64,128]{3,2,1,0:T(8,128)(2,1)S(1)}, u32[]{:S(2)}, u32[]{:S(2)}) %collective-permute-start.3) | collective-permute-done | bytes 131104 | tf_op jit(solution)/shard_map/ppermute | solution.py:383
  74.3 0.0 collective-permute-done.1.second_a
  74.3 0.9 copy-done.8
  75.3 0.1 gather_updates.1.ub
  75.3 0.0 copy-start.3
  75.4 0.0 all-to-all-done.1
  75.4 1.6 %merge_products.1 = (bf16[8,2,2,16,512]{4,3,2,1,0:T(8,128)(2,1)S(1)}, bf16[32,128]{1,0:T(8,128)(2,1)S(1)}, bf16[2,8,2,64,128]{4,3,2,1,0:T(8,128)(2,1)S(1)}, bf16...) custom-call(s32[1]{0:T(128)} %bitcast.1.block, bf16[8,512,128]{2,1,0:T(8,128)(2,1)S(1)} %gather_updates.1.ub, ...), custom_call_target="tpu_custom_call" | custom-call | tf_op jit(solution)/shard_map/merge_products/pallas_call | solution.py:476
  76.9 1.2 collective-permute-start.4
  78.2 1.6 %collective-permute-start.6 = (bf16[1056,128]{1,0:T(8,128)(2,1)S(1)}, bf16[1056,128]{1,0:T(8,128)(2,1)S(1)}, u32[]{:S(2)}, u32[]{:S(2)}) collective-permute-start(bf16[1056,128]{1,0:T(8,128)(2,1)S(1)} %get-tuple-element.24), channel_id=1, source_target_pairs={{0,12},{4,8},{8,4},{12,0},{1,13},{5,9},{9,5},{13,1},{2,14},{6,10},... | collective-permute-start | bytes 811016 | tf_op jit(solution)/shard_map/ppermute | solution.py:383
  79.8 3.7 %collective-permute-start.5 = (bf16[32,128]{1,0:T(8,128)(2,1)S(1)}, bf16[32,128]{1,0:T(8,128)(2,1)S(1)}, u32[]{:S(2)}, u32[]{:S(2)}) collective-permute-start(bf16[32,128]{1,0:T(8,128)(2,1)S(1)} %get-tuple-element.22.own.s0), channel_id=1, source_target_pairs={{0,8},{4,12},{8,0},{12,4},{1,9},{5,13},{9,1},{13,5},{2,10},{6,14},... | collective-permute-start | bytes 24584 | tf_op jit(solution)/shard_map/ppermute | solution.py:383
  83.5 0.0 copy-done.3
  83.5 1.2 score_products.1
  84.7 0.8 copy-done.13
  85.5 9.8 %collective-permute-done.5.second.s2 = bf16[32,128]{1,0:T(8,128)(2,1)S(1)} collective-permute-done((bf16[32,128]{1,0:T(8,128)(2,1)S(1)}, bf16[32,128]{1,0:T(8,128)(2,1)S(1)}, u32[]{:S(2)}, u32[]{:S(2)}) %collective-permute-start.5) | collective-permute-done | bytes 8224 | tf_op jit(solution)/shard_map/ppermute | solution.py:383
  95.4 0.0 collective-permute-done.4.first
  95.4 0.0 collective-permute-done.6.third
  95.4 2.2 %gradients.1 = bf16[8,8,96,128]{3,2,1,0:T(8,128)(2,1)} custom-call(bf16[32,128]{1,0:T(8,128)(2,1)S(1)} %get-tuple-element.22.own.s0, bf16[1056,128]{1,0:T(8,128)(2,1)S(1)} %collective-permute-done.4.first, bf16[32,128]{1,0:T(8,128)(2,1)S(1)} %collective-permute-done.5.second.s2, bf16[1056,128]{1,0:T(8,128)(2,1)S(1)} %collective-permute-done.6.third, ...), custom_call_target="tpu_custom_call" | custom-call | tf_op jit(solution)/shard_map/gradients/pallas_call | solution.py:494
  97.6 0.0 copy-done.15
  97.6 0.0 copy-done.11
  97.6 8.9 %all-to-all-start.2 = ((bf16[64,96,128]{2,1,0:T(8,128)(2,1)}), bf16[64,96,128]{2,1,0:T(8,128)(2,1)S(1)}, u32[]{:S(2)}, u32[]{:S(2)}) async-start(bf16[64,96,128]{2,1,0:T(8,128)(2,1)} %bitcast.13), calls=%async_computation.2 | async-start | bytes 3145728 | tf_op jit(solution)/shard_map/all_to_all | solution.py:379
  106.6 2.6 %context_on_the_way.1 = (bf16[4,2,64,128]{3,2,1,0:T(8,128)(2,1)}, bf16[4,2,64,128]{3,2,1,0:T(8,128)(2,1)}, f32[8,2,64,128]{3,2,1,0:T(8,128)}) custom-call(s32[1]{0:T(128)} %bitcast.1.block, bf16[32,128]{1,0:T(8,128)(2,1)} %copy-done.15, bf16[32,128]{1,0:T(8,128)(2,1)} %copy-done.16, bf16[2,8,2,64,128]{4,3,2,1,0:T(8,128)(2,1)} %copy-done.14, ...), custom_call_target="tpu_custom_call" | custom-call | tf_op jit(solution)/shard_map/context_on_the_way/pallas_call | solution.py:504
  109.2 0.7 collective-permute-start.7
  109.9 1.5 collective-permute-start.8
  111.4 18.1 %collective-permute-done.7 = bf16[4,2,64,128]{3,2,1,0:T(8,128)(2,1)S(1)} collective-permute-done((bf16[4,2,64,128]{3,2,1,0:T(8,128)(2,1)}, bf16[4,2,64,128]{3,2,1,0:T(8,128)(2,1)S(1)}, u32[]{:S(2)}, u32[]{:S(2)}) %collective-permute-start.7) | collective-permute-done | bytes 131104 | tf_op jit(solution)/shard_map/ppermute | solution.py:383
  129.5 0.9 collective-permute-done.8
  130.4 1.8 %add_convert_fusion = bf16[8,2,64,128]{3,2,1,0:T(8,128)(2,1)} fusion(f32[8,2,64,128]{3,2,1,0:T(8,128)} %get-tuple-element.28, bf16[4,2,64,128]{3,2,1,0:T(8,128)(2,1)S(1)} %collective-permute-done.8, bf16[4,2,64,128]{3,2,1,0:T(8,128)(2,1)S(1)} %collective-permute-done.7), kind=kLoop, calls=%fused_computation | loop fusion | flops 524288 | bytes 1048576 | tf_op jit(solution)/shard_map/convert_element_type | solution.py:514
  132.3 0.0 all-to-all-done.2
  132.3 6.9 %all-to-all-start.3 = ((bf16[16,64,128]{2,1,0:T(8,128)(2,1)}), bf16[16,64,128]{2,1,0:T(8,128)(2,1)S(1)}, u32[]{:S(2)}, u32[]{:S(2)}) async-start(bf16[16,64,128]{2,1,0:T(8,128)(2,1)} %bitcast.27), calls=%async_computation.3 | async-start | bytes 524288 | tf_op jit(solution)/shard_map/all_to_all | solution.py:379
  139.2 6.3 %pair_backward.1 = bf16[256,64,128]{2,1,0:T(8,128)(2,1)} custom-call(bf16[256,64,128]{2,1,0:T(8,128)(2,1)} %pair.3, bf16[8,2,4,96,128]{4,3,2,1,0:T(8,128)(2,1)S(1)} %bitcast.19, f32[16,24,1024]{2,1,0:T(8,128)S(1)} %copy-done.9, f32[8,128]{1,0:T(8,128)S(1)} %copy-done.17), custom_call_target="tpu_custom_call" | custom-call | tf_op jit(solution)/shard_map/pair_backward/pallas_call | solution.py:516
  145.5 2.3 %all-to-all-done.3 = bf16[16,64,128]{2,1,0:T(8,128)(2,1)S(1)} async-done(((bf16[16,64,128]{2,1,0:T(8,128)(2,1)}), bf16[16,64,128]{2,1,0:T(8,128)(2,1)S(1)}, u32[]{:S(2)}, u32[]{:S(2)}) %all-to-all-start.3) | async-done | bytes 262176 | tf_op jit(solution)/shard_map/all_to_all | solution.py:379
  147.9 0.7 copy-done.18
  148.6 5.8 %msa_backward.1 = bf16[32,64,64]{2,1,0:T(8,128)(2,1)} custom-call(f32[1,64]{1,0:T(1,128)} %bitcast.34, bf16[64,64]{1,0:T(8,128)(2,1)} %wc.3, bf16[64,64]{1,0:T(8,128)(2,1)} %ws.3, bf16[8,2,4,96,128]{4,3,2,1,0:T(8,128)(2,1)} %bitcast.20, bf16[8,2,64,128]{3,2,1,0:T(8,128)(2,1)} %bitcast.26, f32[8,2,64,128]{3,2,1,0:T(8,128)} %get-tuple-element.31.tail, ...), custom_call_target="tpu_custom_call" | custom-call | tf_op jit(solution)/shard_map/msa_backward/pallas_call | solution.py:531
  (28 shorter events, 0.1 us)
Async XLA Ops:
  21.4 6.9 %copy-start.1 = (bf16[16,64,128]{2,1,0:T(8,128)(2,1)}, bf16[16,64,128]{2,1,0:T(8,128)(2,1)S(1)}, u32[]{:S(2)}) copy-start(bf16[16,64,128]{2,1,0:T(8,128)(2,1)S(1)} %all_to_all.20) | copy-start | bytes 786436
  21.4 19.2 %collective-permute-start.2 = (bf16[8,2,64,128]{3,2,1,0:T(8,128)(2,1)S(1)}, bf16[8,2,64,128]{3,2,1,0:T(8,128)(2,1)S(1)}, u32[]{:S(2)}, u32[]{:S(2)}) collective-permute-start(bf16[8,2,64,128]{3,2,1,0:T(8,128)(2,1)S(1)} %bitcast.21), channel_id=1, source_target_pairs={{0,12},{4,8},{8,4},{12,0},{1,13},{5,9},{9,5},{13,1},{2,14},{6,10},... | collective-permute-start | bytes 786440 | tf_op jit(solution)/shard_map/ppermute | solution.py:383
  26.8 13.8 %collective-permute-start = (bf16[8,2,64,128]{3,2,1,0:T(8,128)(2,1)S(1)}, bf16[8,2,64,128]{3,2,1,0:T(8,128)(2,1)S(1)}, u32[]{:S(2)}, u32[]{:S(2)}) collective-permute-start(bf16[8,2,64,128]{3,2,1,0:T(8,128)(2,1)S(1)} %bitcast.22), channel_id=1, source_target_pairs={{0,4},{4,0},{8,12},{12,8},{1,5},{5,1},{9,13},{13,9},{2,6},{6,2},{1... | collective-permute-start | bytes 786440 | tf_op jit(solution)/shard_map/ppermute | solution.py:383
  40.6 0.7 copy-start.4
  40.6 0.8 copy-start.6
  41.4 5.3 %copy-start.5 = (bf16[8,2,64,128]{3,2,1,0:T(8,128)(2,1)S(1)}, bf16[8,2,64,128]{3,2,1,0:T(8,128)(2,1)}, u32[]{:S(2)}) copy-start(bf16[8,2,64,128]{3,2,1,0:T(8,128)(2,1)} %copy-done.4) | copy-start | bytes 786436
  41.4 6.9 %copy-start.7 = (bf16[8,2,64,128]{3,2,1,0:T(8,128)(2,1)S(1)}, bf16[8,2,64,128]{3,2,1,0:T(8,128)(2,1)}, u32[]{:S(2)}) copy-start(bf16[8,2,64,128]{3,2,1,0:T(8,128)(2,1)} %copy-done.6) | copy-start | bytes 786436
  41.4 32.9 %copy-start.2 = (bf16[16,64,128]{2,1,0:T(8,128)(2,1)S(1)}, bf16[16,64,128]{2,1,0:T(8,128)(2,1)}, u32[]{:S(2)}) copy-start(bf16[16,64,128]{2,1,0:T(8,128)(2,1)} %copy-done.1) | copy-start | bytes 786436
  41.4 33.9 %all-to-all-start.1 = ((bf16[64,112,128]{2,1,0:T(8,128)(2,1)}), bf16[64,112,128]{2,1,0:T(8,128)(2,1)S(1)}, u32[]{:S(2)}, u32[]{:S(2)}) async-start(bf16[64,112,128]{2,1,0:T(8,128)(2,1)} %bitcast.25), calls=%async_computation.1 | async-start | bytes 3670016 | tf_op jit(solution)/shard_map/all_to_all | solution.py:379
  46.7 27.6 %collective-permute-start.3 = (bf16[4,2,64,128]{3,2,1,0:T(8,128)(2,1)S(1)}, bf16[4,2,64,128]{3,2,1,0:T(8,128)(2,1)S(1)}, u32[]{:S(2)}, u32[]{:S(2)}) collective-permute-start(bf16[4,2,64,128]{3,2,1,0:T(8,128)(2,1)S(1)} %slice.9), channel_id=1, source_target_pairs={{0,4},{4,0},{8,12},{12,8},{1,5},{5,1},{9,13},{13,9},{2,6},{6,2},{1... | collective-permute-start | bytes 393224 | tf_op jit(solution)/shard_map/ppermute | solution.py:383
  48.3 26.0 %collective-permute-start.1 = (bf16[4,2,64,128]{3,2,1,0:T(8,128)(2,1)S(1)}, bf16[4,2,64,128]{3,2,1,0:T(8,128)(2,1)S(1)}, u32[]{:S(2)}, u32[]{:S(2)}) collective-permute-start(bf16[4,2,64,128]{3,2,1,0:T(8,128)(2,1)S(1)} %slice.8), channel_id=1, source_target_pairs={{0,12},{4,8},{8,4},{12,0},{1,13},{5,9},{9,5},{13,1},{2,14},{6,10},... | collective-permute-start | bytes 393224 | tf_op jit(solution)/shard_map/ppermute | solution.py:383
  74.3 1.0 copy-start.8
  75.3 8.2 %copy-start.3 = (bf16[32,64,64]{2,1,0:T(8,128)(2,1)S(1)}, bf16[32,64,64]{2,1,0:T(8,128)(2,1)}, u32[]{:S(2)}) copy-start(bf16[32,64,64]{2,1,0:T(8,128)(2,1)} %msa.3) | copy-start | bytes 786436
  76.9 18.4 %copy-start.14 = (bf16[2,8,2,64,128]{4,3,2,1,0:T(8,128)(2,1)}, bf16[2,8,2,64,128]{4,3,2,1,0:T(8,128)(2,1)S(1)}, u32[]{:S(2)}) copy-start(bf16[2,8,2,64,128]{4,3,2,1,0:T(8,128)(2,1)S(1)} %get-tuple-element.27.c) | copy-start | bytes 1572868
  76.9 20.7 %copy-start.15 = (bf16[32,128]{1,0:T(8,128)(2,1)}, bf16[32,128]{1,0:T(8,128)(2,1)S(1)}, u32[]{:S(2)}) copy-start(bf16[32,128]{1,0:T(8,128)(2,1)S(1)} %get-tuple-element.22.own.s0) | copy-start | bytes 24580
  76.9 18.4 %collective-permute-start.4 = (bf16[1056,128]{1,0:T(8,128)(2,1)S(1)}, bf16[1056,128]{1,0:T(8,128)(2,1)S(1)}, u32[]{:S(2)}, u32[]{:S(2)}) collective-permute-start(bf16[1056,128]{1,0:T(8,128)(2,1)S(1)} %get-tuple-element.23), channel_id=1, source_target_pairs={{0,4},{4,0},{8,12},{12,8},{1,5},{5,1},{9,13},{13,9},{2,6},{6,2},{1... | collective-permute-start | bytes 811016 | tf_op jit(solution)/shard_map/ppermute | solution.py:383
  78.2 17.2 %collective-permute-start.6 = (bf16[1056,128]{1,0:T(8,128)(2,1)S(1)}, bf16[1056,128]{1,0:T(8,128)(2,1)S(1)}, u32[]{:S(2)}, u32[]{:S(2)}) collective-permute-start(bf16[1056,128]{1,0:T(8,128)(2,1)S(1)} %get-tuple-element.24), channel_id=1, source_target_pairs={{0,12},{4,8},{8,4},{12,0},{1,13},{5,9},{9,5},{13,1},{2,14},{6,10},... | collective-permute-start | bytes 811016 | tf_op jit(solution)/shard_map/ppermute | solution.py:383
  79.8 15.6 %collective-permute-start.5 = (bf16[32,128]{1,0:T(8,128)(2,1)S(1)}, bf16[32,128]{1,0:T(8,128)(2,1)S(1)}, u32[]{:S(2)}, u32[]{:S(2)}) collective-permute-start(bf16[32,128]{1,0:T(8,128)(2,1)S(1)} %get-tuple-element.22.own.s0), channel_id=1, source_target_pairs={{0,8},{4,12},{8,0},{12,4},{1,9},{5,13},{9,1},{13,5},{2,10},{6,14},... | collective-permute-start | bytes 24584 | tf_op jit(solution)/shard_map/ppermute | solution.py:383
  84.7 0.8 copy-start.13
  85.5 12.1 %copy-start.12 = (f32[1024,128]{1,0:T(8,128)}, f32[1024,128]{1,0:T(8,128)S(1)}, u32[]{:S(2)}) copy-start(f32[1024,128]{1,0:T(8,128)S(1)} %get-tuple-element.32.normed) | copy-start | bytes 1572868
  95.4 2.3 %copy-start.16 = (bf16[32,128]{1,0:T(8,128)(2,1)}, bf16[32,128]{1,0:T(8,128)(2,1)S(1)}, u32[]{:S(2)}) copy-start(bf16[32,128]{1,0:T(8,128)(2,1)S(1)} %collective-permute-done.5.second.s2) | copy-start | bytes 24580
  95.4 2.3 %copy-start.10 = (bf16[1056,128]{1,0:T(8,128)(2,1)}, bf16[1056,128]{1,0:T(8,128)(2,1)S(1)}, u32[]{:S(2)}) copy-start(bf16[1056,128]{1,0:T(8,128)(2,1)S(1)} %collective-permute-done.4.first) | copy-start | bytes 811012
  95.4 2.3 %copy-start.11 = (bf16[1056,128]{1,0:T(8,128)(2,1)}, bf16[1056,128]{1,0:T(8,128)(2,1)S(1)}, u32[]{:S(2)}) copy-start(bf16[1056,128]{1,0:T(8,128)(2,1)S(1)} %collective-permute-done.6.third) | copy-start | bytes 811012
  97.6 34.6 %all-to-all-start.2 = ((bf16[64,96,128]{2,1,0:T(8,128)(2,1)}), bf16[64,96,128]{2,1,0:T(8,128)(2,1)S(1)}, u32[]{:S(2)}, u32[]{:S(2)}) async-start(bf16[64,96,128]{2,1,0:T(8,128)(2,1)} %bitcast.13), calls=%async_computation.2 | async-start | bytes 3145728 | tf_op jit(solution)/shard_map/all_to_all | solution.py:379
  106.6 32.6 %copy-start.9 = (f32[16,24,1024]{2,1,0:T(8,128)S(1)}, f32[16,24,1024]{2,1,0:T(8,128)}, u32[]{:S(2)}) copy-start(f32[16,24,1024]{2,1,0:T(8,128)} %get-tuple-element.34.saved) | copy-start | bytes 4718596
  106.6 32.6 %copy-start.17 = (f32[8,128]{1,0:T(8,128)S(1)}, f32[8,128]{1,0:T(8,128)}, u32[]{:S(2)}) copy-start(f32[8,128]{1,0:T(8,128)} %get-tuple-element.35.proj) | copy-start | bytes 12292
  109.2 20.3 %collective-permute-start.7 = (bf16[4,2,64,128]{3,2,1,0:T(8,128)(2,1)}, bf16[4,2,64,128]{3,2,1,0:T(8,128)(2,1)S(1)}, u32[]{:S(2)}, u32[]{:S(2)}) collective-permute-start(bf16[4,2,64,128]{3,2,1,0:T(8,128)(2,1)} %get-tuple-element.29), channel_id=1, source_target_pairs={{0,12},{4,8},{8,4},{12,0},{1,13},{5,9},{9,5},{13,1},{2,14},{6,10},... | collective-permute-start | bytes 393224 | tf_op jit(solution)/shard_map/ppermute | solution.py:383
  109.9 20.5 %collective-permute-start.8 = (bf16[4,2,64,128]{3,2,1,0:T(8,128)(2,1)}, bf16[4,2,64,128]{3,2,1,0:T(8,128)(2,1)S(1)}, u32[]{:S(2)}, u32[]{:S(2)}) collective-permute-start(bf16[4,2,64,128]{3,2,1,0:T(8,128)(2,1)} %get-tuple-element.30), channel_id=1, source_target_pairs={{0,4},{4,0},{8,12},{12,8},{1,5},{5,1},{9,13},{13,9},{2,6},{6,2},{1... | collective-permute-start | bytes 393224 | tf_op jit(solution)/shard_map/ppermute | solution.py:383
  132.3 13.3 %copy-start = (bf16[64,96,128]{2,1,0:T(8,128)(2,1)}, bf16[64,96,128]{2,1,0:T(8,128)(2,1)S(1)}, u32[]{:S(2)}) copy-start(bf16[64,96,128]{2,1,0:T(8,128)(2,1)S(1)} %all-to-all-done.2) | copy-start | bytes 4718596
  132.3 15.6 %all-to-all-start.3 = ((bf16[16,64,128]{2,1,0:T(8,128)(2,1)}), bf16[16,64,128]{2,1,0:T(8,128)(2,1)S(1)}, u32[]{:S(2)}, u32[]{:S(2)}) async-start(bf16[16,64,128]{2,1,0:T(8,128)(2,1)} %bitcast.27), calls=%async_computation.3 | async-start | bytes 524288 | tf_op jit(solution)/shard_map/all_to_all | solution.py:379
  147.9 0.7 copy-start.18
